TPU v7x, 512 devices: a whole 4x8x8 slice. The times are simulated.
512 devices in a mesh: engine: 4 (over x), fsdp: 16 (over z, y_lo), tensor: 8 (over y_hi, core).
Axes of the slice: x: 4, y: 8 (y_hi: 4, y_lo: 2; y = y_hi * 2 + y_lo), z: 8, core: 2. Of those that a mesh axis runs over, the one named last changes fastest.
Arguments:
- layer_input: bfloat16 [8192, 16384], P(('engine', 'fsdp'), 'tensor'), may hold values from -6 to 6
- norm_gain: bfloat16 [16384], P('tensor'), may hold values from 0.099609375 to 1.8984375
- query_base: bfloat16 [16384, 1024], P(('engine', 'fsdp'), 'tensor'), may hold values from -0.046875 to 0.046875
- query_down: bfloat16 [16384, 64], P(('engine', 'fsdp')), may hold values from -0.046875 to 0.046875
- query_up: bfloat16 [64, 1024], P(None, 'tensor'), may hold values from -0.29882812 to 0.29882812
- kv_base: bfloat16 [8, 2048, 256], P('tensor', ('engine', 'fsdp')), may hold values from -0.046875 to 0.046875
- output_base_weight: bfloat16 [1024, 8, 2048], P(None, 'tensor', ('engine', 'fsdp')), may hold values from -0.1875 to 0.1875
- output_down_factor: bfloat16 [1024, 64], P('tensor'), may hold values from -0.1875 to 0.1875
- output_up_factor: bfloat16 [64, 8, 2048], P(None, 'tensor', ('engine', 'fsdp')), may hold values from -0.29882812 to 0.29882812
- cache_keys: bfloat16 [64, 512, 128], P(('engine', 'fsdp')), may hold values from -250 to 250
- cache_values: bfloat16 [64, 512, 128], P(('engine', 'fsdp')), may hold values from -6 to 6
- positions: int32 [64, 128], P(('engine', 'fsdp')), may hold values from 0 to 767, as said below
- offsets: int32 [64], P(('engine', 'fsdp')), may hold values from 0 to 512, as said below
Outputs:
- attended: bfloat16 [8192, 16384], P(('engine', 'fsdp'), 'tensor')
Inputs may be any that keep to these rules, and one draw needn't show every extreme that they name: `offsets`: each group's offset is its count of valid cache slots; some group has 512 and some group has 0. `positions`: positions rise along each group's row, by 1 or 2 a token; the first is its group's offset or one more; the group with 512 valid slots rises by 2 at every token.
All inputs are finite; a program needn't handle non-finite values.
Results may differ from a plain program's by a relative error of at most 0.03.
Values may be sent and summed in bfloat16 or wider, within the bound.
No kernel may reach another device: no remote copies, remote signals or barrier semaphores. Data moves between devices by JAX's collectives and lax.ppermute only.
A program may use at most 64 MiB of HBM per device.

v0:
```python
import jax
import jax.numpy as jnp
from jax import lax
from jax.sharding import PartitionSpec as P


def rotate(values, places):
    half = values.shape[-1] // 2
    index = jnp.arange(half).astype(jnp.float32)
    inverse = jnp.exp(index * (-2.0 / values.shape[-1]) * jnp.log(jnp.float32(500000.0)))
    angle = places.astype(jnp.float32)[:, None] * inverse[None, :]
    cosine = jnp.cos(angle)
    sine = jnp.sin(angle)
    first = values[:, :half]
    second = values[:, half:]
    return jnp.concatenate([first * cosine - second * sine, second * cosine + first * sine], axis=1)


def attend(query, new_keys, new_values, old_keys, old_values, offset):
    tok_count = query.shape[0]
    slots = old_keys.shape[0]
    keys_all = jnp.concatenate([old_keys, new_keys], axis=0)
    values_all = jnp.concatenate([old_values, new_values], axis=0)
    scores = jnp.dot(query, keys_all.T, preferred_element_type=jnp.float32) * query.shape[-1] ** (
        -0.5
    )
    slot_seen = jnp.broadcast_to(jnp.arange(slots)[None, :] < offset, (tok_count, slots))
    rows = jnp.arange(tok_count)
    new_seen = rows[None, :] <= rows[:, None]
    seen = jnp.concatenate([slot_seen, new_seen], axis=1)
    scores = jnp.where(seen, scores, jnp.float32(-1e30))
    top = jnp.max(scores, axis=1, keepdims=True)
    probs = jnp.exp(scores - top)
    weights = (probs / jnp.sum(probs, axis=1, keepdims=True)).astype(jnp.bfloat16)
    return jnp.dot(weights, values_all, preferred_element_type=jnp.float32).astype(jnp.bfloat16)


def per_device(
    layer_input,
    norm_gain,
    query_base,
    query_down,
    query_up,
    kv_base,
    output_base_weight,
    output_down_factor,
    output_up_factor,
    cache_keys,
    cache_values,
    positions,
    offsets,
):
    head_size = query_base.shape[1]
    tok_count = layer_input.shape[0]
    full_input, full_gain, complete_down_factor = (
        lax.all_gather(layer_input, "tensor", axis=1, tiled=True),
        lax.all_gather(norm_gain, "tensor", axis=0, tiled=True),
        lax.all_gather(output_down_factor, "tensor", axis=0, tiled=True),
    )
    wide = full_input.astype(jnp.float32)
    scale = lax.rsqrt(jnp.mean(wide * wide, axis=1, keepdims=True) + 1e-05)
    normed = (wide * scale * full_gain.astype(jnp.float32)[None, :]).astype(jnp.bfloat16)
    local_normed = (
        layer_input.astype(jnp.float32) * scale * norm_gain.astype(jnp.float32)[None, :]
    ).astype(jnp.bfloat16)
    merged_query = (
        query_base.astype(jnp.float32)
        + 2.0 * jnp.dot(query_down, query_up, preferred_element_type=jnp.float32)
    ).astype(jnp.bfloat16)
    columns = normed
    query_raw = jnp.dot(
        columns,
        lax.all_gather(merged_query, ("engine", "fsdp"), axis=0, tiled=True),
        preferred_element_type=jnp.float32,
    )
    columns = local_normed
    kv_part = jnp.dot(
        columns,
        lax.all_gather(kv_base, ("engine", "fsdp"), axis=1, tiled=True)[0],
        preferred_element_type=jnp.float32,
    )
    kv_total = lax.psum(kv_part.astype(jnp.bfloat16), "tensor").astype(jnp.float32)
    places = positions[0]
    query = rotate(query_raw, places).astype(jnp.bfloat16)
    new_keys = rotate(kv_total[:, :head_size], places).astype(jnp.bfloat16)
    new_values = kv_total[:, head_size:].astype(jnp.bfloat16)
    head_out = attend(query, new_keys, new_values, cache_keys[0], cache_values[0], offsets[0])
    adapter_output_delta = jnp.einsum(
        "lz,zam->lam",
        complete_down_factor.astype(jnp.float32),
        output_up_factor.astype(jnp.float32),
    )
    combined_output_weight = (
        output_base_weight.astype(jnp.float32) + 2.0 * adapter_output_delta
    ).astype(jnp.bfloat16)
    own_rows = lax.all_to_all(
        combined_output_weight, "tensor", split_axis=0, concat_axis=1, tiled=True
    )
    terms = jnp.einsum(
        "tk,kbn->tbn",
        head_out,
        lax.all_gather(own_rows, ("engine", "fsdp"), axis=2, tiled=True),
        preferred_element_type=jnp.float32,
    )
    flat_terms = terms.reshape(tok_count, terms.shape[1] * terms.shape[2])
    attended = lax.psum_scatter(
        flat_terms.astype(jnp.bfloat16), "tensor", scatter_dimension=1, tiled=True
    )
    return attended


def solution(mesh):
    in_specs = (
        P(("engine", "fsdp"), "tensor"),
        P("tensor"),
        P(("engine", "fsdp"), "tensor"),
        P(("engine", "fsdp"), None),
        P(None, "tensor"),
        P("tensor", ("engine", "fsdp"), None),
        P(None, "tensor", ("engine", "fsdp")),
        P("tensor", None),
        P(None, "tensor", ("engine", "fsdp")),
        P(("engine", "fsdp"), None, None),
        P(("engine", "fsdp"), None, None),
        P(("engine", "fsdp"), None),
        P(("engine", "fsdp")),
    )
    out_specs = P(("engine", "fsdp"), "tensor")
    return jax.shard_map(
        per_device, mesh=mesh, in_specs=in_specs, out_specs=out_specs, check_vma=False
    )
```

profile of v0, /device:TPU:1, one launch (start us, length us, event | category | flops | bytes accessed | tf_op | source)
XLA Modules:
  0.0 1155.2 jit_solution(11923218932344114234)
XLA Ops:
  6.6 0.7 all-gather.6.cloned.1.call-update
  7.3 0.7 all-gather.10.cloned.1.call-update
  8.1 0.7 convert_element_type.81
  8.8 60.3 %all-gather.6.cloned.1.call-done = bf16[128,16384]{1,0:T(8,128)(2,1)} async-done(((bf16[128,2048]{1,0:T(8,128)(2,1)}), bf16[128,16384]{1,0:T(8,128)(2,1)}) %all-gather.6.cloned.1.call-update) | async-done | bytes 4194320 | tf_op jit(solution)/shard_map/all_gather | solution.py:56
  69.1 3.1 fusion
  72.1 254.9 %all-gather.10.cloned.1.call-done = bf16[1,2048,256]{2,1,0:T(8,128)(2,1)} async-done(((bf16[1,32,256]{2,1,0:T(8,128)(2,1)}), bf16[1,2048,256]{2,1,0:T(8,128)(2,1)}) %all-gather.10.cloned.1.call-update) | async-done | bytes 1048592 | tf_op jit(solution)/shard_map/all_gather | solution.py:79
  327.1 2.4 convolution_convert_fusion
  329.6 0.8 fusion.17
  330.5 60.6 %all_gather.22 = bf16[1024,64]{0,1:T(8,128)(2,1)S(1)} all-gather(bf16[128,64]{0,1:T(8,128)(2,1)S(1)} %copy-done.5), channel_id=1, replica_groups=mesh['engine'=4,'fsdp'=16,'tensor'=8] {'tensor'}, dimensions={0}, use_global_device_ids=true | all-gather | bytes 147456 | tf_op jit(solution)/shard_map/all_gather | solution.py:58
  391.3 0.5 broadcast.30
  391.8 0.7 reduce
  392.5 0.2 copy.43
  392.7 0.3 reshape.40
  393.0 11.2 all_to_all.18
  404.2 0.3 reshape.41
  404.5 0.3 copy.36
  404.8 0.6 copy.42
  406.2 15.2 %all_gather.19 = bf16[16384]{0:T(1024)(128)(2,1)S(1)} all-gather(bf16[2048]{0:T(1024)(128)(2,1)S(1)} %copy-done.6), channel_id=1, replica_groups=mesh['engine'=4,'fsdp'=16,'tensor'=8] {'tensor'}, dimensions={0}, use_global_device_ids=true | all-gather | bytes 36864 | tf_op jit(solution)/shard_map/all_gather | solution.py:57
  421.5 24.9 %all-reduce.2.cloned.1.call-done = bf16[128,256]{0,1:T(8,128)(2,1)} async-done(((bf16[128,256]{0,1:T(8,128)(2,1)}), bf16[128,256]{0,1:T(8,128)(2,1)}) %all-reduce.2.cloned.1.call-update) | async-done | bytes 65552 | tf_op jit(solution)/shard_map/psum | solution.py:82
  446.4 0.8 slice.28
  447.2 0.9 convert_element_type.84
  448.1 273.7 %all-gather.8.cloned.1.call-done = bf16[16384,128]{1,0:T(8,128)(2,1)} async-done(((bf16[256,128]{1,0:T(8,128)(2,1)}), bf16[16384,128]{1,0:T(8,128)(2,1)}) %all-gather.8.cloned.1.call-update) | async-done | bytes 4194320 | tf_op jit(solution)/shard_map/all_gather | solution.py:73
  721.9 5.5 fusion.3
  727.4 0.2 fusion.45
  727.7 0.3 fusion.59
  728.0 0.2 fusion.22
  728.3 304.5 %all-gather.12.cloned.1.call-done = bf16[128,8,1,2048]{0,1,2,3:T(8,128)(2,1)} async-done(((bf16[128,8,1,32]{0,1,2,3:T(8,128)(2,1)}), bf16[128,8,1,2048]{0,1,2,3:T(8,128)(2,1)}) %all-gather.12.cloned.1.call-update) | async-done | bytes 4194320 | tf_op jit(solution)/shard_map/all_gather | solution.py:102
  1032.7 6.7 copy.38
  1039.4 5.7 fusion.9
  1045.1 6.4 copy.39
  1051.5 94.8 %reduce-scatter.2.cloned.1.call-done = bf16[128,2048]{0,1:T(8,128)(2,1)} async-done(((bf16[128,16384]{0,1:T(8,128)(2,1)}), bf16[128,2048]{0,1:T(8,128)(2,1)}) %reduce-scatter.2.cloned.1.call-update) | async-done | bytes 524304 | tf_op jit(solution)/shard_map/reduce_scatter | solution.py:106
  1146.3 2.0 copy.40
  (43 shorter events, 0.8 us)
Async XLA Ops:
  6.5 323.0 %copy-start = (bf16[256,64]{0,1:T(8,128)(2,1)S(1)}, bf16[256,64]{0,1:T(8,128)(2,1)}, u32[]{:S(2)}) copy-start(bf16[256,64]{0,1:T(8,128)(2,1)} %param.16) | copy-start | bytes 98308
  6.5 320.5 %copy-start.1 = (bf16[128,2048]{1,0:T(8,128)(2,1)S(1)}, bf16[128,2048]{1,0:T(8,128)(2,1)}, u32[]{:S(2)}) copy-start(bf16[128,2048]{1,0:T(8,128)(2,1)} %param.13) | copy-start | bytes 1572868
  6.5 323.0 %copy-start.7 = (bf16[64,128]{1,0:T(8,128)(2,1)S(1)}, bf16[64,128]{1,0:T(8,128)(2,1)}, u32[]{:S(2)}) copy-start(bf16[64,128]{1,0:T(8,128)(2,1)} %param.17) | copy-start | bytes 49156
  6.5 323.0 %copy-start.3 = (bf16[256,128]{1,0:T(8,128)(2,1)S(1)}, bf16[256,128]{1,0:T(8,128)(2,1)}, u32[]{:S(2)}) copy-start(bf16[256,128]{1,0:T(8,128)(2,1)} %param.15) | copy-start | bytes 196612
  6.5 324.0 %copy-start.5 = (bf16[128,64]{0,1:T(8,128)(2,1)S(1)}, bf16[128,64]{0,1:T(8,128)(2,1)}, u32[]{:S(2)}) copy-start(bf16[128,64]{0,1:T(8,128)(2,1)} %param.20) | copy-start | bytes 49156
  6.5 384.6 %copy-start.8 = (bf16[64,1,32]{0,2,1:T(8,128)(2,1)S(1)}, bf16[64,1,32]{0,2,1:T(8,128)(2,1)}, u32[]{:S(2)}) copy-start(bf16[64,1,32]{0,2,1:T(8,128)(2,1)} %param.21) | copy-start | bytes 12292
  6.6 384.6 %copy-start.4 = (bf16[1024,1,32]{0,2,1:T(8,128)(2,1)S(1)}, bf16[1024,1,32]{0,2,1:T(8,128)(2,1)}, u32[]{:S(2)}) copy-start(bf16[1024,1,32]{0,2,1:T(8,128)(2,1)} %param.19) | copy-start | bytes 196612
  6.6 62.5 %all-gather.6.cloned.1.call-start = ((), (), s32[]{:S(2)}) async-start(), calls=%async_computation.2 | async-start | bytes 4718592 | tf_op jit(solution)/shard_map/all_gather | solution.py:56
  7.3 319.8 %all-gather.10.cloned.1.call-start = ((), (), s32[]{:S(2)}) async-start(), calls=%async_computation.4 | async-start | bytes 1064960 | tf_op jit(solution)/shard_map/all_gather | solution.py:79
  8.1 438.3 %all-reduce.2.cloned.1.call-start = ((), (), s32[]{:S(2)}) async-start(), calls=%async_computation.5 | async-start | bytes 131072 | tf_op jit(solution)/shard_map/psum | solution.py:82
  8.8 397.4 %copy-start.6 = (bf16[2048]{0:T(1024)(128)(2,1)S(1)}, bf16[2048]{0:T(1024)(128)(2,1)}, u32[]{:S(2)}) copy-start(bf16[2048]{0:T(1024)(128)(2,1)} %param.14) | copy-start | bytes 12292
  8.8 412.7 %copy-start.10 = (s32[1,128]{1,0:T(1,128)S(1)}, s32[1,128]{1,0:T(1,128)}, u32[]{:S(2)}) copy-start(s32[1,128]{1,0:T(1,128)} %param.24) | copy-start | bytes 1540
  329.5 392.3 %all-gather.8.cloned.1.call-start = ((), (), s32[]{:S(2)}) async-start(), calls=%async_computation.3 | async-start | bytes 4259840 | tf_op jit(solution)/shard_map/all_gather | solution.py:73
  330.4 702.3 %all-gather.12.cloned.1.call-start = ((), (), s32[]{:S(2)}) async-start(), calls=%async_computation.7 | async-start | bytes 4259840 | tf_op jit(solution)/shard_map/all_gather | solution.py:102
  405.5 740.9 %reduce-scatter.2.cloned.1.call-start = ((), (), s32[]{:S(2)}) async-start(), calls=%async_computation.6 | async-start | bytes 4718592 | tf_op jit(solution)/shard_map/reduce_scatter | solution.py:106
  448.1 279.6 %copy-start.9 = (bf16[1,512,128]{2,1,0:T(8,128)(2,1)S(1)}, bf16[1,512,128]{2,1,0:T(8,128)(2,1)}, u32[]{:S(2)}) copy-start(bf16[1,512,128]{2,1,0:T(8,128)(2,1)} %param.22) | copy-start | bytes 393220
  728.3 311.2 %copy-start.2 = (bf16[1,512,128]{2,1,0:T(8,128)(2,1)S(1)}, bf16[1,512,128]{2,1,0:T(8,128)(2,1)}, u32[]{:S(2)}) copy-start(bf16[1,512,128]{2,1,0:T(8,128)(2,1)} %param.23) | copy-start | bytes 393220
Sparse Core Ops, SparseCore 0:
  9.5 59.4 all-gather.5
  71.1 255.8 all-gather.9
  330.0 116.3 all-reduce.1
  448.5 273.3 all-gather.7
  724.0 308.7 all-gather.11
  1051.6 94.6 reduce-scatter.1
where the time goes:
time: 1160 us
  waiting for transfers between devices  1010 us (87%)
  blocking collectives  87.1 us (8%)
  local copies, waits for them, and re-layouts  18.4 us (2%)
  matrix products  14.9 us (1%)
  between operations  14.3 us (1%)
    all_gather x1, waiting for transfers between devices, per_device(): lax.all_gather(own_rows, ('engine', 'fsdp'), axis=2, tiled=True)  304 us
    all_gather x1, waiting for transfers between devices, per_device(): lax.all_gather(merged_query, ('engine', 'fsdp'), axis=0, tiled=True)  274 us
    all_gather x1, waiting for transfers between devices, per_device(): lax.all_gather(kv_base, ('engine', 'fsdp'), axis=1, tiled=True)[0]  255 us
    reduce_scatter x1, waiting for transfers between devices, per_device(): lax.psum_scatter(flat_terms.astype(jnp.bfloat16), 'tensor', scatter_dimen...  94.8 us
    all_gather x1, blocking collectives, per_device(): lax.all_gather(output_down_factor, 'tensor', axis=0, tiled=True)  60.6 us
    all_gather x1, waiting for transfers between devices, per_device(): lax.all_gather(layer_input, 'tensor', axis=1, tiled=True)  60.3 us
    psum x1, waiting for transfers between devices, per_device(): lax.psum(kv_part.astype(jnp.bfloat16), 'tensor').astype(jnp.float32)  24.9 us
  transfers between devices with their start and end apart: 6, of which 6 were waited for; matrix products, arithmetic and copies ran while one was open for 1% of the time, Pallas kernels for 0%

commit v1 on v0

v1 whole, which is shorter than its diff:
```python
import jax
import jax.numpy as jnp
from jax import lax
from jax.sharding import PartitionSpec as P

AXES = ("engine", "fsdp", "tensor")


def rotate(values, places):
    half = values.shape[-1] // 2
    index = jnp.arange(half).astype(jnp.float32)
    inverse = jnp.exp(index * (-2.0 / values.shape[-1]) * jnp.log(jnp.float32(500000.0)))
    angle = places.astype(jnp.float32)[:, None] * inverse[None, :]
    cosine = jnp.cos(angle)
    sine = jnp.sin(angle)
    first = values[:, :half]
    second = values[:, half:]
    return jnp.concatenate([first * cosine - second * sine, second * cosine + first * sine], axis=1)


def attend(query, new_keys, new_values, old_keys, old_values, offset):
    tok_count = query.shape[0]
    slots = old_keys.shape[0]
    keys_all = jnp.concatenate([old_keys, new_keys], axis=0)
    values_all = jnp.concatenate([old_values, new_values], axis=0)
    scores = jnp.dot(query, keys_all.T, preferred_element_type=jnp.float32) * query.shape[-1] ** (
        -0.5
    )
    slot_seen = jnp.broadcast_to(jnp.arange(slots)[None, :] < offset, (tok_count, slots))
    rows = jnp.arange(tok_count)
    new_seen = rows[None, :] <= rows[:, None]
    seen = jnp.concatenate([slot_seen, new_seen], axis=1)
    scores = jnp.where(seen, scores, jnp.float32(-1e30))
    top = jnp.max(scores, axis=1, keepdims=True)
    probs = jnp.exp(scores - top)
    weights = (probs / jnp.sum(probs, axis=1, keepdims=True)).astype(jnp.bfloat16)
    return jnp.dot(weights, values_all, preferred_element_type=jnp.float32).astype(jnp.bfloat16)


def shard_home(e, f, t):
    z, y = f // 2, f % 2
    return t // 2, ((t % 2) * 4 + z % 4) * 2 + y, e * 2 + z // 4


def swap_engine(e, f, t):
    return t // 2, f, e * 2 + t % 2


def pairs(move):
    flat = lambda e, f, t: (e * 16 + f) * 8 + t
    return [
        (flat(e, f, t), flat(*move(e, f, t)))
        for e in range(4)
        for f in range(16)
        for t in range(8)
    ]


def per_device(
    layer_input,
    norm_gain,
    query_base,
    query_down,
    query_up,
    kv_base,
    output_base_weight,
    output_down_factor,
    output_up_factor,
    cache_keys,
    cache_values,
    positions,
    offsets,
):
    engine = lax.axis_index("engine")
    merged_query = (
        query_base.astype(jnp.float32)
        + 2.0 * jnp.dot(query_down, query_up, preferred_element_type=jnp.float32)
    ).astype(jnp.bfloat16)
    query_shard = lax.ppermute(merged_query, AXES, pairs(shard_home))

    keys_half, values_half = kv_base[0, :, :128], kv_base[0, :, 128:]
    kv_parts = jnp.stack([keys_half, keys_half, values_half, values_half])
    kv_parts = lax.all_to_all(kv_parts, "engine", split_axis=0, concat_axis=0, tiled=True)
    kv_shard = lax.dynamic_slice_in_dim(kv_parts, (engine % 2) * 2, 2, axis=0).reshape(64, 128)

    shard = jnp.concatenate([query_shard, kv_shard], axis=0)
    gathered = lax.all_to_all(
        jnp.broadcast_to(shard[None], (16, 320, 128)), "fsdp", split_axis=0, concat_axis=0, tiled=True
    )

    wide = layer_input.astype(jnp.float32)
    squares = lax.all_gather(jnp.sum(wide * wide, axis=1)[None], "tensor", axis=0, tiled=True)
    scale = lax.rsqrt(jnp.sum(squares, axis=0) / 16384.0 + 1e-05)
    normed = (wide * scale[:, None] * norm_gain.astype(jnp.float32)[None, :]).astype(jnp.bfloat16)
    tokens = lax.all_gather(normed, "engine", axis=0, tiled=True)

    query_weight = gathered[:, :256].reshape(2, 2048, 128)
    kv_weight = gathered[:, 256:].reshape(16, 2, 32, 128).transpose(1, 0, 2, 3).reshape(1024, 128)
    some_tokens = lax.dynamic_slice_in_dim(tokens, (engine % 2) * 1024, 1024, axis=1)
    kv_terms = jnp.dot(some_tokens, kv_weight, preferred_element_type=jnp.float32)
    kv_terms = kv_terms.astype(jnp.bfloat16).reshape(4, 1, 128, 128)
    query_terms = jnp.stack(
        [
            jnp.dot(tokens, query_weight[c], preferred_element_type=jnp.float32)
            .astype(jnp.bfloat16)
            .reshape(4, 128, 128)
            for c in range(2)
        ],
        axis=1,
    )
    terms = jnp.concatenate([query_terms, jnp.broadcast_to(kv_terms, (4, 2, 128, 128))], axis=3)
    terms = lax.all_to_all(
        terms.reshape(8, 128, 256), "tensor", split_axis=0, concat_axis=0, tiled=True
    )
    total = jnp.sum(terms.astype(jnp.float32), axis=0)
    kv_all = lax.all_gather(total[:, 128:], "engine", axis=0, tiled=True).reshape(4, 128, 128)

    old = lax.ppermute(jnp.stack([cache_keys[0], cache_values[0]]), AXES, pairs(swap_engine))
    numbers = jnp.concatenate([positions[0], jnp.broadcast_to(offsets, (128,))]).reshape(2, 128)
    numbers = lax.ppermute(numbers, AXES, pairs(swap_engine))
    places = numbers[0]
    query = rotate(total[:, :128], places).astype(jnp.bfloat16)
    new_keys = rotate(kv_all[0] + kv_all[1], places).astype(jnp.bfloat16)
    new_values = (kv_all[2] + kv_all[3]).astype(jnp.bfloat16)
    head_out = attend(query, new_keys, new_values, old[0], old[1], numbers[1, 0])

    down = lax.all_gather(output_down_factor, "tensor", axis=0, tiled=True)
    up = output_up_factor[:, 0, :]
    delta = lax.dot_general(up, down, (((0,), (1,)), ((), ())), preferred_element_type=jnp.float32)
    out_shard = (output_base_weight[:, 0, :].T.astype(jnp.float32) + 2.0 * delta).astype(jnp.bfloat16)
    out_weight = lax.all_gather(out_shard, "fsdp", axis=0, tiled=True)

    heads = lax.all_gather(head_out[None], "tensor", axis=0, tiled=True)
    heads = lax.all_gather(heads[None], "engine", axis=0, tiled=True)
    heads = heads.reshape(4, 4, 2, 128, 128).transpose(1, 3, 0, 2, 4).reshape(512, 1024)
    out = lax.dot_general(
        heads, out_weight, (((1,), (1,)), ((), ())), preferred_element_type=jnp.float32
    ).astype(jnp.bfloat16)
    out = lax.all_to_all(
        out.reshape(4, 128, 512), "engine", split_axis=0, concat_axis=0, tiled=True
    )
    return out.transpose(1, 0, 2).reshape(128, 2048)


def solution(mesh):
    in_specs = (
        P(("engine", "fsdp"), "tensor"),
        P("tensor"),
        P(("engine", "fsdp"), "tensor"),
        P(("engine", "fsdp"), None),
        P(None, "tensor"),
        P("tensor", ("engine", "fsdp"), None),
        P(None, "tensor", ("engine", "fsdp")),
        P("tensor", None),
        P(None, "tensor", ("engine", "fsdp")),
        P(("engine", "fsdp"), None, None),
        P(("engine", "fsdp"), None, None),
        P(("engine", "fsdp"), None),
        P(("engine", "fsdp")),
    )
    out_specs = P(("engine", "fsdp"), "tensor")
    return jax.shard_map(
        per_device, mesh=mesh, in_specs=in_specs, out_specs=out_specs, check_vma=False
    )
```

time: 1160 us -> 284 us (0.24)
  the two profiles are of different devices: /device:TPU:1 before, /device:TPU:8 now
where the time goes in v1:
time: 284 us
  waiting for transfers between devices  129 us (45%)
  blocking collectives  81.6 us (29%)
  starting transfers between devices  37.7 us (13%)
  between operations  14.2 us (5%)
  local copies, waits for them, and re-layouts  7.28 us (3%)
  matrix products  7.15 us (3%)
  other arithmetic  6.62 us (2%)
    all_gather x1, waiting for transfers between devices, per_device(): out_weight = lax.all_gather(out_shard, 'fsdp', axis=0, tiled=True)  73.3 us
    all_to_all x1, waiting for transfers between devices, per_device(): lax.all_to_all(jnp.broadcast_to(shard[None], (16, 320, 128)), 'fsdp', spl...  32.1 us
    all_gather x1, blocking collectives, per_device(): lax.all_gather(total[:, 128:], 'engine', axis=0, tiled=True)  28.3 us
    all_to_all x1, starting transfers between devices, per_device(): lax.all_to_all(jnp.broadcast_to(shard[None], (16, 320, 128)), 'fsdp', spl...  21.2 us
    all_gather x1, blocking collectives, per_device(): heads = lax.all_gather(head_out[None], 'tensor', axis=0, tiled=True)  15.7 us
    all_to_all x1, waiting for transfers between devices, per_device(): lax.all_to_all(terms.reshape(8, 128, 256), 'tensor', split_axis=0, concat...  14.7 us
    all_gather x1, blocking collectives, per_device(): down = lax.all_gather(output_down_factor, 'tensor', axis=0, tiled=True)  13.5 us
    all_to_all x1, blocking collectives, per_device(): lax.all_to_all(out.reshape(4, 128, 512), 'engine', split_axis=0, concat_a...  12.1 us
  transfers between devices with their start and end apart: 9, of which 4 were waited for; matrix products, arithmetic and copies ran while one was open for 4% of the time, Pallas kernels for 0%

profile of v1, /device:TPU:8, one launch (start us, length us, event | category | flops | bytes accessed | tf_op | source)
XLA Modules:
  0.0 283.8 jit_solution(4038580253601726157)
XLA Ops:
  6.5 0.7 fusion.42
  7.3 0.6 pad_maximum_fusion.3
  7.9 4.3 %all-to-all-start = ((bf16[4,32,128]{2,1,0:T(8,128)(2,1)}), bf16[4,32,128]{2,1,0:T(8,128)(2,1)S(1)}, u32[]{:S(2)}, u32[]{:S(2)}) async-start(bf16[4,32,128]{2,1,0:T(8,128)(2,1)} %pad_maximum_fusion.3), calls=%async_computation | async-start | bytes 65536 | tf_op jit(solution)/shard_map/all_to_all | solution.py:83
  12.2 0.7 convert_element_type.73
  12.9 1.2 fusion.5
  14.1 12.0 %all-gather.3 = f32[8,1,128]{2,1,0:T(1,128)S(1)} all-gather(f32[1,1,128]{2,1,0:T(1,128)S(1)} %bitcast.68), channel_id=2, replica_groups=mesh['engine'=4,'fsdp'=16,'tensor'=8] {'tensor'}, dimensions={0}, use_global_device_ids=true | all-gather | bytes 4608 | tf_op jit(solution)/shard_map/all_gather | solution.py:92
  26.1 2.0 fusion.7
  28.4 0.7 collective-permute-start.1
  29.2 1.3 broadcast_in_dim.22
  30.5 21.2 %all-to-all-start.1 = ((bf16[16,320,128]{2,1,0:T(8,128)(2,1)}), bf16[16,320,128]{2,1,0:T(8,128)(2,1)S(1)}, u32[]{:S(2)}, u32[]{:S(2)}) async-start(bf16[16,320,128]{2,1,0:T(8,128)(2,1)} %broadcast_in_dim.22), calls=%async_computation.1 | async-start | bytes 2621440 | tf_op jit(solution)/shard_map/all_to_all | solution.py:87
  51.7 32.1 %all-to-all-done.1 = bf16[16,320,128]{2,1,0:T(8,128)(2,1)S(1)} async-done(((bf16[16,320,128]{2,1,0:T(8,128)(2,1)}), bf16[16,320,128]{2,1,0:T(8,128)(2,1)S(1)}, u32[]{:S(2)}, u32[]{:S(2)}) %all-to-all-start.1) | async-done | bytes 1310752 | tf_op jit(solution)/shard_map/all_to_all | solution.py:87
  83.9 2.4 convolution_convert_fusion.1
  86.4 0.7 convolution_convert_fusion.2
  87.2 0.4 convolution_convert_fusion.3
  87.7 0.9 pad_maximum_fusion
  88.5 10.1 %all-to-all-start.2 = ((bf16[8,128,256]{2,1,0:T(8,128)(2,1)}), bf16[8,128,256]{2,1,0:T(8,128)(2,1)S(1)}, u32[]{:S(2)}, u32[]{:S(2)}) async-start(bf16[8,128,256]{2,1,0:T(8,128)(2,1)} %bitcast.16), calls=%async_computation.2 | async-start | bytes 1048576 | tf_op jit(solution)/shard_map/all_to_all | solution.py:112
  98.7 0.7 collective-permute-start.2
  100.1 0.7 collective-permute-start
  100.8 0.5 slice.66
  101.3 0.6 iota_compare_fusion.1
  101.9 14.7 %all-to-all-done.2 = bf16[8,128,256]{2,1,0:T(8,128)(2,1)S(1)} async-done(((bf16[8,128,256]{2,1,0:T(8,128)(2,1)}), bf16[8,128,256]{2,1,0:T(8,128)(2,1)S(1)}, u32[]{:S(2)}, u32[]{:S(2)}) %all-to-all-start.2) | async-done | bytes 524320 | tf_op jit(solution)/shard_map/all_to_all | solution.py:112
  116.9 28.3 %all_gather.23 = f32[512,128]{0,1:T(8,128)S(1)} all-gather(f32[128,128]{0,1:T(8,128)S(1)} %copy.47), channel_id=1, replica_groups=mesh['engine'=4,'fsdp'=16,'tensor'=8] {'engine'}, dimensions={0}, use_global_device_ids=true | all-gather | bytes 327680 | tf_op jit(solution)/shard_map/all_gather | solution.py:116
  146.7 15.7 %all-gather.1 = bf16[1024,128]{1,0:T(8,128)(2,1)} all-gather(bf16[128,128]{1,0:T(8,128)(2,1)S(1)} %convolution_convert_fusion.4), channel_id=3, replica_groups=mesh['engine'=4,'fsdp'=16,'tensor'=8] {'tensor'}, dimensions={0}, use_global_device_ids=true | all-gather | bytes 294912 | tf_op jit(solution)/shard_map/all_gather | solution.py:133
  162.6 13.5 %all_gather.26 = bf16[1024,64]{0,1:T(8,128)(2,1)S(1)} all-gather(bf16[128,64]{0,1:T(8,128)(2,1)S(1)} %copy-done.6), channel_id=1, replica_groups=mesh['engine'=4,'fsdp'=16,'tensor'=8] {'tensor'}, dimensions={0}, use_global_device_ids=true | all-gather | bytes 147456 | tf_op jit(solution)/shard_map/all_gather | solution.py:127
  176.1 0.8 fusion.3
  176.9 9.1 %all-gather.12.cloned.1.call-done = bf16[32,128,128]{2,1,0:T(8,128)(2,1)} async-done(((bf16[8,128,128]{2,1,0:T(8,128)(2,1)}), bf16[32,128,128]{2,1,0:T(8,128)(2,1)}) %all-gather.12.cloned.1.call-update) | async-done | bytes 1048592 | tf_op jit(solution)/shard_map/all_gather | solution.py:134
  185.9 2.3 copy.43
  188.3 0.8 reshape.77
  189.0 73.3 %all-gather.10.cloned.1.call-done = bf16[512,1024]{1,0:T(8,128)(2,1)} async-done(((bf16[32,1024]{1,0:T(8,128)(2,1)}), bf16[512,1024]{1,0:T(8,128)(2,1)}) %all-gather.10.cloned.1.call-update) | async-done | bytes 1048592 | tf_op jit(solution)/shard_map/all_gather | solution.py:131
  262.3 2.0 convolution_convert_fusion
  264.2 12.1 %all_to_all.20 = bf16[4,128,512]{2,1,0:T(8,128)(2,1)S(1)} all-to-all(bf16[4,128,512]{2,1,0:T(8,128)(2,1)S(1)} %bitcast.63), channel_id=1, replica_groups=mesh['engine'=4,'fsdp'=16,'tensor'=8] {'engine'}, dimensions={0} | all-to-all | bytes 1048576 | tf_op jit(solution)/shard_map/all_to_all | solution.py:139
  276.4 0.8 copy.48
  (61 shorter events, 2.4 us)
Async XLA Ops:
  6.5 21.7 %copy-start = (bf16[256,64]{0,1:T(8,128)(2,1)S(1)}, bf16[256,64]{0,1:T(8,128)(2,1)}, u32[]{:S(2)}) copy-start(bf16[256,64]{0,1:T(8,128)(2,1)} %param.16) | copy-start | bytes 98308
  6.5 21.7 %copy-start.7 = (bf16[64,128]{1,0:T(8,128)(2,1)S(1)}, bf16[64,128]{1,0:T(8,128)(2,1)}, u32[]{:S(2)}) copy-start(bf16[64,128]{1,0:T(8,128)(2,1)} %param.17) | copy-start | bytes 49156
  6.5 21.7 %copy-start.4 = (bf16[256,128]{1,0:T(8,128)(2,1)S(1)}, bf16[256,128]{1,0:T(8,128)(2,1)}, u32[]{:S(2)}) copy-start(bf16[256,128]{1,0:T(8,128)(2,1)} %param.15) | copy-start | bytes 196612
  7.9 21.2 %all-to-all-start = ((bf16[4,32,128]{2,1,0:T(8,128)(2,1)}), bf16[4,32,128]{2,1,0:T(8,128)(2,1)S(1)}, u32[]{:S(2)}, u32[]{:S(2)}) async-start(bf16[4,32,128]{2,1,0:T(8,128)(2,1)} %pad_maximum_fusion.3), calls=%async_computation | async-start | bytes 65536 | tf_op jit(solution)/shard_map/all_to_all | solution.py:83
  12.2 71.7 %all-gather.8.cloned.1.call-start = ((), (), s32[]{:S(2)}) async-start(), calls=%async_computation.4 | async-start | bytes 2621440 | tf_op jit(solution)/shard_map/all_gather | solution.py:95
  28.4 0.7 collective-permute-start.1
  30.5 53.3 %all-to-all-start.1 = ((bf16[16,320,128]{2,1,0:T(8,128)(2,1)}), bf16[16,320,128]{2,1,0:T(8,128)(2,1)S(1)}, u32[]{:S(2)}, u32[]{:S(2)}) async-start(bf16[16,320,128]{2,1,0:T(8,128)(2,1)} %broadcast_in_dim.22), calls=%async_computation.1 | async-start | bytes 2621440 | tf_op jit(solution)/shard_map/all_to_all | solution.py:87
  83.9 2.5 copy-start.1
  87.1 11.6 %copy-start.2 = (bf16[1,512,128]{2,1,0:T(8,128)(2,1)S(1)}, bf16[1,512,128]{2,1,0:T(8,128)(2,1)}, u32[]{:S(2)}) copy-start(bf16[1,512,128]{2,1,0:T(8,128)(2,1)} %param.23) | copy-start | bytes 393220
  87.1 11.5 %copy-start.3 = (bf16[1,512,128]{2,1,0:T(8,128)(2,1)S(1)}, bf16[1,512,128]{2,1,0:T(8,128)(2,1)}, u32[]{:S(2)}) copy-start(bf16[1,512,128]{2,1,0:T(8,128)(2,1)} %param.22) | copy-start | bytes 393220
  87.1 12.9 %copy-start.9 = (s32[1,128]{1,0:T(1,128)S(1)}, s32[1,128]{1,0:T(1,128)}, u32[]{:S(2)}) copy-start(s32[1,128]{1,0:T(1,128)} %param.24) | copy-start | bytes 1540
  88.5 28.2 %all-to-all-start.2 = ((bf16[8,128,256]{2,1,0:T(8,128)(2,1)}), bf16[8,128,256]{2,1,0:T(8,128)(2,1)S(1)}, u32[]{:S(2)}, u32[]{:S(2)}) async-start(bf16[8,128,256]{2,1,0:T(8,128)(2,1)} %bitcast.16), calls=%async_computation.2 | async-start | bytes 1048576 | tf_op jit(solution)/shard_map/all_to_all | solution.py:112
  98.6 87.3 %all-gather.12.cloned.1.call-start = ((), (), s32[]{:S(2)}) async-start(), calls=%async_computation.6 | async-start | bytes 1310720 | tf_op jit(solution)/shard_map/all_gather | solution.py:134
  98.7 3.2 %collective-permute-start.2 = (bf16[2,512,128]{2,1,0:T(8,128)(2,1)S(1)}, bf16[2,512,128]{2,1,0:T(8,128)(2,1)S(1)}, u32[]{:S(2)}, u32[]{:S(2)}) collective-permute-start(bf16[2,512,128]{2,1,0:T(8,128)(2,1)S(1)} %pad_maximum_fusion.1), channel_id=1, source_target_pairs={{0,0},{1,1},{2,128},{3,129},{4,256},{5,257},{6,384},{7,385},{8,8},... | collective-permute-start | bytes 786440 | tf_op jit(solution)/shard_map/ppermute | solution.py:118
  100.1 0.7 collective-permute-start
  145.2 17.3 %copy-start.6 = (bf16[128,64]{0,1:T(8,128)(2,1)S(1)}, bf16[128,64]{0,1:T(8,128)(2,1)}, u32[]{:S(2)}) copy-start(bf16[128,64]{0,1:T(8,128)(2,1)} %param.20) | copy-start | bytes 49156
  145.2 30.8 %copy-start.5 = (bf16[1024,1,32]{0,2,1:T(8,128)(2,1)S(1)}, bf16[1024,1,32]{0,2,1:T(8,128)(2,1)}, u32[]{:S(2)}) copy-start(bf16[1024,1,32]{0,2,1:T(8,128)(2,1)} %param.19) | copy-start | bytes 196612
  145.2 30.8 %copy-start.8 = (bf16[64,1,32]{0,2,1:T(8,128)(2,1)S(1)}, bf16[64,1,32]{0,2,1:T(8,128)(2,1)}, u32[]{:S(2)}) copy-start(bf16[64,1,32]{0,2,1:T(8,128)(2,1)} %param.21) | copy-start | bytes 12292
  162.5 99.8 %all-gather.10.cloned.1.call-start = ((), (), s32[]{:S(2)}) async-start(), calls=%async_computation.5 | async-start | bytes 1114112 | tf_op jit(solution)/shard_map/all_gather | solution.py:131
Sparse Core Ops, SparseCore 0:
  28.3 38.6 all-gather.7
  162.6 23.2 all-gather.11
  188.0 74.1 all-gather.9

commit v2 on v1

--- a/solution.py
+++ b/solution.py
@@ -72,6 +72,8 @@
     offsets,
 ):
     engine = lax.axis_index("engine")
+    tokens = lax.all_gather(layer_input, "engine", axis=0, tiled=True)
+
     merged_query = (
         query_base.astype(jnp.float32)
         + 2.0 * jnp.dot(query_down, query_up, preferred_element_type=jnp.float32)
@@ -88,20 +90,33 @@
         jnp.broadcast_to(shard[None], (16, 320, 128)), "fsdp", split_axis=0, concat_axis=0, tiled=True
     )
 
-    wide = layer_input.astype(jnp.float32)
-    squares = lax.all_gather(jnp.sum(wide * wide, axis=1)[None], "tensor", axis=0, tiled=True)
-    scale = lax.rsqrt(jnp.sum(squares, axis=0) / 16384.0 + 1e-05)
-    normed = (wide * scale[:, None] * norm_gain.astype(jnp.float32)[None, :]).astype(jnp.bfloat16)
-    tokens = lax.all_gather(normed, "engine", axis=0, tiled=True)
+    numbers = jnp.concatenate([positions, jnp.broadcast_to(offsets[:, None], (1, 128))])
+    numbers = jnp.concatenate([numbers // 256, numbers % 256, jnp.zeros((12, 128), jnp.int32)])
+    group = jnp.concatenate([cache_keys[0], cache_values[0], numbers.astype(jnp.bfloat16)])
+    group = lax.ppermute(group, AXES, pairs(swap_engine))
+
+    down = lax.all_gather(output_down_factor, "tensor", axis=0, tiled=True)
+    up = output_up_factor[:, 0, :]
+    delta = lax.dot_general(up, down, (((0,), (1,)), ((), ())), preferred_element_type=jnp.float32)
+    out_shard = (output_base_weight[:, 0, :].T.astype(jnp.float32) + 2.0 * delta).astype(jnp.bfloat16)
+    gathered, _, group = lax.optimization_barrier((gathered, out_shard, group))
+    out_weight = lax.all_gather(out_shard, "fsdp", axis=0, tiled=True)
+
+    wide = tokens.astype(jnp.float32)
+    scaled = (wide * norm_gain.astype(jnp.float32)[None, :]).astype(jnp.bfloat16)
+    squares = jnp.sum(wide * wide, axis=1).reshape(4, 1, 1, 128)
+    squares_high = squares.astype(jnp.bfloat16)
+    squares_low = (squares - squares_high.astype(jnp.float32)).astype(jnp.bfloat16)
+    squares = jnp.concatenate([squares_high, squares_low], axis=3)
 
     query_weight = gathered[:, :256].reshape(2, 2048, 128)
     kv_weight = gathered[:, 256:].reshape(16, 2, 32, 128).transpose(1, 0, 2, 3).reshape(1024, 128)
-    some_tokens = lax.dynamic_slice_in_dim(tokens, (engine % 2) * 1024, 1024, axis=1)
+    some_tokens = lax.dynamic_slice_in_dim(scaled, (engine % 2) * 1024, 1024, axis=1)
     kv_terms = jnp.dot(some_tokens, kv_weight, preferred_element_type=jnp.float32)
     kv_terms = kv_terms.astype(jnp.bfloat16).reshape(4, 1, 128, 128)
     query_terms = jnp.stack(
         [
-            jnp.dot(tokens, query_weight[c], preferred_element_type=jnp.float32)
+            jnp.dot(scaled, query_weight[c], preferred_element_type=jnp.float32)
             .astype(jnp.bfloat16)
             .reshape(4, 128, 128)
             for c in range(2)
@@ -109,29 +124,27 @@
         axis=1,
     )
     terms = jnp.concatenate([query_terms, jnp.broadcast_to(kv_terms, (4, 2, 128, 128))], axis=3)
+    terms = jnp.concatenate([terms, jnp.broadcast_to(squares, (4, 2, 8, 256))], axis=2)
     terms = lax.all_to_all(
-        terms.reshape(8, 128, 256), "tensor", split_axis=0, concat_axis=0, tiled=True
+        terms.reshape(8, 136, 256), "tensor", split_axis=0, concat_axis=0, tiled=True
     )
     total = jnp.sum(terms.astype(jnp.float32), axis=0)
+    mean = (total[128, :128] + total[128, 128:]) / 16384.0
+    total = total[:128] * lax.rsqrt(mean + 1e-05)[:, None]
     kv_all = lax.all_gather(total[:, 128:], "engine", axis=0, tiled=True).reshape(4, 128, 128)
 
-    old = lax.ppermute(jnp.stack([cache_keys[0], cache_values[0]]), AXES, pairs(swap_engine))
-    numbers = jnp.concatenate([positions[0], jnp.broadcast_to(offsets, (128,))]).reshape(2, 128)
-    numbers = lax.ppermute(numbers, AXES, pairs(swap_engine))
+    numbers = group[1024:].astype(jnp.float32)
+    numbers = (numbers[0:2] * 256.0 + numbers[2:4]).astype(jnp.int32)
     places = numbers[0]
     query = rotate(total[:, :128], places).astype(jnp.bfloat16)
     new_keys = rotate(kv_all[0] + kv_all[1], places).astype(jnp.bfloat16)
     new_values = (kv_all[2] + kv_all[3]).astype(jnp.bfloat16)
-    head_out = attend(query, new_keys, new_values, old[0], old[1], numbers[1, 0])
-
-    down = lax.all_gather(output_down_factor, "tensor", axis=0, tiled=True)
-    up = output_up_factor[:, 0, :]
-    delta = lax.dot_general(up, down, (((0,), (1,)), ((), ())), preferred_element_type=jnp.float32)
-    out_shard = (output_base_weight[:, 0, :].T.astype(jnp.float32) + 2.0 * delta).astype(jnp.bfloat16)
-    out_weight = lax.all_gather(out_shard, "fsdp", axis=0, tiled=True)
+    head_out = attend(query, new_keys, new_values, group[:512], group[512:1024], numbers[1, 0])
 
     heads = lax.all_gather(head_out[None], "tensor", axis=0, tiled=True)
-    heads = lax.all_gather(heads[None], "engine", axis=0, tiled=True)
+    heads = lax.all_to_all(
+        jnp.broadcast_to(heads[None], (4, 8, 128, 128)), "engine", split_axis=0, concat_axis=0, tiled=True
+    )
     heads = heads.reshape(4, 4, 2, 128, 128).transpose(1, 3, 0, 2, 4).reshape(512, 1024)
     out = lax.dot_general(
         heads, out_weight, (((1,), (1,)), ((), ())), preferred_element_type=jnp.float32

time: 284 us -> 186 us (0.65)
  the two profiles are of different devices: /device:TPU:8 before, /device:TPU:1 now
where the time goes in v2:
time: 186 us; the launch traced here: 183 us
  blocking collectives  104 us (56%)
  starting transfers between devices  28.1 us (15%)
  waiting for transfers between devices  19.3 us (10%)
  between operations  14.5 us (8%)
  matrix products  6.27 us (3%)
  local copies, waits for them, and re-layouts  6.22 us (3%)
  other arithmetic  4.97 us (3%)
    all_gather x1, blocking collectives, per_device(): down = lax.all_gather(output_down_factor, 'tensor', axis=0, tiled=True)  43.3 us
    all_gather x1, blocking collectives, per_device(): heads = lax.all_gather(head_out[None], 'tensor', axis=0, tiled=True)  17.4 us
    all_to_all x1, blocking collectives, per_device(): lax.all_to_all(jnp.broadcast_to(heads[None], (4, 8, 128, 128)), 'engine',...  17.3 us
    all_to_all x1, waiting for transfers between devices, per_device(): lax.all_to_all(terms.reshape(8, 136, 256), 'tensor', split_axis=0, concat...  16.6 us
    all_gather x1, blocking collectives, per_device(): lax.all_gather(total[:, 128:], 'engine', axis=0, tiled=True)  14.8 us
    ppermute x1, starting transfers between devices, per_device(): query_shard = lax.ppermute(merged_query, AXES, pairs(shard_home))  11.5 us
    all_to_all x1, blocking collectives, per_device(): lax.all_to_all(out.reshape(4, 128, 512), 'engine', split_axis=0, concat_a...  10.7 us
    all_to_all x1, starting transfers between devices, per_device(): lax.all_to_all(jnp.broadcast_to(shard[None], (16, 320, 128)), 'fsdp', spl...  5.73 us
  transfers between devices with their start and end apart: 7, of which 2 were waited for; matrix products, arithmetic and copies ran while one was open for 8% of the time, Pallas kernels for 0%

profile of v2, /device:TPU:1, one launch (start us, length us, event | category | flops | bytes accessed | tf_op | source)
XLA Modules:
  0.0 182.9 jit_solution(15810591635513590027)
XLA Ops:
  6.5 0.7 all-gather.4.cloned.1.call-update
  7.3 0.7 fusion.46
  8.0 0.6 pad_maximum_fusion.2
  8.6 4.8 %all-to-all-start = ((bf16[4,32,128]{2,1,0:T(8,128)(2,1)}), bf16[4,32,128]{2,1,0:T(8,128)(2,1)S(1)}, u32[]{:S(2)}, u32[]{:S(2)}) async-start(bf16[4,32,128]{2,1,0:T(8,128)(2,1)} %pad_maximum_fusion.2), calls=%async_computation | async-start | bytes 65536 | tf_op jit(solution)/shard_map/all_to_all | solution.py:85
  13.4 1.1 fusion.6
  14.5 11.5 %collective-permute-start = (bf16[256,128]{1,0:T(8,128)(2,1)S(1)}, bf16[256,128]{1,0:T(8,128)(2,1)S(1)}, u32[]{:S(2)}, u32[]{:S(2)}) collective-permute-start(bf16[256,128]{1,0:T(8,128)(2,1)S(1)} %fusion.6), channel_id=1, source_target_pairs={{0,0},{1,64},{2,128},{3,192},{4,256},{5,320},{6,384},{7,448},{8,8}... | collective-permute-start | bytes 196616 | tf_op jit(solution)/shard_map/ppermute | solution.py:81
  26.0 2.0 %collective-permute-done = bf16[256,128]{1,0:T(8,128)(2,1)S(1)} collective-permute-done((bf16[256,128]{1,0:T(8,128)(2,1)S(1)}, bf16[256,128]{1,0:T(8,128)(2,1)S(1)}, u32[]{:S(2)}, u32[]{:S(2)}) %collective-permute-start) | collective-permute-done | bytes 65568 | tf_op jit(solution)/shard_map/ppermute | solution.py:81
  28.0 1.3 broadcast_in_dim.23
  29.4 5.7 %all-to-all-start.1 = ((bf16[16,320,128]{2,1,0:T(8,128)(2,1)}), bf16[16,320,128]{2,1,0:T(8,128)(2,1)S(1)}, u32[]{:S(2)}, u32[]{:S(2)}) async-start(bf16[16,320,128]{2,1,0:T(8,128)(2,1)} %broadcast_in_dim.23), calls=%async_computation.1 | async-start | bytes 2621440 | tf_op jit(solution)/shard_map/all_to_all | solution.py:89
  36.1 0.7 collective-permute-start.1
  36.8 43.3 %all_gather.15 = bf16[1024,64]{0,1:T(8,128)(2,1)S(1)} all-gather(bf16[128,64]{0,1:T(8,128)(2,1)S(1)} %copy-done.4), channel_id=1, replica_groups=mesh['engine'=4,'fsdp'=16,'tensor'=8] {'tensor'}, dimensions={0}, use_global_device_ids=true | all-gather | bytes 147456 | tf_op jit(solution)/shard_map/all_gather | solution.py:98
  80.1 0.8 fusion.5
  81.2 2.3 %fusion = (bf16[512,2048]{1,0:T(8,128)(2,1)S(1)}, f32[512]{0:T(512)S(1)}) fusion(bf16[512,2048]{1,0:T(8,128)(2,1)} %all-gather.4.cloned.1.call-done, f32[2048]{0:T(1024)S(1)} %convert_element_type.125), kind=kLoop, calls=%fused_computation.2 | loop fusion | flops 5242368 | bytes 4204544 | tf_op jit(solution)/shard_map/convert_element_type | solution.py:106
  83.4 0.7 convolution_convert_fusion.1
  84.2 0.7 convolution_convert_fusion.2
  84.9 0.4 convolution_convert_fusion.3
  85.4 0.9 pad_maximum_fusion
  86.3 5.3 %all-to-all-start.2 = ((bf16[8,136,256]{2,1,0:T(8,128)(2,1)}), bf16[8,136,256]{2,1,0:T(8,128)(2,1)S(1)}, u32[]{:S(2)}, u32[]{:S(2)}) async-start(bf16[8,136,256]{2,1,0:T(8,128)(2,1)} %bitcast.20), calls=%async_computation.2 | async-start | bytes 1114112 | tf_op jit(solution)/shard_map/all_to_all | solution.py:128
  91.6 0.5 slice.89
  92.1 0.6 iota_compare_fusion.1
  92.8 16.6 %all-to-all-done.2 = bf16[8,136,256]{2,1,0:T(8,128)(2,1)S(1)} async-done(((bf16[8,136,256]{2,1,0:T(8,128)(2,1)}), bf16[8,136,256]{2,1,0:T(8,128)(2,1)S(1)}, u32[]{:S(2)}, u32[]{:S(2)}) %all-to-all-start.2) | async-done | bytes 557088 | tf_op jit(solution)/shard_map/all_to_all | solution.py:128
  109.6 14.8 %all_gather.17 = f32[512,128]{0,1:T(8,128)S(1)} all-gather(f32[128,128]{0,1:T(8,128)S(1)} %slice.115), channel_id=1, replica_groups=mesh['engine'=4,'fsdp'=16,'tensor'=8] {'engine'}, dimensions={0}, use_global_device_ids=true | all-gather | bytes 327680 | tf_op jit(solution)/shard_map/all_gather | solution.py:134
  124.9 0.3 fusion.47
  125.5 0.3 convolution_convert_fusion.4
  125.8 17.4 %all-gather = bf16[1024,128]{1,0:T(8,128)(2,1)S(1)} all-gather(bf16[128,128]{1,0:T(8,128)(2,1)S(1)} %convolution_convert_fusion.4), channel_id=2, replica_groups=mesh['engine'=4,'fsdp'=16,'tensor'=8] {'tensor'}, dimensions={0}, use_global_device_ids=true | all-gather | bytes 294912 | tf_op jit(solution)/shard_map/all_gather | solution.py:144
  143.1 0.2 broadcast_in_dim.34
  143.4 17.3 %all_to_all.25 = bf16[4,8,128,128]{3,2,1,0:T(8,128)(2,1)S(1)} all-to-all(bf16[4,8,128,128]{3,2,1,0:T(8,128)(2,1)S(1)} %broadcast_in_dim.34), channel_id=1, replica_groups=mesh['engine'=4,'fsdp'=16,'tensor'=8] {'engine'}, dimensions={0} | all-to-all | bytes 2097152 | tf_op jit(solution)/shard_map/all_to_all | solution.py:145
  160.7 1.1 copy.43
  161.7 0.8 reshape.130
  162.5 2.0 %convolution_convert_fusion = bf16[512,512]{1,0:T(8,128)(2,1)S(1)} fusion(bf16[512,1024]{1,0:T(8,128)(2,1)S(1)} %reshape.130, bf16[512,1024]{1,0:T(8,128)(2,1)} %all-gather.6.cloned.1.call-done), kind=kOutput, calls=%fused_computation.4 | convolution fusion | flops 537133056 | bytes 2621440 | tf_op jit(solution)/shard_map/dot_general | solution.py:149
  164.5 10.7 %all_to_all.26 = bf16[4,128,512]{2,1,0:T(8,128)(2,1)S(1)} all-to-all(bf16[4,128,512]{2,1,0:T(8,128)(2,1)S(1)} %bitcast.67), channel_id=1, replica_groups=mesh['engine'=4,'fsdp'=16,'tensor'=8] {'engine'}, dimensions={0} | all-to-all | bytes 1048576 | tf_op jit(solution)/shard_map/all_to_all | solution.py:152
  175.2 0.8 copy.46
  (56 shorter events, 1.5 us)
Async XLA Ops:
  6.5 6.9 %copy-start = (bf16[256,64]{0,1:T(8,128)(2,1)S(1)}, bf16[256,64]{0,1:T(8,128)(2,1)}, u32[]{:S(2)}) copy-start(bf16[256,64]{0,1:T(8,128)(2,1)} %param.16) | copy-start | bytes 98308
  6.5 74.6 %all-gather.4.cloned.1.call-start = ((), (), s32[]{:S(2)}) async-start(), calls=%async_computation.5 | async-start | bytes 2621440 | tf_op jit(solution)/shard_map/all_gather | solution.py:75
  8.6 17.4 %all-to-all-start = ((bf16[4,32,128]{2,1,0:T(8,128)(2,1)}), bf16[4,32,128]{2,1,0:T(8,128)(2,1)S(1)}, u32[]{:S(2)}, u32[]{:S(2)}) async-start(bf16[4,32,128]{2,1,0:T(8,128)(2,1)} %pad_maximum_fusion.2), calls=%async_computation | async-start | bytes 65536 | tf_op jit(solution)/shard_map/all_to_all | solution.py:85
  14.5 13.5 %collective-permute-start = (bf16[256,128]{1,0:T(8,128)(2,1)S(1)}, bf16[256,128]{1,0:T(8,128)(2,1)S(1)}, u32[]{:S(2)}, u32[]{:S(2)}) collective-permute-start(bf16[256,128]{1,0:T(8,128)(2,1)S(1)} %fusion.6), channel_id=1, source_target_pairs={{0,0},{1,64},{2,128},{3,192},{4,256},{5,320},{6,384},{7,448},{8,8}... | collective-permute-start | bytes 196616 | tf_op jit(solution)/shard_map/ppermute | solution.py:81
  26.0 9.8 %copy-start.7 = (s32[1,128]{1,0:T(1,128)S(1)}, s32[1,128]{1,0:T(1,128)}, u32[]{:S(2)}) copy-start(s32[1,128]{1,0:T(1,128)} %param.24) | copy-start | bytes 1540
  28.0 7.9 %copy-start.1 = (bf16[1,512,128]{2,1,0:T(8,128)(2,1)S(1)}, bf16[1,512,128]{2,1,0:T(8,128)(2,1)}, u32[]{:S(2)}) copy-start(bf16[1,512,128]{2,1,0:T(8,128)(2,1)} %param.22) | copy-start | bytes 393220
  28.0 7.9 %copy-start.2 = (bf16[1,512,128]{2,1,0:T(8,128)(2,1)S(1)}, bf16[1,512,128]{2,1,0:T(8,128)(2,1)}, u32[]{:S(2)}) copy-start(bf16[1,512,128]{2,1,0:T(8,128)(2,1)} %param.23) | copy-start | bytes 393220
  28.0 8.8 %copy-start.4 = (bf16[128,64]{0,1:T(8,128)(2,1)S(1)}, bf16[128,64]{0,1:T(8,128)(2,1)}, u32[]{:S(2)}) copy-start(bf16[128,64]{0,1:T(8,128)(2,1)} %param.20) | copy-start | bytes 49156
  28.0 52.1 %copy-start.3 = (bf16[1024,1,32]{0,2,1:T(8,128)(2,1)S(1)}, bf16[1024,1,32]{0,2,1:T(8,128)(2,1)}, u32[]{:S(2)}) copy-start(bf16[1024,1,32]{0,2,1:T(8,128)(2,1)} %param.19) | copy-start | bytes 196612
  28.0 52.1 %copy-start.5 = (bf16[64,1,32]{0,2,1:T(8,128)(2,1)S(1)}, bf16[64,1,32]{0,2,1:T(8,128)(2,1)}, u32[]{:S(2)}) copy-start(bf16[64,1,32]{0,2,1:T(8,128)(2,1)} %param.21) | copy-start | bytes 12292
  29.4 51.5 %copy-start.6 = (bf16[2048]{0:T(1024)(128)(2,1)S(1)}, bf16[2048]{0:T(1024)(128)(2,1)}, u32[]{:S(2)}) copy-start(bf16[2048]{0:T(1024)(128)(2,1)} %param.14) | copy-start | bytes 12292
  29.4 51.6 %all-to-all-start.1 = ((bf16[16,320,128]{2,1,0:T(8,128)(2,1)}), bf16[16,320,128]{2,1,0:T(8,128)(2,1)S(1)}, u32[]{:S(2)}, u32[]{:S(2)}) async-start(bf16[16,320,128]{2,1,0:T(8,128)(2,1)} %broadcast_in_dim.23), calls=%async_computation.1 | async-start | bytes 2621440 | tf_op jit(solution)/shard_map/all_to_all | solution.py:89
  35.1 127.4 %all-gather.6.cloned.1.call-start = ((), (), s32[]{:S(2)}) async-start(), calls=%async_computation.6 | async-start | bytes 1114112 | tf_op jit(solution)/shard_map/all_gather | solution.py:103
  36.1 44.9 %collective-permute-start.1 = (bf16[1040,128]{1,0:T(8,128)(2,1)S(1)}, bf16[1040,128]{1,0:T(8,128)(2,1)S(1)}, u32[]{:S(2)}, u32[]{:S(2)}) collective-permute-start(bf16[1040,128]{1,0:T(8,128)(2,1)S(1)} %concatenate.40), channel_id=1, source_target_pairs={{0,0},{1,1},{2,128},{3,129},{4,256},{5,257},{6,384},{7,385},{8,8},... | collective-permute-start | bytes 798728 | tf_op jit(solution)/shard_map/ppermute | solution.py:96
  86.3 23.1 %all-to-all-start.2 = ((bf16[8,136,256]{2,1,0:T(8,128)(2,1)}), bf16[8,136,256]{2,1,0:T(8,128)(2,1)S(1)}, u32[]{:S(2)}, u32[]{:S(2)}) async-start(bf16[8,136,256]{2,1,0:T(8,128)(2,1)} %bitcast.20), calls=%async_computation.2 | async-start | bytes 1114112 | tf_op jit(solution)/shard_map/all_to_all | solution.py:128
Sparse Core Ops, SparseCore 0:
  9.5 44.7 all-gather.3
  81.0 69.7 all-gather.5

commit v3 on v1

v3 whole, which is shorter than its diff:
```python
import jax
import jax.numpy as jnp
from jax import lax
from jax.experimental import pallas as pl
from jax.experimental.pallas import tpu as pltpu
from jax.sharding import PartitionSpec as P

AXES = ("engine", "fsdp", "tensor")


def rotate(values, places):
    half = values.shape[-1] // 2
    index = jnp.arange(half).astype(jnp.float32)
    inverse = jnp.exp(index * (-2.0 / values.shape[-1]) * jnp.log(jnp.float32(500000.0)))
    angle = places.astype(jnp.float32)[:, None] * inverse[None, :]
    cosine = jnp.cos(angle)
    sine = jnp.sin(angle)
    first = values[:, :half]
    second = values[:, half:]
    return jnp.concatenate([first * cosine - second * sine, second * cosine + first * sine], axis=1)


def attend(query, new_keys, new_values, old_keys, old_values, offset):
    tok_count = query.shape[0]
    slots = old_keys.shape[0]
    keys_all = jnp.concatenate([old_keys, new_keys], axis=0)
    values_all = jnp.concatenate([old_values, new_values], axis=0)
    scores = jnp.dot(query, keys_all.T, preferred_element_type=jnp.float32) * query.shape[-1] ** (
        -0.5
    )
    slot_seen = jnp.broadcast_to(jnp.arange(slots)[None, :] < offset, (tok_count, slots))
    rows = jnp.arange(tok_count)
    new_seen = rows[None, :] <= rows[:, None]
    seen = jnp.concatenate([slot_seen, new_seen], axis=1)
    scores = jnp.where(seen, scores, jnp.float32(-1e30))
    top = jnp.max(scores, axis=1, keepdims=True)
    probs = jnp.exp(scores - top)
    weights = (probs / jnp.sum(probs, axis=1, keepdims=True)).astype(jnp.bfloat16)
    return jnp.dot(weights, values_all, preferred_element_type=jnp.float32).astype(jnp.bfloat16)


ACROSS = [[0, 2, 4, 6], [1, 3, 5, 7]]
ALONG_Z = [[2 * z + y for z in range(8)] for y in range(2)]


def shard_home(e, f, t):
    z, y = f // 2, f % 2
    return t // 2, (((t % 2) ^ (z // 4)) * 4 + z % 4) * 2 + y, e * 2 + z // 4


def other_core(e, f, t):
    return e, f, t ^ 1


def other_y(e, f, t):
    return e, f ^ 1, t


def next_engine(e, f, t):
    return (e + 1) % 4, f, t


def last_engine(e, f, t):
    return (e + 3) % 4, f, t


def move(array, where):
    flat = lambda e, f, t: (e * 16 + f) * 8 + t
    pairs = [
        (flat(e, f, t), flat(*where(e, f, t)))
        for e in range(4)
        for f in range(16)
        for t in range(8)
    ]
    return lax.ppermute(array, AXES, pairs)


def from_engines(array):
    half = array.shape[0] // 2
    before, after = move(array, next_engine), move(array, last_engine)
    across_low, across_high = move(before[:half], next_engine), move(after[half:], last_engine)
    return array, after, across_low, across_high, before


def exchange(array, axis, groups=None):
    return lax.all_to_all(
        array, axis, split_axis=0, concat_axis=0, tiled=True, axis_index_groups=groups
    )


def spread(array, axis, groups=None):
    return exchange(jnp.broadcast_to(array[None], (4, *array.shape)), axis, groups)


def split(sums):
    high = sums.astype(jnp.bfloat16)
    return jnp.concatenate([high, (sums - high.astype(jnp.float32)).astype(jnp.bfloat16)], axis=1)


def project_kernel(place_ref, own_ref, other_ref, own_w, after_w, low_w, high_w, before_w, out_ref):
    engine, core = place_ref[0], place_ref[1]
    rows = []
    for i in range(4):
        own, other = own_ref[i], other_ref[i]
        rows += [jnp.where(core == 0, own, other), jnp.where(core == 0, other, own)]
    rows = jnp.concatenate(rows, axis=1)
    heads, down = rows[:128], rows[128:]
    inner = (((1,), (1,)), ((), ()))
    mixed = lax.dot_general(heads, down, inner, preferred_element_type=jnp.float32)
    mixed = (2.0 * mixed).astype(jnp.bfloat16)
    for weight_ref, step, start in (
        (own_w, 0, 0),
        (after_w, 1, 0),
        (low_w, 2, 0),
        (high_w, 2, 256),
        (before_w, 3, 0),
    ):
        width = weight_ref.shape[0]
        out = lax.dot_general(
            heads, weight_ref[:, :1024], inner, preferred_element_type=jnp.float32
        ) + lax.dot_general(
            mixed, weight_ref[:, 1024:1088], inner, preferred_element_type=jnp.float32
        )
        place = pl.multiple_of(lax.rem(engine + step, 4) * 512 + start, 256)
        out_ref[:, pl.ds(place, width)] = out.astype(jnp.bfloat16)


def project(place, own, other, weights):
    return pl.pallas_call(
        project_kernel,
        out_shape=jax.ShapeDtypeStruct((128, 2048), jnp.bfloat16),
        in_specs=[pl.BlockSpec(memory_space=pltpu.SMEM)]
        + [pl.BlockSpec(memory_space=pltpu.VMEM)] * 7,
        out_specs=pl.BlockSpec(memory_space=pltpu.VMEM),
        compiler_params=pltpu.CompilerParams(vmem_limit_bytes=24 * 2**20),
    )(place, own, other, *weights)


def per_device(
    layer_input,
    norm_gain,
    query_base,
    query_down,
    query_up,
    kv_base,
    output_base_weight,
    output_down_factor,
    output_up_factor,
    cache_keys,
    cache_values,
    positions,
    offsets,
):
    engine = lax.axis_index("engine")
    fsdp = lax.axis_index("fsdp")
    core = lax.axis_index("tensor") % 2

    merged_query = (
        query_base.astype(jnp.float32)
        + 2.0 * jnp.dot(query_down, query_up, preferred_element_type=jnp.float32)
    ).astype(jnp.bfloat16)
    merged_query, kv_base = lax.optimization_barrier((merged_query, kv_base))
    query_shard = move(merged_query, shard_home)

    out_shard = jnp.concatenate(
        [output_base_weight[:, 0, :].T, output_up_factor[:, 0, :].T, jnp.zeros((32, 64), jnp.bfloat16)],
        axis=1,
    )
    out_other = move(out_shard, other_y)
    first = fsdp % 2 == 0
    out_shard = jnp.concatenate(
        [jnp.where(first, out_shard, out_other), jnp.where(first, out_other, out_shard)], axis=0
    )
    out_weight = lax.all_gather(out_shard, "fsdp", axis=0, tiled=True, axis_index_groups=ALONG_Z)

    keys_half, values_half = kv_base[0, :, :128], kv_base[0, :, 128:]
    kv_parts = exchange(jnp.stack([keys_half, keys_half, values_half, values_half]), "engine")
    kv_shard = lax.dynamic_slice_in_dim(kv_parts, (engine % 2) * 2, 2, axis=0).reshape(64, 128)

    shard = jnp.concatenate([query_shard, kv_shard], axis=0)
    shards = jnp.broadcast_to(shard[None], (16, 320, 128))
    shards, layer_input = lax.optimization_barrier((shards, layer_input))
    gathered = exchange(shards, "fsdp")

    wide = layer_input.astype(jnp.float32)
    squares = jnp.sum(wide * wide, axis=1)[None]
    scaled = (wide * norm_gain.astype(jnp.float32)[None, :]).astype(jnp.bfloat16)
    tokens = jnp.concatenate(from_engines(scaled), axis=0)
    out_weights = from_engines(out_weight)
    gathered, tokens, squares = lax.optimization_barrier((gathered, tokens, squares))

    query_weight = gathered[:, :256].reshape(2, 2048, 128)
    kv_weight = gathered[:, 256:].reshape(16, 2, 32, 128).transpose(1, 0, 2, 3).reshape(1024, 128)
    some_tokens = lax.dynamic_slice_in_dim(tokens, (engine % 2) * 1024, 1024, axis=1)
    terms = [
        jnp.dot(tokens, query_weight[0], preferred_element_type=jnp.float32),
        jnp.dot(tokens, query_weight[1], preferred_element_type=jnp.float32),
        jnp.dot(some_tokens, kv_weight, preferred_element_type=jnp.float32),
    ]
    terms = jnp.concatenate([term.astype(jnp.bfloat16) for term in terms], axis=1)
    terms = terms.reshape(4, 128, 384)
    terms = lax.dynamic_slice_in_dim(jnp.concatenate([terms, terms]), 4 - engine, 4, axis=0)
    terms = exchange(terms, "engine").astype(jnp.float32)
    kv_terms = jnp.concatenate(
        [terms[0, :, 256:] + terms[1, :, 256:], terms[2, :, 256:] + terms[3, :, 256:]], axis=1
    )
    own = jnp.concatenate([terms[i, :, :128] for i in range(4)] + [kv_terms], axis=1)
    other = jnp.concatenate([terms[i, :, 128:256] for i in range(4)] + [kv_terms], axis=1)
    given = jnp.concatenate(
        [other.astype(jnp.bfloat16), jnp.tile(split(squares), (8, 3))], axis=0
    )
    given = move(given, other_core).astype(jnp.float32)
    own = (own + given[:128]).astype(jnp.bfloat16)
    squares = squares + given[128:129, :128] + given[128:129, 128:256]
    squares = jnp.tile(split(squares), (1, 2))[:, :384]
    terms = jnp.stack(
        [
            jnp.concatenate(
                [
                    jnp.concatenate([own[:, i * 128 : (i + 1) * 128], own[:, 512:]], axis=1),
                    jnp.broadcast_to(squares, (8, 384)),
                ],
                axis=0,
            )
            for i in range(4)
        ]
    )
    terms = exchange(terms, "tensor", ACROSS)
    total = jnp.sum(terms.astype(jnp.float32), axis=0)
    mean = (total[128, :128] + total[128, 128:256]) / 16384.0
    total = total[:128] * lax.rsqrt(mean + 1e-05)[:, None]

    places = positions[0]
    query = rotate(total[:, :128], places).astype(jnp.bfloat16)
    new_keys = rotate(total[:, 128:256], places).astype(jnp.bfloat16)
    new_values = total[:, 256:].astype(jnp.bfloat16)
    head_out = attend(query, new_keys, new_values, cache_keys[0], cache_values[0], offsets[0])

    heads = jnp.concatenate([head_out, output_down_factor.T], axis=0)
    own = spread(heads, "tensor", ACROSS)
    other = move(own, other_core)
    place = jnp.stack([engine, core]).astype(jnp.int32)
    return project(place, own, other, out_weights)


def solution(mesh):
    in_specs = (
        P(("engine", "fsdp"), "tensor"),
        P("tensor"),
        P(("engine", "fsdp"), "tensor"),
        P(("engine", "fsdp"), None),
        P(None, "tensor"),
        P("tensor", ("engine", "fsdp"), None),
        P(None, "tensor", ("engine", "fsdp")),
        P("tensor", None),
        P(None, "tensor", ("engine", "fsdp")),
        P(("engine", "fsdp"), None, None),
        P(("engine", "fsdp"), None, None),
        P(("engine", "fsdp"), None),
        P(("engine", "fsdp")),
    )
    out_specs = P(("engine", "fsdp"), "tensor")
    return jax.shard_map(
        per_device, mesh=mesh, in_specs=in_specs, out_specs=out_specs, check_vma=False
    )
```

time: 284 us -> 187 us (0.66)
  the two profiles are of different devices: /device:TPU:8 before, /device:TPU:1 now
where the time goes in v3:
time: 187 us; the launch traced here: 186 us
  starting transfers between devices  83.1 us (44%)
  waiting for transfers between devices  45.7 us (24%)
  between operations  14.8 us (8%)
  blocking collectives  13.5 us (7%)
  local copies, waits for them, and re-layouts  11.6 us (6%)
  other arithmetic  8.11 us (4%)
  matrix products  5.63 us (3%)
  Pallas kernels  3.66 us (2%)
    ppermute x12, starting transfers between devices, move(): return lax.ppermute(array, AXES, pairs)  61.2 us
    all_gather x1, waiting for transfers between devices, per_device(): lax.all_gather(out_shard, 'fsdp', axis=0, tiled=True, axis_index_groups=A...  30 us
    all_to_all x4, starting transfers between devices, exchange(): lax.all_to_all(array, axis, split_axis=0, concat_axis=0, tiled=True, axis...  21.8 us
    ppermute x12, waiting for transfers between devices, move(): return lax.ppermute(array, AXES, pairs)  15.1 us
    all_to_all x1, blocking collectives, exchange(): lax.all_to_all(array, axis, split_axis=0, concat_axis=0, tiled=True, axis...  13.5 us
    unnamed x32, local copies, waits for them, and re-layouts  5.14 us
  transfers between devices with their start and end apart: 17, of which 9 were waited for; matrix products, arithmetic and copies ran while one was open for 10% of the time, Pallas kernels for 0%

profile of v3, /device:TPU:1, one launch (start us, length us, event | category | flops | bytes accessed | tf_op | source)
XLA Modules:
  0.0 186.1 jit_solution(9185009393538740507)
XLA Ops:
  7.3 1.1 fusion.2
  9.7 4.8 %all-to-all-start = ((bf16[4,32,128]{2,1,0:T(8,128)(2,1)}), bf16[4,32,128]{2,1,0:T(8,128)(2,1)S(1)}, u32[]{:S(2)}, u32[]{:S(2)}) async-start(bf16[4,32,128]{2,1,0:T(8,128)(2,1)} %pad_maximum_fusion.13), calls=%async_computation | async-start | bytes 65536 | tf_op jit(solution)/shard_map/all_to_all | solution.py:86
  14.5 11.5 %collective-permute-start = (bf16[256,128]{1,0:T(8,128)(2,1)S(1)}, bf16[256,128]{1,0:T(8,128)(2,1)S(1)}, u32[]{:S(2)}, u32[]{:S(2)}) collective-permute-start(bf16[256,128]{1,0:T(8,128)(2,1)S(1)} %fusion.2), channel_id=1, source_target_pairs={{0,0},{1,64},{2,128},{3,192},{4,256},{5,320},{6,384},{7,448},{8,8}... | collective-permute-start | bytes 196616 | tf_op jit(solution)/shard_map/ppermute | solution.py:75
  26.1 1.4 collective-permute-done
  27.5 1.3 broadcast_in_dim.18
  28.8 6.1 %all-to-all-start.1 = ((bf16[16,320,128]{2,1,0:T(8,128)(2,1)}), bf16[16,320,128]{2,1,0:T(8,128)(2,1)S(1)}, u32[]{:S(2)}, u32[]{:S(2)}) async-start(bf16[16,320,128]{2,1,0:T(8,128)(2,1)} %broadcast_in_dim.18), calls=%async_computation.1 | async-start | bytes 2621440 | tf_op jit(solution)/shard_map/all_to_all | solution.py:86
  35.1 3.3 %collective-permute-start.7 = (bf16[32,1152]{1,0:T(8,128)(2,1)S(1)}, bf16[32,1152]{1,0:T(8,128)(2,1)}, u32[]{:S(2)}, u32[]{:S(2)}) collective-permute-start(bf16[32,1152]{1,0:T(8,128)(2,1)S(1)} %concatenate.104), channel_id=1, source_target_pairs={{0,8},{1,9},{2,10},{3,11},{4,12},{5,13},{6,14},{7,15},{8,0},{9,1},... | collective-permute-start | bytes 221192 | tf_op jit(solution)/shard_map/ppermute | solution.py:75
  38.4 2.0 %constant_dynamic-update-slice_fusion.4 = (bf16[512,2048]{1,0:T(8,128)(2,1)S(1)}, bf16[128,2048]{1,0:T(8,128)(2,1)}) fusion(f32[2048]{0:T(1024)S(1)} %convert_element_type.86, bf16[128,2048]{1,0:T(8,128)(2,1)} %param.13), kind=kLoop, calls=%fused_computation.77 | loop fusion | flops 786431 | bytes 1581056
  40.4 8.5 %collective-permute-start.1 = (bf16[128,2048]{1,0:T(8,128)(2,1)}, bf16[128,2048]{1,0:T(8,128)(2,1)}, u32[]{:S(2)}, u32[]{:S(2)}) collective-permute-start(bf16[128,2048]{1,0:T(8,128)(2,1)} %get-tuple-element.22), channel_id=1, source_target_pairs={{0,384},{1,385},{2,386},{3,387},{4,388},{5,389},{6,390},{7,391},{8... | collective-permute-start | bytes 1572872 | tf_op jit(solution)/shard_map/ppermute | solution.py:75
  48.9 1.9 %collective-permute-start.2 = (bf16[128,2048]{1,0:T(8,128)(2,1)}, bf16[128,2048]{1,0:T(8,128)(2,1)S(1)}, u32[]{:S(2)}, u32[]{:S(2)}) collective-permute-start(bf16[128,2048]{1,0:T(8,128)(2,1)} %get-tuple-element.22), channel_id=1, source_target_pairs={{0,128},{1,129},{2,130},{3,131},{4,132},{5,133},{6,134},{7,135},{8... | collective-permute-start | bytes 1572872 | tf_op jit(solution)/shard_map/ppermute | solution.py:75
  50.8 1.2 fusion.4
  53.6 6.9 %collective-permute-done.2 = bf16[128,2048]{1,0:T(8,128)(2,1)S(1)} collective-permute-done((bf16[128,2048]{1,0:T(8,128)(2,1)}, bf16[128,2048]{1,0:T(8,128)(2,1)S(1)}, u32[]{:S(2)}, u32[]{:S(2)}) %collective-permute-start.2) | collective-permute-done | bytes 524320 | tf_op jit(solution)/shard_map/ppermute | solution.py:75
  62.1 1.9 %collective-permute-start.3 = (bf16[64,2048]{1,0:T(8,128)(2,1)}, bf16[64,2048]{1,0:T(8,128)(2,1)}, u32[]{:S(2)}, u32[]{:S(2)}) collective-permute-start(bf16[64,2048]{1,0:T(8,128)(2,1)} %slice.169), channel_id=1, source_target_pairs={{0,128},{1,129},{2,130},{3,131},{4,132},{5,133},{6,134},{7,135},{8... | collective-permute-start | bytes 786440 | tf_op jit(solution)/shard_map/ppermute | solution.py:75
  65.7 4.6 %collective-permute-start.4 = (bf16[64,2048]{1,0:T(8,128)(2,1)S(1)}, bf16[64,2048]{1,0:T(8,128)(2,1)S(1)}, u32[]{:S(2)}, u32[]{:S(2)}) collective-permute-start(bf16[64,2048]{1,0:T(8,128)(2,1)S(1)} %slice.170), channel_id=1, source_target_pairs={{0,384},{1,385},{2,386},{3,387},{4,388},{5,389},{6,390},{7,391},{8... | collective-permute-start | bytes 786440 | tf_op jit(solution)/shard_map/ppermute | solution.py:75
  70.3 1.1 constant_dynamic-update-slice_fusion.3
  72.4 1.2 collective-permute-done.4
  77.2 4.4 %all-to-all-start.2 = ((bf16[4,128,384]{2,1,0:T(8,128)(2,1)}), bf16[4,128,384]{2,1,0:T(8,128)(2,1)S(1)}, u32[]{:S(2)}, u32[]{:S(2)}) async-start(bf16[4,128,384]{2,1,0:T(8,128)(2,1)} %fusion.6), calls=%async_computation.2 | async-start | bytes 786432 | tf_op jit(solution)/shard_map/all_to_all | solution.py:86
  81.6 30.0 %all-gather.2.cloned.1.call-done.own_w = bf16[512,1152]{1,0:T(8,128)(2,1)} async-done(((bf16[64,1152]{1,0:T(8,128)(2,1)}), bf16[512,1152]{1,0:T(8,128)(2,1)}) %all-gather.2.cloned.1.call-update) | async-done | bytes 1179664 | tf_op jit(solution)/shard_map/all_gather | solution.py:174
  111.6 3.1 %collective-permute-start.9 = (bf16[512,1152]{1,0:T(8,128)(2,1)}, bf16[512,1152]{1,0:T(8,128)(2,1)S(1)}, u32[]{:S(2)}, u32[]{:S(2)}) collective-permute-start(bf16[512,1152]{1,0:T(8,128)(2,1)} %all-gather.2.cloned.1.call-done.own_w), channel_id=1, source_target_pairs={{0,128},{1,129},{2,130},{3,131},{4,132},{5,133},{6,134},{7,135},{8... | collective-permute-start | bytes 3538952 | tf_op jit(solution)/shard_map/ppermute | solution.py:75
  114.7 3.4 %collective-permute-start.8 = (bf16[512,1152]{1,0:T(8,128)(2,1)}, bf16[512,1152]{1,0:T(8,128)(2,1)S(1)}, u32[]{:S(2)}, u32[]{:S(2)}) collective-permute-start(bf16[512,1152]{1,0:T(8,128)(2,1)} %all-gather.2.cloned.1.call-done.own_w), channel_id=1, source_target_pairs={{0,384},{1,385},{2,386},{3,387},{4,388},{5,389},{6,390},{7,391},{8... | collective-permute-start | bytes 3538952 | tf_op jit(solution)/shard_map/ppermute | solution.py:75
  118.4 7.0 %collective-permute-start.5 = (bf16[136,768]{1,0:T(8,128)(2,1)S(1)}, bf16[136,768]{1,0:T(8,128)(2,1)S(1)}, u32[]{:S(2)}, u32[]{:S(2)}) collective-permute-start(bf16[136,768]{1,0:T(8,128)(2,1)S(1)} %pad_maximum_fusion.6), channel_id=1, source_target_pairs={{0,1},{1,0},{2,3},{3,2},{4,5},{5,4},{6,7},{7,6},{8,9},{9,8},{10,11... | collective-permute-start | bytes 626696 | tf_op jit(solution)/shard_map/ppermute | solution.py:75
  125.5 1.0 collective-permute-done.5
  127.7 6.5 %all-to-all-start.3 = ((bf16[4,136,384]{2,1,0:T(8,128)(2,1)}), bf16[4,136,384]{2,1,0:T(8,128)(2,1)S(1)}, u32[]{:S(2)}, u32[]{:S(2)}) async-start(bf16[4,136,384]{2,1,0:T(8,128)(2,1)} %pad_maximum_fusion), calls=%async_computation.3 | async-start | bytes 835584 | tf_op jit(solution)/shard_map/all_to_all | solution.py:86
  134.9 2.8 %collective-permute-done.9.before_w = bf16[512,1152]{1,0:T(8,128)(2,1)S(1)} collective-permute-done((bf16[512,1152]{1,0:T(8,128)(2,1)}, bf16[512,1152]{1,0:T(8,128)(2,1)S(1)}, u32[]{:S(2)}, u32[]{:S(2)}) %collective-permute-start.9) | collective-permute-done | bytes 1179680 | tf_op jit(solution)/shard_map/ppermute | solution.py:75
  138.7 1.9 %collective-permute-start.10 = (bf16[256,1152]{1,0:T(8,128)(2,1)}, bf16[256,1152]{1,0:T(8,128)(2,1)S(1)}, u32[]{:S(2)}, u32[]{:S(2)}) collective-permute-start(bf16[256,1152]{1,0:T(8,128)(2,1)} %slice.199), channel_id=1, source_target_pairs={{0,128},{1,129},{2,130},{3,131},{4,132},{5,133},{6,134},{7,135},{8... | collective-permute-start | bytes 1769480 | tf_op jit(solution)/shard_map/ppermute | solution.py:75
  141.5 4.6 %collective-permute-start.11 = (bf16[256,1152]{1,0:T(8,128)(2,1)}, bf16[256,1152]{1,0:T(8,128)(2,1)}, u32[]{:S(2)}, u32[]{:S(2)}) collective-permute-start(bf16[256,1152]{1,0:T(8,128)(2,1)} %slice.200), channel_id=1, source_target_pairs={{0,384},{1,385},{2,386},{3,387},{4,388},{5,389},{6,390},{7,391},{8... | collective-permute-start | bytes 1769480 | tf_op jit(solution)/shard_map/ppermute | solution.py:75
  147.4 1.2 fusion.54
  148.8 1.2 convolution_convert_fusion.3
  150.1 13.5 %all_to_all.25.own_ref = bf16[4,192,128]{2,1,0:T(8,128)(2,1)S(1)} all-to-all(bf16[4,192,128]{2,1,0:T(8,128)(2,1)S(1)} %broadcast_in_dim.23), channel_id=1, replica_groups={{0,2,4,6},{1,3,5,7},{8,10,12,14},{9,11,13,15},{16,18,20,22},{17,19,21,2..., dimensions={0} | all-to-all | bytes 393216 | tf_op jit(solution)/shard_map/all_to_all | solution.py:86
  163.6 9.6 %collective-permute-start.6 = (bf16[4,192,128]{2,1,0:T(8,128)(2,1)S(1)}, bf16[4,192,128]{2,1,0:T(8,128)(2,1)S(1)}, u32[]{:S(2)}, u32[]{:S(2)}) collective-permute-start(bf16[4,192,128]{2,1,0:T(8,128)(2,1)S(1)} %all_to_all.25.own_ref), channel_id=1, source_target_pairs={{0,1},{1,0},{2,3},{3,2},{4,5},{5,4},{6,7},{7,6},{8,9},{9,8},{10,11... | collective-permute-start | bytes 589832 | tf_op jit(solution)/shard_map/ppermute | solution.py:75
  174.3 1.3 copy-done.1
  175.5 3.7 %shard_map.127 = bf16[128,2048]{1,0:T(8,128)(2,1)} custom-call(s32[2]{0:T(128)S(1)} %pad_add_fusion.place_ref, bf16[4,192,128]{2,1,0:T(8,128)(2,1)S(1)} %all_to_all.25.own_ref, bf16[4,192,128]{2,1,0:T(8,128)(2,1)S(1)} %collective-permute-done.6.other_ref, bf16[512,1152]{1,0:T(8,128)(2,1)S(1)} %copy-done.1, ...), custom_call_target="tpu_custom_call" | custom-call | tf_op jit(solution)/shard_map/pallas_call | solution.py:129
  (107 shorter events, 17.2 us)
Async XLA Ops:
  6.5 0.8 copy-start
  9.7 16.3 %all-to-all-start = ((bf16[4,32,128]{2,1,0:T(8,128)(2,1)}), bf16[4,32,128]{2,1,0:T(8,128)(2,1)S(1)}, u32[]{:S(2)}, u32[]{:S(2)}) async-start(bf16[4,32,128]{2,1,0:T(8,128)(2,1)} %pad_maximum_fusion.13), calls=%async_computation | async-start | bytes 65536 | tf_op jit(solution)/shard_map/all_to_all | solution.py:86
  14.5 13.0 %collective-permute-start = (bf16[256,128]{1,0:T(8,128)(2,1)S(1)}, bf16[256,128]{1,0:T(8,128)(2,1)S(1)}, u32[]{:S(2)}, u32[]{:S(2)}) collective-permute-start(bf16[256,128]{1,0:T(8,128)(2,1)S(1)} %fusion.2), channel_id=1, source_target_pairs={{0,0},{1,64},{2,128},{3,192},{4,256},{5,320},{6,384},{7,448},{8,8}... | collective-permute-start | bytes 196616 | tf_op jit(solution)/shard_map/ppermute | solution.py:75
  26.0 8.9 %copy-start.4 = (bf16[1024,1,32]{0,2,1:T(8,128)(2,1)S(1)}, bf16[1024,1,32]{0,2,1:T(8,128)(2,1)}, u32[]{:S(2)}) copy-start(bf16[1024,1,32]{0,2,1:T(8,128)(2,1)} %param.19) | copy-start | bytes 196612
  26.1 8.9 %copy-start.6 = (bf16[64,1,32]{0,2,1:T(8,128)(2,1)S(1)}, bf16[64,1,32]{0,2,1:T(8,128)(2,1)}, u32[]{:S(2)}) copy-start(bf16[64,1,32]{0,2,1:T(8,128)(2,1)} %param.21) | copy-start | bytes 12292
  27.5 10.9 %copy-start.7 = (bf16[2048]{0:T(1024)(128)(2,1)S(1)}, bf16[2048]{0:T(1024)(128)(2,1)}, u32[]{:S(2)}) copy-start(bf16[2048]{0:T(1024)(128)(2,1)} %param.14) | copy-start | bytes 12292
  28.8 44.8 %all-to-all-start.1 = ((bf16[16,320,128]{2,1,0:T(8,128)(2,1)}), bf16[16,320,128]{2,1,0:T(8,128)(2,1)S(1)}, u32[]{:S(2)}, u32[]{:S(2)}) async-start(bf16[16,320,128]{2,1,0:T(8,128)(2,1)} %broadcast_in_dim.18), calls=%async_computation.1 | async-start | bytes 2621440 | tf_op jit(solution)/shard_map/all_to_all | solution.py:86
  34.9 76.7 %all-gather.2.cloned.1.call-start = ((), (), s32[]{:S(2)}) async-start(), calls=%async_computation.5 | async-start | bytes 1327104 | tf_op jit(solution)/shard_map/all_gather | solution.py:174
  35.1 17.6 %collective-permute-start.7 = (bf16[32,1152]{1,0:T(8,128)(2,1)S(1)}, bf16[32,1152]{1,0:T(8,128)(2,1)}, u32[]{:S(2)}, u32[]{:S(2)}) collective-permute-start(bf16[32,1152]{1,0:T(8,128)(2,1)S(1)} %concatenate.104), channel_id=1, source_target_pairs={{0,8},{1,9},{2,10},{3,11},{4,12},{5,13},{6,14},{7,15},{8,0},{9,1},... | collective-permute-start | bytes 221192 | tf_op jit(solution)/shard_map/ppermute | solution.py:75
  40.4 24.3 %collective-permute-start.1 = (bf16[128,2048]{1,0:T(8,128)(2,1)}, bf16[128,2048]{1,0:T(8,128)(2,1)}, u32[]{:S(2)}, u32[]{:S(2)}) collective-permute-start(bf16[128,2048]{1,0:T(8,128)(2,1)} %get-tuple-element.22), channel_id=1, source_target_pairs={{0,384},{1,385},{2,386},{3,387},{4,388},{5,389},{6,390},{7,391},{8... | collective-permute-start | bytes 1572872 | tf_op jit(solution)/shard_map/ppermute | solution.py:75
  48.9 11.6 %collective-permute-start.2 = (bf16[128,2048]{1,0:T(8,128)(2,1)}, bf16[128,2048]{1,0:T(8,128)(2,1)S(1)}, u32[]{:S(2)}, u32[]{:S(2)}) collective-permute-start(bf16[128,2048]{1,0:T(8,128)(2,1)} %get-tuple-element.22), channel_id=1, source_target_pairs={{0,128},{1,129},{2,130},{3,131},{4,132},{5,133},{6,134},{7,135},{8... | collective-permute-start | bytes 1572872 | tf_op jit(solution)/shard_map/ppermute | solution.py:75
  60.5 0.8 copy-start.2
  62.1 9.3 %collective-permute-start.3 = (bf16[64,2048]{1,0:T(8,128)(2,1)}, bf16[64,2048]{1,0:T(8,128)(2,1)}, u32[]{:S(2)}, u32[]{:S(2)}) collective-permute-start(bf16[64,2048]{1,0:T(8,128)(2,1)} %slice.169), channel_id=1, source_target_pairs={{0,128},{1,129},{2,130},{3,131},{4,132},{5,133},{6,134},{7,135},{8... | collective-permute-start | bytes 786440 | tf_op jit(solution)/shard_map/ppermute | solution.py:75
  64.7 8.9 %copy-start.3 = (bf16[128,2048]{1,0:T(8,128)(2,1)S(1)}, bf16[128,2048]{1,0:T(8,128)(2,1)}, u32[]{:S(2)}) copy-start(bf16[128,2048]{1,0:T(8,128)(2,1)} %copy-done.2) | copy-start | bytes 1572868
  65.7 7.9 %collective-permute-start.4 = (bf16[64,2048]{1,0:T(8,128)(2,1)S(1)}, bf16[64,2048]{1,0:T(8,128)(2,1)S(1)}, u32[]{:S(2)}, u32[]{:S(2)}) collective-permute-start(bf16[64,2048]{1,0:T(8,128)(2,1)S(1)} %slice.170), channel_id=1, source_target_pairs={{0,384},{1,385},{2,386},{3,387},{4,388},{5,389},{6,390},{7,391},{8... | collective-permute-start | bytes 786440 | tf_op jit(solution)/shard_map/ppermute | solution.py:75
  77.2 41.0 %all-to-all-start.2 = ((bf16[4,128,384]{2,1,0:T(8,128)(2,1)}), bf16[4,128,384]{2,1,0:T(8,128)(2,1)S(1)}, u32[]{:S(2)}, u32[]{:S(2)}) async-start(bf16[4,128,384]{2,1,0:T(8,128)(2,1)} %fusion.6), calls=%async_computation.2 | async-start | bytes 786432 | tf_op jit(solution)/shard_map/all_to_all | solution.py:86
  111.6 26.2 %collective-permute-start.9 = (bf16[512,1152]{1,0:T(8,128)(2,1)}, bf16[512,1152]{1,0:T(8,128)(2,1)S(1)}, u32[]{:S(2)}, u32[]{:S(2)}) collective-permute-start(bf16[512,1152]{1,0:T(8,128)(2,1)} %all-gather.2.cloned.1.call-done.own_w), channel_id=1, source_target_pairs={{0,128},{1,129},{2,130},{3,131},{4,132},{5,133},{6,134},{7,135},{8... | collective-permute-start | bytes 3538952 | tf_op jit(solution)/shard_map/ppermute | solution.py:75
  114.7 25.9 %collective-permute-start.8 = (bf16[512,1152]{1,0:T(8,128)(2,1)}, bf16[512,1152]{1,0:T(8,128)(2,1)S(1)}, u32[]{:S(2)}, u32[]{:S(2)}) collective-permute-start(bf16[512,1152]{1,0:T(8,128)(2,1)} %all-gather.2.cloned.1.call-done.own_w), channel_id=1, source_target_pairs={{0,384},{1,385},{2,386},{3,387},{4,388},{5,389},{6,390},{7,391},{8... | collective-permute-start | bytes 3538952 | tf_op jit(solution)/shard_map/ppermute | solution.py:75
  118.4 8.1 %collective-permute-start.5 = (bf16[136,768]{1,0:T(8,128)(2,1)S(1)}, bf16[136,768]{1,0:T(8,128)(2,1)S(1)}, u32[]{:S(2)}, u32[]{:S(2)}) collective-permute-start(bf16[136,768]{1,0:T(8,128)(2,1)S(1)} %pad_maximum_fusion.6), channel_id=1, source_target_pairs={{0,1},{1,0},{2,3},{3,2},{4,5},{5,4},{6,7},{7,6},{8,9},{9,8},{10,11... | collective-permute-start | bytes 626696 | tf_op jit(solution)/shard_map/ppermute | solution.py:75
  126.6 8.3 %copy-start.8 = (s32[1,128]{1,0:T(1,128)S(1)}, s32[1,128]{1,0:T(1,128)}, u32[]{:S(2)}) copy-start(s32[1,128]{1,0:T(1,128)} %param.24) | copy-start | bytes 1540
  127.7 18.9 %all-to-all-start.3 = ((bf16[4,136,384]{2,1,0:T(8,128)(2,1)}), bf16[4,136,384]{2,1,0:T(8,128)(2,1)S(1)}, u32[]{:S(2)}, u32[]{:S(2)}) async-start(bf16[4,136,384]{2,1,0:T(8,128)(2,1)} %pad_maximum_fusion), calls=%async_computation.3 | async-start | bytes 835584 | tf_op jit(solution)/shard_map/all_to_all | solution.py:86
  138.7 34.7 %collective-permute-start.10 = (bf16[256,1152]{1,0:T(8,128)(2,1)}, bf16[256,1152]{1,0:T(8,128)(2,1)S(1)}, u32[]{:S(2)}, u32[]{:S(2)}) collective-permute-start(bf16[256,1152]{1,0:T(8,128)(2,1)} %slice.199), channel_id=1, source_target_pairs={{0,128},{1,129},{2,130},{3,131},{4,132},{5,133},{6,134},{7,135},{8... | collective-permute-start | bytes 1769480 | tf_op jit(solution)/shard_map/ppermute | solution.py:75
  141.5 31.9 %collective-permute-start.11 = (bf16[256,1152]{1,0:T(8,128)(2,1)}, bf16[256,1152]{1,0:T(8,128)(2,1)}, u32[]{:S(2)}, u32[]{:S(2)}) collective-permute-start(bf16[256,1152]{1,0:T(8,128)(2,1)} %slice.200), channel_id=1, source_target_pairs={{0,384},{1,385},{2,386},{3,387},{4,388},{5,389},{6,390},{7,391},{8... | collective-permute-start | bytes 1769480 | tf_op jit(solution)/shard_map/ppermute | solution.py:75
  146.7 3.3 %copy-start.5 = (bf16[128,64]{0,1:T(8,128)(2,1)S(1)}, bf16[128,64]{0,1:T(8,128)(2,1)}, u32[]{:S(2)}) copy-start(bf16[128,64]{0,1:T(8,128)(2,1)} %param.20) | copy-start | bytes 49156
  163.6 10.7 %collective-permute-start.6 = (bf16[4,192,128]{2,1,0:T(8,128)(2,1)S(1)}, bf16[4,192,128]{2,1,0:T(8,128)(2,1)S(1)}, u32[]{:S(2)}, u32[]{:S(2)}) collective-permute-start(bf16[4,192,128]{2,1,0:T(8,128)(2,1)S(1)} %all_to_all.25.own_ref), channel_id=1, source_target_pairs={{0,1},{1,0},{2,3},{3,2},{4,5},{5,4},{6,7},{7,6},{8,9},{9,8},{10,11... | collective-permute-start | bytes 589832 | tf_op jit(solution)/shard_map/ppermute | solution.py:75
  174.3 1.3 copy-start.1
Sparse Core Ops, SparseCore 0:
  64.8 46.7 all-gather.1

commit v4 on v3

v4 whole, which is shorter than its diff:
```python
import jax
import jax.numpy as jnp
from jax import lax
from jax.experimental import pallas as pl
from jax.experimental.pallas import tpu as pltpu
from jax.sharding import PartitionSpec as P

AXES = ("engine", "fsdp", "tensor")


def rotate(values, places):
    half = values.shape[-1] // 2
    index = jnp.arange(half).astype(jnp.float32)
    inverse = jnp.exp(index * (-2.0 / values.shape[-1]) * jnp.log(jnp.float32(500000.0)))
    angle = places.astype(jnp.float32)[:, None] * inverse[None, :]
    cosine = jnp.cos(angle)
    sine = jnp.sin(angle)
    first = values[:, :half]
    second = values[:, half:]
    return jnp.concatenate([first * cosine - second * sine, second * cosine + first * sine], axis=1)


def attend(query, new_keys, new_values, old_keys, old_values, offset):
    tok_count = query.shape[0]
    slots = old_keys.shape[0]
    keys_all = jnp.concatenate([old_keys, new_keys], axis=0)
    values_all = jnp.concatenate([old_values, new_values], axis=0)
    scores = jnp.dot(query, keys_all.T, preferred_element_type=jnp.float32) * query.shape[-1] ** (
        -0.5
    )
    slot_seen = jnp.broadcast_to(jnp.arange(slots)[None, :] < offset, (tok_count, slots))
    rows = jnp.arange(tok_count)
    new_seen = rows[None, :] <= rows[:, None]
    seen = jnp.concatenate([slot_seen, new_seen], axis=1)
    scores = jnp.where(seen, scores, jnp.float32(-1e30))
    top = jnp.max(scores, axis=1, keepdims=True)
    probs = jnp.exp(scores - top)
    weights = (probs / jnp.sum(probs, axis=1, keepdims=True)).astype(jnp.bfloat16)
    return jnp.dot(weights, values_all, preferred_element_type=jnp.float32).astype(jnp.bfloat16)


ACROSS = [[0, 2, 4, 6], [1, 3, 5, 7]]
CORES = [[0, 1], [2, 3], [4, 5], [6, 7]]
ALONG_Z = [[2 * z + y for z in range(8)] for y in range(2)]


def shard_home(e, f, t):
    z, y = f // 2, f % 2
    home = z if t % 2 == z // 4 else 7 - z
    return t // 2, home * 2 + y, e * 2 + z // 4


def other_core(e, f, t):
    return e, f, t ^ 1


def other_y(e, f, t):
    return e, f ^ 1, t


def next_engine(e, f, t):
    return (e + 1) % 4, f, t


def last_engine(e, f, t):
    return (e + 3) % 4, f, t


def move(array, where):
    flat = lambda e, f, t: (e * 16 + f) * 8 + t
    pairs = [
        (flat(e, f, t), flat(*where(e, f, t)))
        for e in range(4)
        for f in range(16)
        for t in range(8)
    ]
    return lax.ppermute(array, AXES, pairs)


def exchange(array, axis, groups=None):
    return lax.all_to_all(
        array, axis, split_axis=0, concat_axis=0, tiled=True, axis_index_groups=groups
    )


def spread(array, count, axis, groups=None):
    return exchange(jnp.broadcast_to(array[None], (count, *array.shape)), axis, groups)


def split(sums):
    high = sums.astype(jnp.bfloat16)
    return jnp.concatenate([high, (sums - high.astype(jnp.float32)).astype(jnp.bfloat16)], axis=1)


def terms_kernel(place_ref, weight_ref, *refs):
    token_refs, out_ref = refs[:-1], refs[-1]
    engine, core = place_ref[0], place_ref[1]
    own = weight_ref[pl.ds(core * 8, 8), :256].reshape(2048, 128)
    other = weight_ref[pl.ds((1 - core) * 8, 8), :256].reshape(4, 512, 128)
    other = jnp.concatenate([other[3 - i] for i in range(4)], axis=0)
    query_weight = jnp.concatenate([own, other], axis=1)
    kv_weight = jnp.concatenate(
        [weight_ref[:, i : i + 32].reshape(512, 128) for i in (256, 288)], axis=1
    )
    some = pl.ds(pl.multiple_of(engine * 512, 512), 512)
    for ref, step, start in zip(token_refs, (0, 1, 2, 2, 3), (0, 0, 0, 64, 0), strict=True):
        rows = ref.shape[0]
        terms = jnp.concatenate(
            [
                jnp.dot(ref[...], query_weight, preferred_element_type=jnp.float32),
                jnp.dot(ref[:, some], kv_weight, preferred_element_type=jnp.float32),
            ],
            axis=1,
        )
        out_ref[lax.rem(engine + step, 4), start : start + rows] = terms.astype(jnp.bfloat16)


def project_kernel(place_ref, own_ref, other_ref, *refs):
    weight_refs, out_ref, weight_ref = refs[:8], refs[8], refs[9]
    engine, core, y = place_ref[0], place_ref[1], place_ref[2]
    rows = []
    for i in range(4):
        own, other = own_ref[i], other_ref[i]
        rows += [jnp.where(core == 0, own, other), jnp.where(core == 0, other, own)]
    rows = jnp.concatenate(rows, axis=1)
    heads, down = rows[:128], rows[128:]
    inner = (((1,), (1,)), ((), ()))
    mixed = lax.dot_general(heads, down, inner, preferred_element_type=jnp.float32)
    mixed = (2.0 * mixed).astype(jnp.bfloat16)
    heads = jnp.concatenate([heads, mixed, jnp.zeros_like(mixed)], axis=1)
    for step in range(4):
        for ref, half in zip(weight_refs[2 * step : 2 * step + 2], (y, 1 - y), strict=True):
            for z in range(8):
                at = pl.multiple_of(z * 64 + half * 32, 32)
                weight_ref[step, pl.ds(at, 32)] = ref[z * 32 : z * 32 + 32]
        out = lax.dot_general(
            heads, weight_ref[step], inner, preferred_element_type=jnp.float32
        )
        place = pl.multiple_of(lax.rem(engine + step, 4) * 512, 512)
        out_ref[:, pl.ds(place, 512)] = out.astype(jnp.bfloat16)


def compute(kernel, shape, place, arrays, scratch=()):
    return pl.pallas_call(
        kernel,
        out_shape=jax.ShapeDtypeStruct(shape, jnp.bfloat16),
        in_specs=[pl.BlockSpec(memory_space=pltpu.SMEM)]
        + [pl.BlockSpec(memory_space=pltpu.VMEM)] * len(arrays),
        out_specs=pl.BlockSpec(memory_space=pltpu.VMEM),
        scratch_shapes=[pltpu.VMEM(sizes, jnp.bfloat16) for sizes in scratch],
        compiler_params=pltpu.CompilerParams(vmem_limit_bytes=24 * 2**20),
    )(place, *arrays)


def per_device(
    layer_input,
    norm_gain,
    query_base,
    query_down,
    query_up,
    kv_base,
    output_base_weight,
    output_down_factor,
    output_up_factor,
    cache_keys,
    cache_values,
    positions,
    offsets,
):
    engine = lax.axis_index("engine")
    core = lax.axis_index("tensor") % 2
    place = jnp.stack([engine, core, lax.axis_index("fsdp") % 2]).astype(jnp.int32)

    merged_query = (
        query_base.astype(jnp.float32)
        + 2.0 * jnp.dot(query_down, query_up, preferred_element_type=jnp.float32)
    ).astype(jnp.bfloat16)
    out_shard = jnp.concatenate(
        [output_base_weight[:, 0, :].T, output_up_factor[:, 0, :].T, jnp.zeros((32, 64), jnp.bfloat16)],
        axis=1,
    )
    merged_query, out_shard = lax.optimization_barrier((merged_query, out_shard))
    query_shard = move(merged_query, shard_home)
    mine = spread(out_shard, 8, "fsdp", ALONG_Z).reshape(256, 1152)

    shard = jnp.concatenate([query_shard, kv_base[0, :, :128], kv_base[0, :, 128:]], axis=0)
    shards = jnp.broadcast_to(shard[None], (16, 320, 128))
    shards, mine, layer_input = lax.optimization_barrier((shards, mine, layer_input))
    gathered = exchange(shards, "fsdp")

    wide = layer_input.astype(jnp.float32)
    squares = jnp.sum(wide * wide, axis=1)[None]
    squares = lax.all_gather(squares, "tensor", axis=0, tiled=True, axis_index_groups=CORES)
    squares = jnp.sum(squares, axis=0, keepdims=True)
    scaled = (wide * norm_gain.astype(jnp.float32)[None, :]).astype(jnp.bfloat16)
    scaled, squares, mine = lax.optimization_barrier((scaled, squares, mine))
    before, after = move(scaled, next_engine), move(scaled, last_engine)
    theirs = move(mine, other_y)
    across_low, across_high = move(before[:64], next_engine), move(after[64:], last_engine)
    tokens = (scaled, after, across_low, across_high, before)

    terms = compute(terms_kernel, (4, 128, 512), place, (gathered, *tokens))
    terms, theirs = lax.optimization_barrier((terms, theirs))
    mine_before, theirs_after = move(mine, next_engine), move(theirs, last_engine)
    mine_after, theirs_before = move(mine, last_engine), move(theirs, next_engine)
    terms = exchange(terms, "engine").astype(jnp.float32)
    kv_terms = jnp.sum(terms[:, :, 256:], axis=0)
    own = jnp.concatenate([terms[i, :, :128] for i in range(4)] + [kv_terms], axis=1)
    other = jnp.concatenate([terms[i, :, 128:256] for i in range(4)] + [kv_terms], axis=1)
    given = move(other.astype(jnp.bfloat16), other_core).astype(jnp.float32)
    own = (own + given).astype(jnp.bfloat16)
    squares = jnp.tile(split(squares), (1, 2))[:, :384]
    terms = jnp.stack(
        [
            jnp.concatenate(
                [
                    jnp.concatenate([own[:, i * 128 : (i + 1) * 128], own[:, 512:]], axis=1),
                    jnp.broadcast_to(squares, (8, 384)),
                ],
                axis=0,
            )
            for i in range(4)
        ]
    )
    terms, mine_before, mine_after, theirs_before, theirs_after = lax.optimization_barrier(
        (terms, mine_before, mine_after, theirs_before, theirs_after)
    )
    mine_across, theirs_across = move(mine_before, next_engine), move(theirs_after, last_engine)
    terms = exchange(terms, "tensor", ACROSS)
    total = jnp.sum(terms.astype(jnp.float32), axis=0)
    mean = (total[128, :128] + total[128, 128:256]) / 16384.0
    total = total[:128] * lax.rsqrt(mean + 1e-05)[:, None]

    places = positions[0]
    query = rotate(total[:, :128], places).astype(jnp.bfloat16)
    new_keys = rotate(total[:, 128:256], places).astype(jnp.bfloat16)
    new_values = total[:, 256:].astype(jnp.bfloat16)
    head_out = attend(query, new_keys, new_values, cache_keys[0], cache_values[0], offsets[0])

    head_out, mine_across, theirs_across = lax.optimization_barrier(
        (head_out, mine_across, theirs_across)
    )
    heads = jnp.concatenate([head_out, output_down_factor.T], axis=0)
    own = spread(heads, 4, "tensor", ACROSS)
    other = move(own, other_core)
    out_weights = (
        mine, theirs, mine_after, theirs_after, mine_across, theirs_across, mine_before, theirs_before
    )
    return compute(
        project_kernel, (128, 2048), place, (own, other, *out_weights), ((4, 512, 1152),)
    )


def solution(mesh):
    in_specs = (
        P(("engine", "fsdp"), "tensor"),
        P("tensor"),
        P(("engine", "fsdp"), "tensor"),
        P(("engine", "fsdp"), None),
        P(None, "tensor"),
        P("tensor", ("engine", "fsdp"), None),
        P(None, "tensor", ("engine", "fsdp")),
        P("tensor", None),
        P(None, "tensor", ("engine", "fsdp")),
        P(("engine", "fsdp"), None, None),
        P(("engine", "fsdp"), None, None),
        P(("engine", "fsdp"), None),
        P(("engine", "fsdp")),
    )
    out_specs = P(("engine", "fsdp"), "tensor")
    return jax.shard_map(
        per_device, mesh=mesh, in_specs=in_specs, out_specs=out_specs, check_vma=False
    )
```

time: 187 us -> 157 us (0.84)
  between operations: 14.8 us -> 1.21 us
  waiting for transfers between devices: 45.7 us -> 38.9 us
  local copies, waits for them, and re-layouts: 11.6 us -> 5.21 us
  other arithmetic: 8.11 us -> 3.03 us
  blocking collectives: 13.5 us -> 17 us
  Pallas kernels: 3.66 us -> 6.85 us
  matrix products: 5.63 us -> 2.56 us
  starting transfers between devices: 83.1 us -> 80.7 us
    all_gather x1 -> x0, waiting for transfers between devices: 30 us -> none  [per_device(): lax.all_gather(out_shard, 'fsdp', axis=0, tiled=True, axis_index_groups=A...]
    ppermute x12 -> x14, waiting for transfers between devices: 15.1 us -> 33.2 us  [move(): return lax.ppermute(array, AXES, pairs)]
    ppermute x12 -> x14, starting transfers between devices: 61.2 us -> 54.5 us  [move(): return lax.ppermute(array, AXES, pairs)]
    all_to_all x4, waiting for transfers between devices: 0.61 us -> 5.64 us  [exchange(): lax.all_to_all(array, axis, split_axis=0, concat_axis=0, tiled=True, axis...]
    unnamed x32 -> x25, local copies, waits for them, and re-layouts: 5.14 us -> 0.26 us
    all_to_all x4, starting transfers between devices: 21.8 us -> 26.2 us  [exchange(): lax.all_to_all(array, axis, split_axis=0, concat_axis=0, tiled=True, axis...]
    pallas_call x1 -> x2, Pallas kernels: 3.66 us -> 6.85 us  [compute(): pl.pallas_call(kernel, out_shape=jax.ShapeDtypeStruct(shape, jnp.bfloat16...]
    slice x7 -> x2, local copies, waits for them, and re-layouts: 4.32 us -> 1.43 us  [the longest x1 0.72 us: per_device(): before[:64]]
  transfers between devices with their start and end apart: 17 -> 18, of which waited for: 9 -> 11; matrix products, arithmetic and copies ran while one was open for 10% -> 4% of each run, Pallas kernels for 0% -> 2%
where the time goes in v4:
time: 157 us; the launch traced here: 155 us
  starting transfers between devices  80.7 us (51%)
  waiting for transfers between devices  38.9 us (25%)
  blocking collectives  17 us (11%)
  Pallas kernels  6.85 us (4%)
  local copies, waits for them, and re-layouts  5.21 us (3%)
  other arithmetic  3.03 us (2%)
  matrix products  2.56 us (2%)
    ppermute x14, starting transfers between devices, move(): return lax.ppermute(array, AXES, pairs)  54.5 us
    ppermute x14, waiting for transfers between devices, move(): return lax.ppermute(array, AXES, pairs)  33.2 us
    all_to_all x4, starting transfers between devices, exchange(): lax.all_to_all(array, axis, split_axis=0, concat_axis=0, tiled=True, axis...  26.2 us
    all_to_all x1, blocking collectives, exchange(): lax.all_to_all(array, axis, split_axis=0, concat_axis=0, tiled=True, axis...  14.6 us
    pallas_call x2, Pallas kernels, compute(): pl.pallas_call(kernel, out_shape=jax.ShapeDtypeStruct(shape, jnp.bfloat16...  6.85 us
    all_to_all x4, waiting for transfers between devices, exchange(): lax.all_to_all(array, axis, split_axis=0, concat_axis=0, tiled=True, axis...  5.64 us
  transfers between devices with their start and end apart: 18, of which 11 were waited for; matrix products, arithmetic and copies ran while one was open for 4% of the time, Pallas kernels for 2%

profile of v4, /device:TPU:1, one launch (start us, length us, event | category | flops | bytes accessed | tf_op | source)
XLA Modules:
  0.0 155.4 jit_solution(10356162166295493238)
XLA Ops:
  1.0 1.1 fusion.2
  2.9 10.9 %all-to-all-start = ((bf16[8,32,1152]{2,1,0:T(8,128)(2,1)}), bf16[8,32,1152]{2,1,0:T(8,128)(2,1)S(1)}, u32[]{:S(2)}, u32[]{:S(2)}) async-start(bf16[8,32,1152]{2,1,0:T(8,128)(2,1)} %broadcast_in_dim.24), calls=%async_computation | async-start | bytes 1179648 | tf_op jit(solution)/shard_map/all_to_all | solution.py:81
  13.8 5.7 %collective-permute-start = (bf16[256,128]{1,0:T(8,128)(2,1)S(1)}, bf16[256,128]{1,0:T(8,128)(2,1)S(1)}, u32[]{:S(2)}, u32[]{:S(2)}) collective-permute-start(bf16[256,128]{1,0:T(8,128)(2,1)S(1)} %fusion.2), channel_id=1, source_target_pairs={{0,0},{1,112},{2,128},{3,240},{4,256},{5,368},{6,384},{7,496},{8,8... | collective-permute-start | bytes 196616 | tf_op jit(solution)/shard_map/ppermute | solution.py:77
  19.5 16.4 %collective-permute-done = bf16[256,128]{1,0:T(8,128)(2,1)S(1)} collective-permute-done((bf16[256,128]{1,0:T(8,128)(2,1)S(1)}, bf16[256,128]{1,0:T(8,128)(2,1)S(1)}, u32[]{:S(2)}, u32[]{:S(2)}) %collective-permute-start) | collective-permute-done | bytes 65568 | tf_op jit(solution)/shard_map/ppermute | solution.py:77
  35.9 1.3 broadcast_in_dim.23
  37.2 5.5 %all-to-all-start.1 = ((bf16[16,320,128]{2,1,0:T(8,128)(2,1)}), bf16[16,320,128]{2,1,0:T(8,128)(2,1)S(1)}, u32[]{:S(2)}, u32[]{:S(2)}) async-start(bf16[16,320,128]{2,1,0:T(8,128)(2,1)} %broadcast_in_dim.23), calls=%async_computation.1 | async-start | bytes 2621440 | tf_op jit(solution)/shard_map/all_to_all | solution.py:81
  43.0 2.4 %all-gather.1 = f32[2,1,128]{2,1,0:T(1,128)S(1)} all-gather(f32[1,1,128]{2,1,0:T(1,128)S(1)} %bitcast.79), channel_id=2, replica_groups={{0,1},{2,3},{4,5},{6,7},{8,9},{10,11},{12,13},{14,15},{16,17},{18,19},{..., dimensions={0}, use_global_device_ids=true | all-gather | bytes 1536 | tf_op jit(solution)/shard_map/all_gather | solution.py:193
  45.4 1.9 %collective-permute-start.2 = (bf16[128,2048]{1,0:T(8,128)(2,1)S(1)}, bf16[128,2048]{1,0:T(8,128)(2,1)S(1)}, u32[]{:S(2)}, u32[]{:S(2)}) collective-permute-start(bf16[128,2048]{1,0:T(8,128)(2,1)S(1)} %get-tuple-element.28.refs_0_), channel_id=1, source_target_pairs={{0,128},{1,129},{2,130},{3,131},{4,132},{5,133},{6,134},{7,135},{8... | collective-permute-start | bytes 1572872 | tf_op jit(solution)/shard_map/ppermute | solution.py:77
  47.3 4.6 %collective-permute-start.1 = (bf16[128,2048]{1,0:T(8,128)(2,1)S(1)}, bf16[128,2048]{1,0:T(8,128)(2,1)S(1)}, u32[]{:S(2)}, u32[]{:S(2)}) collective-permute-start(bf16[128,2048]{1,0:T(8,128)(2,1)S(1)} %get-tuple-element.28.refs_0_), channel_id=1, source_target_pairs={{0,384},{1,385},{2,386},{3,387},{4,388},{5,389},{6,390},{7,391},{8... | collective-permute-start | bytes 1572872 | tf_op jit(solution)/shard_map/ppermute | solution.py:77
  51.9 3.6 %collective-permute-start.5 = (bf16[256,1152]{1,0:T(8,128)(2,1)S(1)}, bf16[256,1152]{1,0:T(8,128)(2,1)}, u32[]{:S(2)}, u32[]{:S(2)}) collective-permute-start(bf16[256,1152]{1,0:T(8,128)(2,1)S(1)} %bitcast.71), channel_id=1, source_target_pairs={{0,8},{1,9},{2,10},{3,11},{4,12},{5,13},{6,14},{7,15},{8,0},{9,1},... | collective-permute-start | bytes 1769480 | tf_op jit(solution)/shard_map/ppermute | solution.py:77
  55.5 6.2 %collective-permute-done.2.refs_4_ = bf16[128,2048]{1,0:T(8,128)(2,1)S(1)} collective-permute-done((bf16[128,2048]{1,0:T(8,128)(2,1)S(1)}, bf16[128,2048]{1,0:T(8,128)(2,1)S(1)}, u32[]{:S(2)}, u32[]{:S(2)}) %collective-permute-start.2) | collective-permute-done | bytes 524320 | tf_op jit(solution)/shard_map/ppermute | solution.py:77
  62.4 1.9 %collective-permute-start.3 = (bf16[64,2048]{1,0:T(8,128)(2,1)}, bf16[64,2048]{1,0:T(8,128)(2,1)}, u32[]{:S(2)}, u32[]{:S(2)}) collective-permute-start(bf16[64,2048]{1,0:T(8,128)(2,1)} %slice.120), channel_id=1, source_target_pairs={{0,128},{1,129},{2,130},{3,131},{4,132},{5,133},{6,134},{7,135},{8... | collective-permute-start | bytes 786440 | tf_op jit(solution)/shard_map/ppermute | solution.py:77
  65.1 4.6 %collective-permute-start.4 = (bf16[64,2048]{1,0:T(8,128)(2,1)}, bf16[64,2048]{1,0:T(8,128)(2,1)}, u32[]{:S(2)}, u32[]{:S(2)}) collective-permute-start(bf16[64,2048]{1,0:T(8,128)(2,1)} %slice.121), channel_id=1, source_target_pairs={{0,384},{1,385},{2,386},{3,387},{4,388},{5,389},{6,390},{7,391},{8... | collective-permute-start | bytes 786440 | tf_op jit(solution)/shard_map/ppermute | solution.py:77
  69.7 1.9 %collective-permute-start.8 = (bf16[256,1152]{1,0:T(8,128)(2,1)S(1)}, bf16[256,1152]{1,0:T(8,128)(2,1)}, u32[]{:S(2)}, u32[]{:S(2)}) collective-permute-start(bf16[256,1152]{1,0:T(8,128)(2,1)S(1)} %bitcast.72), channel_id=1, source_target_pairs={{0,384},{1,385},{2,386},{3,387},{4,388},{5,389},{6,390},{7,391},{8... | collective-permute-start | bytes 1769480 | tf_op jit(solution)/shard_map/ppermute | solution.py:77
  71.7 3.4 %collective-permute-start.7 = (bf16[256,1152]{1,0:T(8,128)(2,1)S(1)}, bf16[256,1152]{1,0:T(8,128)(2,1)}, u32[]{:S(2)}, u32[]{:S(2)}) collective-permute-start(bf16[256,1152]{1,0:T(8,128)(2,1)S(1)} %bitcast.73), channel_id=1, source_target_pairs={{0,128},{1,129},{2,130},{3,131},{4,132},{5,133},{6,134},{7,135},{8... | collective-permute-start | bytes 1769480 | tf_op jit(solution)/shard_map/ppermute | solution.py:77
  75.1 3.0 %shard_map.127 = bf16[4,128,512]{2,1,0:T(8,128)(2,1)} custom-call(s32[3]{0:T(128)S(1)} %pad_add_fusion.place_ref, bf16[16,320,128]{2,1,0:T(8,128)(2,1)S(1)} %all-to-all-done.1.weight_ref, bf16[128,2048]{1,0:T(8,128)(2,1)S(1)} %get-tuple-element.28.refs_0_, bf16[128,2048]{1,0:T(8,128)(2,1)S(1)} %collective-permute-done.1.refs_1_, ...), custom_call_target="tpu_custom_call" | custom-call | tf_op jit(solution)/shard_map/pallas_call | solution.py:144
  78.1 3.7 %all-to-all-start.2 = ((bf16[4,128,512]{2,1,0:T(8,128)(2,1)}), bf16[4,128,512]{2,1,0:T(8,128)(2,1)S(1)}, u32[]{:S(2)}, u32[]{:S(2)}) async-start(bf16[4,128,512]{2,1,0:T(8,128)(2,1)} %shard_map.127), calls=%async_computation.2 | async-start | bytes 1048576 | tf_op jit(solution)/shard_map/all_to_all | solution.py:81
  81.9 4.6 %collective-permute-start.10 = (bf16[256,1152]{1,0:T(8,128)(2,1)}, bf16[256,1152]{1,0:T(8,128)(2,1)S(1)}, u32[]{:S(2)}, u32[]{:S(2)}) collective-permute-start(bf16[256,1152]{1,0:T(8,128)(2,1)} %collective-permute-done.5.refs_1_), channel_id=1, source_target_pairs={{0,384},{1,385},{2,386},{3,387},{4,388},{5,389},{6,390},{7,391},{8... | collective-permute-start | bytes 1769480 | tf_op jit(solution)/shard_map/ppermute | solution.py:77
  86.5 1.9 %collective-permute-start.9 = (bf16[256,1152]{1,0:T(8,128)(2,1)}, bf16[256,1152]{1,0:T(8,128)(2,1)S(1)}, u32[]{:S(2)}, u32[]{:S(2)}) collective-permute-start(bf16[256,1152]{1,0:T(8,128)(2,1)} %collective-permute-done.5.refs_1_), channel_id=1, source_target_pairs={{0,128},{1,129},{2,130},{3,131},{4,132},{5,133},{6,134},{7,135},{8... | collective-permute-start | bytes 1769480 | tf_op jit(solution)/shard_map/ppermute | solution.py:77
  88.4 3.8 %all-to-all-done.2 = bf16[4,128,512]{2,1,0:T(8,128)(2,1)S(1)} async-done(((bf16[4,128,512]{2,1,0:T(8,128)(2,1)}), bf16[4,128,512]{2,1,0:T(8,128)(2,1)S(1)}, u32[]{:S(2)}, u32[]{:S(2)}) %all-to-all-start.2) | async-done | bytes 524320 | tf_op jit(solution)/shard_map/all_to_all | solution.py:81
  92.5 7.6 %collective-permute-start.6 = (bf16[128,768]{1,0:T(8,128)(2,1)S(1)}, bf16[128,768]{1,0:T(8,128)(2,1)S(1)}, u32[]{:S(2)}, u32[]{:S(2)}) collective-permute-start(bf16[128,768]{1,0:T(8,128)(2,1)S(1)} %convert_dynamic-update-slice_fusion), channel_id=1, source_target_pairs={{0,1},{1,0},{2,3},{3,2},{4,5},{5,4},{6,7},{7,6},{8,9},{9,8},{10,11... | collective-permute-start | bytes 589832 | tf_op jit(solution)/shard_map/ppermute | solution.py:77
  102.2 2.9 %collective-permute-done.10.refs_3_ = bf16[256,1152]{1,0:T(8,128)(2,1)S(1)} collective-permute-done((bf16[256,1152]{1,0:T(8,128)(2,1)}, bf16[256,1152]{1,0:T(8,128)(2,1)S(1)}, u32[]{:S(2)}, u32[]{:S(2)}) %collective-permute-start.10) | collective-permute-done | bytes 589856 | tf_op jit(solution)/shard_map/ppermute | solution.py:77
  106.0 6.2 %all-to-all-start.3 = ((bf16[4,136,384]{2,1,0:T(8,128)(2,1)}), bf16[4,136,384]{2,1,0:T(8,128)(2,1)}, u32[]{:S(2)}, u32[]{:S(2)}) async-start(bf16[4,136,384]{2,1,0:T(8,128)(2,1)} %pad_maximum_fusion), calls=%async_computation.3 | async-start | bytes 835584 | tf_op jit(solution)/shard_map/all_to_all | solution.py:81
  112.9 1.9 %collective-permute-start.11 = (bf16[256,1152]{1,0:T(8,128)(2,1)}, bf16[256,1152]{1,0:T(8,128)(2,1)S(1)}, u32[]{:S(2)}, u32[]{:S(2)}) collective-permute-start(bf16[256,1152]{1,0:T(8,128)(2,1)} %collective-permute-done.7.refs_6_), channel_id=1, source_target_pairs={{0,128},{1,129},{2,130},{3,131},{4,132},{5,133},{6,134},{7,135},{8... | collective-permute-start | bytes 1769480 | tf_op jit(solution)/shard_map/ppermute | solution.py:77
  114.8 4.6 %collective-permute-start.12 = (bf16[256,1152]{1,0:T(8,128)(2,1)S(1)}, bf16[256,1152]{1,0:T(8,128)(2,1)S(1)}, u32[]{:S(2)}, u32[]{:S(2)}) collective-permute-start(bf16[256,1152]{1,0:T(8,128)(2,1)S(1)} %collective-permute-done.10.refs_3_), channel_id=1, source_target_pairs={{0,384},{1,385},{2,386},{3,387},{4,388},{5,389},{6,390},{7,391},{8... | collective-permute-start | bytes 1769480 | tf_op jit(solution)/shard_map/ppermute | solution.py:77
  119.4 1.8 %all-to-all-done.3 = bf16[4,136,384]{2,1,0:T(8,128)(2,1)} async-done(((bf16[4,136,384]{2,1,0:T(8,128)(2,1)}), bf16[4,136,384]{2,1,0:T(8,128)(2,1)}, u32[]{:S(2)}, u32[]{:S(2)}) %all-to-all-start.3) | async-done | bytes 417824 | tf_op jit(solution)/shard_map/all_to_all | solution.py:81
  121.2 1.1 convert_reduce_fusion
  123.6 1.2 convolution_convert_fusion
  124.8 4.0 %collective-permute-done.11.refs_4_ = bf16[256,1152]{1,0:T(8,128)(2,1)S(1)} collective-permute-done((bf16[256,1152]{1,0:T(8,128)(2,1)}, bf16[256,1152]{1,0:T(8,128)(2,1)S(1)}, u32[]{:S(2)}, u32[]{:S(2)}) %collective-permute-start.11) | collective-permute-done | bytes 589856 | tf_op jit(solution)/shard_map/ppermute | solution.py:77
  129.5 14.6 %all_to_all.25.own_ref = bf16[4,192,128]{2,1,0:T(8,128)(2,1)S(1)} all-to-all(bf16[4,192,128]{2,1,0:T(8,128)(2,1)S(1)} %broadcast_in_dim.30), channel_id=1, replica_groups={{0,2,4,6},{1,3,5,7},{8,10,12,14},{9,11,13,15},{16,18,20,22},{17,19,21,2..., dimensions={0} | all-to-all | bytes 393216 | tf_op jit(solution)/shard_map/all_to_all | solution.py:81
  144.1 6.4 %collective-permute-start.13 = (bf16[4,192,128]{2,1,0:T(8,128)(2,1)S(1)}, bf16[4,192,128]{2,1,0:T(8,128)(2,1)S(1)}, u32[]{:S(2)}, u32[]{:S(2)}) collective-permute-start(bf16[4,192,128]{2,1,0:T(8,128)(2,1)S(1)} %all_to_all.25.own_ref), channel_id=1, source_target_pairs={{0,1},{1,0},{2,3},{3,2},{4,5},{5,4},{6,7},{7,6},{8,9},{9,8},{10,11... | collective-permute-start | bytes 589832 | tf_op jit(solution)/shard_map/ppermute | solution.py:77
  151.6 3.9 %shard_map.128 = bf16[128,2048]{1,0:T(8,128)(2,1)} custom-call(s32[3]{0:T(128)S(1)} %pad_add_fusion.place_ref, bf16[4,192,128]{2,1,0:T(8,128)(2,1)S(1)} %all_to_all.25.own_ref, bf16[4,192,128]{2,1,0:T(8,128)(2,1)S(1)} %collective-permute-done.13.other_ref, bf16[256,1152]{1,0:T(8,128)(2,1)S(1)} %bitcast.74, bf16[256,1152]{1,0:T(8,128)(2,1)} %collective-permute-done.5.refs_1_, ...), custom_call_target="tpu_custom_call" | custom-call | tf_op jit(solution)/shard_map/pallas_call | solution.py:144
  (79 shorter events, 9.9 us)
Async XLA Ops:
  0.0 1.0 copy-start
  0.0 19.5 %copy-start.2 = (bf16[1,32,256]{2,1,0:T(8,128)(2,1)S(1)}, bf16[1,32,256]{2,1,0:T(8,128)(2,1)}, u32[]{:S(2)}) copy-start(bf16[1,32,256]{2,1,0:T(8,128)(2,1)} %param.18) | copy-start | bytes 49156
  2.9 33.0 %all-to-all-start = ((bf16[8,32,1152]{2,1,0:T(8,128)(2,1)}), bf16[8,32,1152]{2,1,0:T(8,128)(2,1)S(1)}, u32[]{:S(2)}, u32[]{:S(2)}) async-start(bf16[8,32,1152]{2,1,0:T(8,128)(2,1)} %broadcast_in_dim.24), calls=%async_computation | async-start | bytes 1179648 | tf_op jit(solution)/shard_map/all_to_all | solution.py:81
  13.8 22.1 %collective-permute-start = (bf16[256,128]{1,0:T(8,128)(2,1)S(1)}, bf16[256,128]{1,0:T(8,128)(2,1)S(1)}, u32[]{:S(2)}, u32[]{:S(2)}) collective-permute-start(bf16[256,128]{1,0:T(8,128)(2,1)S(1)} %fusion.2), channel_id=1, source_target_pairs={{0,0},{1,112},{2,128},{3,240},{4,256},{5,368},{6,384},{7,496},{8,8... | collective-permute-start | bytes 196616 | tf_op jit(solution)/shard_map/ppermute | solution.py:77
  37.2 5.5 %copy-start.4 = (bf16[2048]{0:T(1024)(128)(2,1)S(1)}, bf16[2048]{0:T(1024)(128)(2,1)}, u32[]{:S(2)}) copy-start(bf16[2048]{0:T(1024)(128)(2,1)} %param.14) | copy-start | bytes 12292
  37.2 5.5 %copy-start.1 = (bf16[128,2048]{1,0:T(8,128)(2,1)S(1)}, bf16[128,2048]{1,0:T(8,128)(2,1)}, u32[]{:S(2)}) copy-start(bf16[128,2048]{1,0:T(8,128)(2,1)} %param.13) | copy-start | bytes 1572868
  37.2 37.9 %all-to-all-start.1 = ((bf16[16,320,128]{2,1,0:T(8,128)(2,1)}), bf16[16,320,128]{2,1,0:T(8,128)(2,1)S(1)}, u32[]{:S(2)}, u32[]{:S(2)}) async-start(bf16[16,320,128]{2,1,0:T(8,128)(2,1)} %broadcast_in_dim.23), calls=%async_computation.1 | async-start | bytes 2621440 | tf_op jit(solution)/shard_map/all_to_all | solution.py:81
  45.4 16.3 %collective-permute-start.2 = (bf16[128,2048]{1,0:T(8,128)(2,1)S(1)}, bf16[128,2048]{1,0:T(8,128)(2,1)S(1)}, u32[]{:S(2)}, u32[]{:S(2)}) collective-permute-start(bf16[128,2048]{1,0:T(8,128)(2,1)S(1)} %get-tuple-element.28.refs_0_), channel_id=1, source_target_pairs={{0,128},{1,129},{2,130},{3,131},{4,132},{5,133},{6,134},{7,135},{8... | collective-permute-start | bytes 1572872 | tf_op jit(solution)/shard_map/ppermute | solution.py:77
  47.3 17.0 %collective-permute-start.1 = (bf16[128,2048]{1,0:T(8,128)(2,1)S(1)}, bf16[128,2048]{1,0:T(8,128)(2,1)S(1)}, u32[]{:S(2)}, u32[]{:S(2)}) collective-permute-start(bf16[128,2048]{1,0:T(8,128)(2,1)S(1)} %get-tuple-element.28.refs_0_), channel_id=1, source_target_pairs={{0,384},{1,385},{2,386},{3,387},{4,388},{5,389},{6,390},{7,391},{8... | collective-permute-start | bytes 1572872 | tf_op jit(solution)/shard_map/ppermute | solution.py:77
  51.9 26.2 %collective-permute-start.5 = (bf16[256,1152]{1,0:T(8,128)(2,1)S(1)}, bf16[256,1152]{1,0:T(8,128)(2,1)}, u32[]{:S(2)}, u32[]{:S(2)}) collective-permute-start(bf16[256,1152]{1,0:T(8,128)(2,1)S(1)} %bitcast.71), channel_id=1, source_target_pairs={{0,8},{1,9},{2,10},{3,11},{4,12},{5,13},{6,14},{7,15},{8,0},{9,1},... | collective-permute-start | bytes 1769480 | tf_op jit(solution)/shard_map/ppermute | solution.py:77
  62.4 12.6 %collective-permute-start.3 = (bf16[64,2048]{1,0:T(8,128)(2,1)}, bf16[64,2048]{1,0:T(8,128)(2,1)}, u32[]{:S(2)}, u32[]{:S(2)}) collective-permute-start(bf16[64,2048]{1,0:T(8,128)(2,1)} %slice.120), channel_id=1, source_target_pairs={{0,128},{1,129},{2,130},{3,131},{4,132},{5,133},{6,134},{7,135},{8... | collective-permute-start | bytes 786440 | tf_op jit(solution)/shard_map/ppermute | solution.py:77
  65.1 10.0 %collective-permute-start.4 = (bf16[64,2048]{1,0:T(8,128)(2,1)}, bf16[64,2048]{1,0:T(8,128)(2,1)}, u32[]{:S(2)}, u32[]{:S(2)}) collective-permute-start(bf16[64,2048]{1,0:T(8,128)(2,1)} %slice.121), channel_id=1, source_target_pairs={{0,384},{1,385},{2,386},{3,387},{4,388},{5,389},{6,390},{7,391},{8... | collective-permute-start | bytes 786440 | tf_op jit(solution)/shard_map/ppermute | solution.py:77
  69.7 32.4 %collective-permute-start.8 = (bf16[256,1152]{1,0:T(8,128)(2,1)S(1)}, bf16[256,1152]{1,0:T(8,128)(2,1)}, u32[]{:S(2)}, u32[]{:S(2)}) collective-permute-start(bf16[256,1152]{1,0:T(8,128)(2,1)S(1)} %bitcast.72), channel_id=1, source_target_pairs={{0,384},{1,385},{2,386},{3,387},{4,388},{5,389},{6,390},{7,391},{8... | collective-permute-start | bytes 1769480 | tf_op jit(solution)/shard_map/ppermute | solution.py:77
  71.7 30.5 %collective-permute-start.7 = (bf16[256,1152]{1,0:T(8,128)(2,1)S(1)}, bf16[256,1152]{1,0:T(8,128)(2,1)}, u32[]{:S(2)}, u32[]{:S(2)}) collective-permute-start(bf16[256,1152]{1,0:T(8,128)(2,1)S(1)} %bitcast.73), channel_id=1, source_target_pairs={{0,128},{1,129},{2,130},{3,131},{4,132},{5,133},{6,134},{7,135},{8... | collective-permute-start | bytes 1769480 | tf_op jit(solution)/shard_map/ppermute | solution.py:77
  78.1 14.1 %all-to-all-start.2 = ((bf16[4,128,512]{2,1,0:T(8,128)(2,1)}), bf16[4,128,512]{2,1,0:T(8,128)(2,1)S(1)}, u32[]{:S(2)}, u32[]{:S(2)}) async-start(bf16[4,128,512]{2,1,0:T(8,128)(2,1)} %shard_map.127), calls=%async_computation.2 | async-start | bytes 1048576 | tf_op jit(solution)/shard_map/all_to_all | solution.py:81
  81.9 23.1 %collective-permute-start.10 = (bf16[256,1152]{1,0:T(8,128)(2,1)}, bf16[256,1152]{1,0:T(8,128)(2,1)S(1)}, u32[]{:S(2)}, u32[]{:S(2)}) collective-permute-start(bf16[256,1152]{1,0:T(8,128)(2,1)} %collective-permute-done.5.refs_1_), channel_id=1, source_target_pairs={{0,384},{1,385},{2,386},{3,387},{4,388},{5,389},{6,390},{7,391},{8... | collective-permute-start | bytes 1769480 | tf_op jit(solution)/shard_map/ppermute | solution.py:77
  86.5 19.5 %collective-permute-start.9 = (bf16[256,1152]{1,0:T(8,128)(2,1)}, bf16[256,1152]{1,0:T(8,128)(2,1)S(1)}, u32[]{:S(2)}, u32[]{:S(2)}) collective-permute-start(bf16[256,1152]{1,0:T(8,128)(2,1)} %collective-permute-done.5.refs_1_), channel_id=1, source_target_pairs={{0,128},{1,129},{2,130},{3,131},{4,132},{5,133},{6,134},{7,135},{8... | collective-permute-start | bytes 1769480 | tf_op jit(solution)/shard_map/ppermute | solution.py:77
  92.5 8.6 %collective-permute-start.6 = (bf16[128,768]{1,0:T(8,128)(2,1)S(1)}, bf16[128,768]{1,0:T(8,128)(2,1)S(1)}, u32[]{:S(2)}, u32[]{:S(2)}) collective-permute-start(bf16[128,768]{1,0:T(8,128)(2,1)S(1)} %convert_dynamic-update-slice_fusion), channel_id=1, source_target_pairs={{0,1},{1,0},{2,3},{3,2},{4,5},{5,4},{6,7},{7,6},{8,9},{9,8},{10,11... | collective-permute-start | bytes 589832 | tf_op jit(solution)/shard_map/ppermute | solution.py:77
  101.2 11.7 %copy-start.6 = (s32[1,128]{1,0:T(1,128)S(1)}, s32[1,128]{1,0:T(1,128)}, u32[]{:S(2)}) copy-start(s32[1,128]{1,0:T(1,128)} %param.24) | copy-start | bytes 1540
  106.0 15.3 %all-to-all-start.3 = ((bf16[4,136,384]{2,1,0:T(8,128)(2,1)}), bf16[4,136,384]{2,1,0:T(8,128)(2,1)}, u32[]{:S(2)}, u32[]{:S(2)}) async-start(bf16[4,136,384]{2,1,0:T(8,128)(2,1)} %pad_maximum_fusion), calls=%async_computation.3 | async-start | bytes 835584 | tf_op jit(solution)/shard_map/all_to_all | solution.py:81
  112.1 10.9 %copy-start.5 = (bf16[1,512,128]{2,1,0:T(8,128)(2,1)S(1)}, bf16[1,512,128]{2,1,0:T(8,128)(2,1)}, u32[]{:S(2)}) copy-start(bf16[1,512,128]{2,1,0:T(8,128)(2,1)} %param.22) | copy-start | bytes 393220
  112.9 15.8 %collective-permute-start.11 = (bf16[256,1152]{1,0:T(8,128)(2,1)}, bf16[256,1152]{1,0:T(8,128)(2,1)S(1)}, u32[]{:S(2)}, u32[]{:S(2)}) collective-permute-start(bf16[256,1152]{1,0:T(8,128)(2,1)} %collective-permute-done.7.refs_6_), channel_id=1, source_target_pairs={{0,128},{1,129},{2,130},{3,131},{4,132},{5,133},{6,134},{7,135},{8... | collective-permute-start | bytes 1769480 | tf_op jit(solution)/shard_map/ppermute | solution.py:77
  114.8 14.6 %collective-permute-start.12 = (bf16[256,1152]{1,0:T(8,128)(2,1)S(1)}, bf16[256,1152]{1,0:T(8,128)(2,1)S(1)}, u32[]{:S(2)}, u32[]{:S(2)}) collective-permute-start(bf16[256,1152]{1,0:T(8,128)(2,1)S(1)} %collective-permute-done.10.refs_3_), channel_id=1, source_target_pairs={{0,384},{1,385},{2,386},{3,387},{4,388},{5,389},{6,390},{7,391},{8... | collective-permute-start | bytes 1769480 | tf_op jit(solution)/shard_map/ppermute | solution.py:77
  123.0 6.4 %copy-start.3 = (bf16[128,64]{0,1:T(8,128)(2,1)S(1)}, bf16[128,64]{0,1:T(8,128)(2,1)}, u32[]{:S(2)}) copy-start(bf16[128,64]{0,1:T(8,128)(2,1)} %param.20) | copy-start | bytes 49156
  144.1 7.5 %collective-permute-start.13 = (bf16[4,192,128]{2,1,0:T(8,128)(2,1)S(1)}, bf16[4,192,128]{2,1,0:T(8,128)(2,1)S(1)}, u32[]{:S(2)}, u32[]{:S(2)}) collective-permute-start(bf16[4,192,128]{2,1,0:T(8,128)(2,1)S(1)} %all_to_all.25.own_ref), channel_id=1, source_target_pairs={{0,1},{1,0},{2,3},{3,2},{4,5},{5,4},{6,7},{7,6},{8,9},{9,8},{10,11... | collective-permute-start | bytes 589832 | tf_op jit(solution)/shard_map/ppermute | solution.py:77

commit v5 on v4

--- a/solution.py
+++ b/solution.py
@@ -8,35 +8,50 @@
 AXES = ("engine", "fsdp", "tensor")
 
 
-def rotate(values, places):
-    half = values.shape[-1] // 2
-    index = jnp.arange(half).astype(jnp.float32)
-    inverse = jnp.exp(index * (-2.0 / values.shape[-1]) * jnp.log(jnp.float32(500000.0)))
+def turns(places):
+    index = jnp.arange(64).astype(jnp.float32)
+    inverse = jnp.exp(index * (-2.0 / 128) * jnp.log(jnp.float32(500000.0)))
     angle = places.astype(jnp.float32)[:, None] * inverse[None, :]
-    cosine = jnp.cos(angle)
-    sine = jnp.sin(angle)
-    first = values[:, :half]
-    second = values[:, half:]
-    return jnp.concatenate([first * cosine - second * sine, second * cosine + first * sine], axis=1)
-
-
-def attend(query, new_keys, new_values, old_keys, old_values, offset):
-    tok_count = query.shape[0]
-    slots = old_keys.shape[0]
-    keys_all = jnp.concatenate([old_keys, new_keys], axis=0)
-    values_all = jnp.concatenate([old_values, new_values], axis=0)
-    scores = jnp.dot(query, keys_all.T, preferred_element_type=jnp.float32) * query.shape[-1] ** (
-        -0.5
-    )
-    slot_seen = jnp.broadcast_to(jnp.arange(slots)[None, :] < offset, (tok_count, slots))
-    rows = jnp.arange(tok_count)
-    new_seen = rows[None, :] <= rows[:, None]
-    seen = jnp.concatenate([slot_seen, new_seen], axis=1)
-    scores = jnp.where(seen, scores, jnp.float32(-1e30))
-    top = jnp.max(scores, axis=1, keepdims=True)
-    probs = jnp.exp(scores - top)
-    weights = (probs / jnp.sum(probs, axis=1, keepdims=True)).astype(jnp.bfloat16)
-    return jnp.dot(weights, values_all, preferred_element_type=jnp.float32).astype(jnp.bfloat16)
+    cosine, sine = jnp.cos(angle), jnp.sin(angle)
+    return jnp.concatenate([cosine, cosine], axis=1), jnp.concatenate([-sine, sine], axis=1)
+
+
+def attend_kernel(
+    offset_ref, terms_ref, cosine_ref, sine_ref, keys_ref, values_ref, down_ref, out_ref
+):
+    sums = terms_ref[0].astype(jnp.float32)
+    for i in range(1, 4):
+        sums = sums + terms_ref[i].astype(jnp.float32)
+    mean = (sums[128:129, :128] + sums[128:129, 128:256]) / 16384.0
+    scale = jnp.broadcast_to(lax.rsqrt(mean + 1e-05), (128, 128)).T
+    query, new_keys, new_values = (sums[:128, i : i + 128] * scale for i in (0, 128, 256))
+    cosine, sine = cosine_ref[...], sine_ref[...]
+    query, new_keys = (
+        (values * cosine + pltpu.roll(values, 64, 1) * sine).astype(jnp.bfloat16)
+        for values in (query, new_keys)
+    )
+    inner = (((1,), (1,)), ((), ()))
+    old = lax.dot_general(query, keys_ref[...], inner, preferred_element_type=jnp.float32)
+    new = lax.dot_general(query, new_keys, inner, preferred_element_type=jnp.float32)
+    old = jnp.where(
+        lax.broadcasted_iota(jnp.int32, old.shape, 1) < offset_ref[0], old * 128**-0.5, -1e30
+    )
+    token = lax.broadcasted_iota(jnp.int32, new.shape, 0)
+    new = jnp.where(
+        lax.broadcasted_iota(jnp.int32, new.shape, 1) <= token, new * 128**-0.5, -1e30
+    )
+    top = jnp.maximum(jnp.max(old, axis=1, keepdims=True), jnp.max(new, axis=1, keepdims=True))
+    old, new = jnp.exp(old - top), jnp.exp(new - top)
+    whole = jnp.sum(old, axis=1, keepdims=True) + jnp.sum(new, axis=1, keepdims=True)
+    out = jnp.dot(
+        (old / whole).astype(jnp.bfloat16), values_ref[...], preferred_element_type=jnp.float32
+    ) + jnp.dot(
+        (new / whole).astype(jnp.bfloat16),
+        new_values.astype(jnp.bfloat16),
+        preferred_element_type=jnp.float32,
+    )
+    out_ref[:128] = out.astype(jnp.bfloat16)
+    out_ref[128:] = down_ref[...]
 
 
 ACROSS = [[0, 2, 4, 6], [1, 3, 5, 7]]
@@ -115,14 +130,10 @@
         out_ref[lax.rem(engine + step, 4), start : start + rows] = terms.astype(jnp.bfloat16)
 
 
-def project_kernel(place_ref, own_ref, other_ref, *refs):
+def project_kernel(place_ref, heads_ref, *refs):
     weight_refs, out_ref, weight_ref = refs[:8], refs[8], refs[9]
-    engine, core, y = place_ref[0], place_ref[1], place_ref[2]
-    rows = []
-    for i in range(4):
-        own, other = own_ref[i], other_ref[i]
-        rows += [jnp.where(core == 0, own, other), jnp.where(core == 0, other, own)]
-    rows = jnp.concatenate(rows, axis=1)
+    engine, y = place_ref[0], place_ref[2]
+    rows = jnp.concatenate([heads_ref[i] for i in range(8)], axis=1)
     heads, down = rows[:128], rows[128:]
     inner = (((1,), (1,)), ((), ()))
     mixed = lax.dot_general(heads, down, inner, preferred_element_type=jnp.float32)
@@ -185,24 +196,29 @@
 
     shard = jnp.concatenate([query_shard, kv_base[0, :, :128], kv_base[0, :, 128:]], axis=0)
     shards = jnp.broadcast_to(shard[None], (16, 320, 128))
-    shards, mine, layer_input = lax.optimization_barrier((shards, mine, layer_input))
+    wide = layer_input.astype(jnp.float32)
+    scaled = (wide * norm_gain.astype(jnp.float32)[None, :]).astype(jnp.bfloat16)
+    before, after = move(scaled, next_engine), move(scaled, last_engine)
+    shards, mine, before, after, layer_input = lax.optimization_barrier(
+        (shards, mine, before, after, layer_input)
+    )
     gathered = exchange(shards, "fsdp")
 
     wide = layer_input.astype(jnp.float32)
     squares = jnp.sum(wide * wide, axis=1)[None]
     squares = lax.all_gather(squares, "tensor", axis=0, tiled=True, axis_index_groups=CORES)
     squares = jnp.sum(squares, axis=0, keepdims=True)
-    scaled = (wide * norm_gain.astype(jnp.float32)[None, :]).astype(jnp.bfloat16)
-    scaled, squares, mine = lax.optimization_barrier((scaled, squares, mine))
-    before, after = move(scaled, next_engine), move(scaled, last_engine)
-    theirs = move(mine, other_y)
+    cosine, sine = turns(positions[0])
+    squares, mine, before, after = lax.optimization_barrier((squares, mine, before, after))
     across_low, across_high = move(before[:64], next_engine), move(after[64:], last_engine)
     tokens = (scaled, after, across_low, across_high, before)
+    theirs = move(mine, other_y)
+    mine_before, mine_after = move(mine, next_engine), move(mine, last_engine)
+    gathered, mine_before, mine_after = lax.optimization_barrier((gathered, mine_before, mine_after))
+    mine_across = move(mine_before, next_engine)
 
     terms = compute(terms_kernel, (4, 128, 512), place, (gathered, *tokens))
-    terms, theirs = lax.optimization_barrier((terms, theirs))
-    mine_before, theirs_after = move(mine, next_engine), move(theirs, last_engine)
-    mine_after, theirs_before = move(mine, last_engine), move(theirs, next_engine)
+    theirs_before, theirs_after = move(theirs, next_engine), move(theirs, last_engine)
     terms = exchange(terms, "engine").astype(jnp.float32)
     kv_terms = jnp.sum(terms[:, :, 256:], axis=0)
     own = jnp.concatenate([terms[i, :, :128] for i in range(4)] + [kv_terms], axis=1)
@@ -222,32 +238,23 @@
             for i in range(4)
         ]
     )
-    terms, mine_before, mine_after, theirs_before, theirs_after = lax.optimization_barrier(
-        (terms, mine_before, mine_after, theirs_before, theirs_after)
-    )
-    mine_across, theirs_across = move(mine_before, next_engine), move(theirs_after, last_engine)
+    terms, mine_across, theirs_after, cosine, sine = lax.optimization_barrier(
+        (terms, mine_across, theirs_after, cosine, sine)
+    )
+    theirs_across = move(theirs_after, last_engine)
     terms = exchange(terms, "tensor", ACROSS)
-    total = jnp.sum(terms.astype(jnp.float32), axis=0)
-    mean = (total[128, :128] + total[128, 128:256]) / 16384.0
-    total = total[:128] * lax.rsqrt(mean + 1e-05)[:, None]
-
-    places = positions[0]
-    query = rotate(total[:, :128], places).astype(jnp.bfloat16)
-    new_keys = rotate(total[:, 128:256], places).astype(jnp.bfloat16)
-    new_values = total[:, 256:].astype(jnp.bfloat16)
-    head_out = attend(query, new_keys, new_values, cache_keys[0], cache_values[0], offsets[0])
-
-    head_out, mine_across, theirs_across = lax.optimization_barrier(
-        (head_out, mine_across, theirs_across)
-    )
-    heads = jnp.concatenate([head_out, output_down_factor.T], axis=0)
-    own = spread(heads, 4, "tensor", ACROSS)
-    other = move(own, other_core)
+    heads = compute(
+        attend_kernel,
+        (192, 128),
+        offsets,
+        (terms, cosine, sine, cache_keys[0], cache_values[0], output_down_factor.T),
+    )
+    heads = lax.all_gather(heads[None], "tensor", axis=0, tiled=True)
     out_weights = (
         mine, theirs, mine_after, theirs_after, mine_across, theirs_across, mine_before, theirs_before
     )
     return compute(
-        project_kernel, (128, 2048), place, (own, other, *out_weights), ((4, 512, 1152),)
+        project_kernel, (128, 2048), place, (heads, *out_weights), ((4, 512, 1152),)
     )
 
 

time: 157 us -> 147 us (0.936)
  waiting for transfers between devices: 38.9 us -> 20.8 us
  blocking collectives: 17 us -> 22.5 us
  other arithmetic: 3.03 us -> 5.25 us
    ppermute x14 -> x13, waiting for transfers between devices: 33.2 us -> 9.53 us  [move(): return lax.ppermute(array, AXES, pairs)]
    all_gather x0 -> x1, blocking collectives: none -> 20.3 us  [per_device(): heads = lax.all_gather(heads[None], 'tensor', axis=0, tiled=True)]
    all_to_all x1 -> x0, blocking collectives: 14.6 us -> none  [exchange(): lax.all_to_all(array, axis, split_axis=0, concat_axis=0, tiled=True, axis...]
    all_to_all x4, waiting for transfers between devices: 5.64 us -> 11.3 us  [exchange(): lax.all_to_all(array, axis, split_axis=0, concat_axis=0, tiled=True, axis...]
    all_to_all x4, starting transfers between devices: 26.2 us -> 31.3 us  [exchange(): lax.all_to_all(array, axis, split_axis=0, concat_axis=0, tiled=True, axis...]
    ppermute x14 -> x13, starting transfers between devices: 54.5 us -> 50.7 us  [move(): return lax.ppermute(array, AXES, pairs)]
    concatenate x2 -> x1, other arithmetic: 0.01 us -> 1.68 us  [turns(): jnp.concatenate([cosine, cosine], axis=1)]
    pallas_call x2 -> x3, Pallas kernels: 6.85 us -> 7.77 us  [compute(): pl.pallas_call(kernel, out_shape=jax.ShapeDtypeStruct(shape, jnp.bfloat16...]
  transfers between devices with their start and end apart: 18 -> 17, of which waited for: 11 -> 11; matrix products, arithmetic and copies ran while one was open for 4% -> 5% of each run, Pallas kernels for 2% -> 3%
where the time goes in v5:
time: 147 us; the launch traced here: 146 us
  starting transfers between devices  82 us (56%)
  blocking collectives  22.5 us (15%)
  waiting for transfers between devices  20.8 us (14%)
  Pallas kernels  7.77 us (5%)
  local copies, waits for them, and re-layouts  5.55 us (4%)
  other arithmetic  5.25 us (4%)
    ppermute x13, starting transfers between devices, move(): return lax.ppermute(array, AXES, pairs)  50.7 us
    all_to_all x4, starting transfers between devices, exchange(): lax.all_to_all(array, axis, split_axis=0, concat_axis=0, tiled=True, axis...  31.3 us
    all_gather x1, blocking collectives, per_device(): heads = lax.all_gather(heads[None], 'tensor', axis=0, tiled=True)  20.3 us
    all_to_all x4, waiting for transfers between devices, exchange(): lax.all_to_all(array, axis, split_axis=0, concat_axis=0, tiled=True, axis...  11.3 us
    ppermute x13, waiting for transfers between devices, move(): return lax.ppermute(array, AXES, pairs)  9.53 us
    pallas_call x3, Pallas kernels, compute(): pl.pallas_call(kernel, out_shape=jax.ShapeDtypeStruct(shape, jnp.bfloat16...  7.77 us
  transfers between devices with their start and end apart: 17, of which 11 were waited for; matrix products, arithmetic and copies ran while one was open for 5% of the time, Pallas kernels for 3%

profile of v5, /device:TPU:1, one launch (start us, length us, event | category | flops | bytes accessed | tf_op | source)
XLA Modules:
  0.0 145.9 jit_solution(15352767844359984441)
XLA Ops:
  0.8 1.1 fusion.1
  3.6 10.9 %all-to-all-start = ((bf16[8,32,1152]{2,1,0:T(8,128)(2,1)}), bf16[8,32,1152]{2,1,0:T(8,128)(2,1)S(1)}, u32[]{:S(2)}, u32[]{:S(2)}) async-start(bf16[8,32,1152]{2,1,0:T(8,128)(2,1)} %broadcast_in_dim.18), calls=%async_computation | async-start | bytes 1179648 | tf_op jit(solution)/shard_map/all_to_all | solution.py:96
  14.6 3.1 %collective-permute-start.1 = (bf16[128,2048]{1,0:T(8,128)(2,1)S(1)}, bf16[128,2048]{1,0:T(8,128)(2,1)S(1)}, u32[]{:S(2)}, u32[]{:S(2)}) collective-permute-start(bf16[128,2048]{1,0:T(8,128)(2,1)S(1)} %multiply_convert_fusion.refs_0_), channel_id=1, source_target_pairs={{0,128},{1,129},{2,130},{3,131},{4,132},{5,133},{6,134},{7,135},{8... | collective-permute-start | bytes 1572872 | tf_op jit(solution)/shard_map/ppermute | solution.py:92
  17.8 3.4 %collective-permute-start.2 = (bf16[128,2048]{1,0:T(8,128)(2,1)S(1)}, bf16[128,2048]{1,0:T(8,128)(2,1)S(1)}, u32[]{:S(2)}, u32[]{:S(2)}) collective-permute-start(bf16[128,2048]{1,0:T(8,128)(2,1)S(1)} %multiply_convert_fusion.refs_0_), channel_id=1, source_target_pairs={{0,384},{1,385},{2,386},{3,387},{4,388},{5,389},{6,390},{7,391},{8... | collective-permute-start | bytes 1572872 | tf_op jit(solution)/shard_map/ppermute | solution.py:92
  21.1 6.3 %collective-permute-start = (bf16[256,128]{1,0:T(8,128)(2,1)S(1)}, bf16[256,128]{1,0:T(8,128)(2,1)S(1)}, u32[]{:S(2)}, u32[]{:S(2)}) collective-permute-start(bf16[256,128]{1,0:T(8,128)(2,1)S(1)} %fusion.1), channel_id=1, source_target_pairs={{0,0},{1,112},{2,128},{3,240},{4,256},{5,368},{6,384},{7,496},{8,8... | collective-permute-start | bytes 196616 | tf_op jit(solution)/shard_map/ppermute | solution.py:92
  27.4 3.7 %collective-permute-done = bf16[256,128]{1,0:T(8,128)(2,1)S(1)} collective-permute-done((bf16[256,128]{1,0:T(8,128)(2,1)S(1)}, bf16[256,128]{1,0:T(8,128)(2,1)S(1)}, u32[]{:S(2)}, u32[]{:S(2)}) %collective-permute-start) | collective-permute-done | bytes 65568 | tf_op jit(solution)/shard_map/ppermute | solution.py:92
  31.8 2.9 %all-to-all-done = bf16[8,32,1152]{2,1,0:T(8,128)(2,1)S(1)} async-done(((bf16[8,32,1152]{2,1,0:T(8,128)(2,1)}), bf16[8,32,1152]{2,1,0:T(8,128)(2,1)S(1)}, u32[]{:S(2)}, u32[]{:S(2)}) %all-to-all-start) | async-done | bytes 589856 | tf_op jit(solution)/shard_map/all_to_all | solution.py:96
  34.7 1.3 broadcast_in_dim.17
  36.1 7.4 %all-to-all-start.1 = ((bf16[16,320,128]{2,1,0:T(8,128)(2,1)}), bf16[16,320,128]{2,1,0:T(8,128)(2,1)S(1)}, u32[]{:S(2)}, u32[]{:S(2)}) async-start(bf16[16,320,128]{2,1,0:T(8,128)(2,1)} %broadcast_in_dim.17), calls=%async_computation.1 | async-start | bytes 2621440 | tf_op jit(solution)/shard_map/all_to_all | solution.py:96
  43.5 1.2 multiply_reduce_fusion
  44.7 2.2 %all-gather.2 = f32[2,1,128]{2,1,0:T(1,128)S(1)} all-gather(f32[1,1,128]{2,1,0:T(1,128)S(1)} %bitcast.79), channel_id=2, replica_groups={{0,1},{2,3},{4,5},{6,7},{8,9},{10,11},{12,13},{14,15},{16,17},{18,19},{..., dimensions={0}, use_global_device_ids=true | all-gather | bytes 1536 | tf_op jit(solution)/shard_map/all_gather | solution.py:209
  46.9 2.5 %collective-permute-start.3 = (bf16[256,1152]{1,0:T(8,128)(2,1)S(1)}, bf16[256,1152]{1,0:T(8,128)(2,1)}, u32[]{:S(2)}, u32[]{:S(2)}) collective-permute-start(bf16[256,1152]{1,0:T(8,128)(2,1)S(1)} %bitcast.68), channel_id=1, source_target_pairs={{0,128},{1,129},{2,130},{3,131},{4,132},{5,133},{6,134},{7,135},{8... | collective-permute-start | bytes 1769480 | tf_op jit(solution)/shard_map/ppermute | solution.py:92
  49.3 5.4 %collective-permute-start.4 = (bf16[256,1152]{1,0:T(8,128)(2,1)S(1)}, bf16[256,1152]{1,0:T(8,128)(2,1)}, u32[]{:S(2)}, u32[]{:S(2)}) collective-permute-start(bf16[256,1152]{1,0:T(8,128)(2,1)S(1)} %bitcast.69), channel_id=1, source_target_pairs={{0,384},{1,385},{2,386},{3,387},{4,388},{5,389},{6,390},{7,391},{8... | collective-permute-start | bytes 1769480 | tf_op jit(solution)/shard_map/ppermute | solution.py:92
  55.5 2.6 %collective-permute-start.5 = (bf16[64,2048]{1,0:T(8,128)(2,1)}, bf16[64,2048]{1,0:T(8,128)(2,1)}, u32[]{:S(2)}, u32[]{:S(2)}) collective-permute-start(bf16[64,2048]{1,0:T(8,128)(2,1)} %slice.65), channel_id=1, source_target_pairs={{0,128},{1,129},{2,130},{3,131},{4,132},{5,133},{6,134},{7,135},{8... | collective-permute-start | bytes 786440 | tf_op jit(solution)/shard_map/ppermute | solution.py:92
  58.9 3.8 %collective-permute-start.6 = (bf16[64,2048]{1,0:T(8,128)(2,1)}, bf16[64,2048]{1,0:T(8,128)(2,1)}, u32[]{:S(2)}, u32[]{:S(2)}) collective-permute-start(bf16[64,2048]{1,0:T(8,128)(2,1)} %slice.66), channel_id=1, source_target_pairs={{0,384},{1,385},{2,386},{3,387},{4,388},{5,389},{6,390},{7,391},{8... | collective-permute-start | bytes 786440 | tf_op jit(solution)/shard_map/ppermute | solution.py:92
  62.7 1.0 fusion.14
  63.7 1.7 %pad_maximum_fusion.9 = (f32[128,128]{1,0:T(8,128)}, f32[128,128]{1,0:T(8,128)}) fusion(f32[128,64]{1,0:T(8,128)} %get-tuple-element.54, f32[128,64]{1,0:T(8,128)} %get-tuple-element.53, f32[128,64]{1,0:T(8,128)} %get-tuple-element.52), kind=kLoop, calls=%fused_computation.30 | loop fusion | flops 32768 | bytes 229376 | tf_op jit(solution)/shard_map/concatenate | solution.py:16
  65.4 3.5 %collective-permute-start.9 = (bf16[256,1152]{1,0:T(8,128)(2,1)S(1)}, bf16[256,1152]{1,0:T(8,128)(2,1)}, u32[]{:S(2)}, u32[]{:S(2)}) collective-permute-start(bf16[256,1152]{1,0:T(8,128)(2,1)S(1)} %bitcast.70), channel_id=1, source_target_pairs={{0,8},{1,9},{2,10},{3,11},{4,12},{5,13},{6,14},{7,15},{8,0},{9,1},... | collective-permute-start | bytes 1769480 | tf_op jit(solution)/shard_map/ppermute | solution.py:92
  69.1 5.2 %all-to-all-done.1.weight_ref = bf16[16,320,128]{2,1,0:T(8,128)(2,1)S(1)} async-done(((bf16[16,320,128]{2,1,0:T(8,128)(2,1)}), bf16[16,320,128]{2,1,0:T(8,128)(2,1)S(1)}, u32[]{:S(2)}, u32[]{:S(2)}) %all-to-all-start.1) | async-done | bytes 1310752 | tf_op jit(solution)/shard_map/all_to_all | solution.py:96
  74.4 3.0 %shard_map.127 = bf16[4,128,512]{2,1,0:T(8,128)(2,1)} custom-call(s32[3]{0:T(128)S(1)} %pad_add_fusion.place_ref, bf16[16,320,128]{2,1,0:T(8,128)(2,1)S(1)} %all-to-all-done.1.weight_ref, bf16[128,2048]{1,0:T(8,128)(2,1)S(1)} %multiply_convert_fusion.refs_0_, bf16[128,2048]{1,0:T(8,128)(2,1)S(1)} %collective-permute-done.2.refs_1_, ...), custom_call_target="tpu_custom_call" | custom-call | tf_op jit(solution)/shard_map/pallas_call | solution.py:155
  77.4 3.5 %all-to-all-start.2 = ((bf16[4,128,512]{2,1,0:T(8,128)(2,1)}), bf16[4,128,512]{2,1,0:T(8,128)(2,1)S(1)}, u32[]{:S(2)}, u32[]{:S(2)}) async-start(bf16[4,128,512]{2,1,0:T(8,128)(2,1)} %shard_map.127), calls=%async_computation.2 | async-start | bytes 1048576 | tf_op jit(solution)/shard_map/all_to_all | solution.py:96
  81.5 4.0 %collective-permute-start.10 = (bf16[256,1152]{1,0:T(8,128)(2,1)}, bf16[256,1152]{1,0:T(8,128)(2,1)S(1)}, u32[]{:S(2)}, u32[]{:S(2)}) collective-permute-start(bf16[256,1152]{1,0:T(8,128)(2,1)} %collective-permute-done.9.refs_1_), channel_id=1, source_target_pairs={{0,384},{1,385},{2,386},{3,387},{4,388},{5,389},{6,390},{7,391},{8... | collective-permute-start | bytes 1769480 | tf_op jit(solution)/shard_map/ppermute | solution.py:92
  85.5 1.9 %collective-permute-start.8 = (bf16[256,1152]{1,0:T(8,128)(2,1)}, bf16[256,1152]{1,0:T(8,128)(2,1)S(1)}, u32[]{:S(2)}, u32[]{:S(2)}) collective-permute-start(bf16[256,1152]{1,0:T(8,128)(2,1)} %collective-permute-done.3.refs_6_), channel_id=1, source_target_pairs={{0,128},{1,129},{2,130},{3,131},{4,132},{5,133},{6,134},{7,135},{8... | collective-permute-start | bytes 1769480 | tf_op jit(solution)/shard_map/ppermute | solution.py:92
  88.1 7.6 %collective-permute-start.7 = (bf16[128,768]{1,0:T(8,128)(2,1)S(1)}, bf16[128,768]{1,0:T(8,128)(2,1)S(1)}, u32[]{:S(2)}, u32[]{:S(2)}) collective-permute-start(bf16[128,768]{1,0:T(8,128)(2,1)S(1)} %convert_dynamic-update-slice_fusion), channel_id=1, source_target_pairs={{0,1},{1,0},{2,3},{3,2},{4,5},{5,4},{6,7},{7,6},{8,9},{9,8},{10,11... | collective-permute-start | bytes 589832 | tf_op jit(solution)/shard_map/ppermute | solution.py:92
  95.7 1.0 collective-permute-done.7
  98.1 3.2 %collective-permute-done.8.refs_4_ = bf16[256,1152]{1,0:T(8,128)(2,1)S(1)} collective-permute-done((bf16[256,1152]{1,0:T(8,128)(2,1)}, bf16[256,1152]{1,0:T(8,128)(2,1)S(1)}, u32[]{:S(2)}, u32[]{:S(2)}) %collective-permute-start.8) | collective-permute-done | bytes 589856 | tf_op jit(solution)/shard_map/ppermute | solution.py:92
  101.3 9.6 %all-to-all-start.3 = ((bf16[4,136,384]{2,1,0:T(8,128)(2,1)}), bf16[4,136,384]{2,1,0:T(8,128)(2,1)S(1)}, u32[]{:S(2)}, u32[]{:S(2)}) async-start(bf16[4,136,384]{2,1,0:T(8,128)(2,1)} %pad_maximum_fusion), calls=%async_computation.3 | async-start | bytes 835584 | tf_op jit(solution)/shard_map/all_to_all | solution.py:96
  110.8 2.8 %collective-permute-start.12 = (bf16[256,1152]{1,0:T(8,128)(2,1)}, bf16[256,1152]{1,0:T(8,128)(2,1)S(1)}, u32[]{:S(2)}, u32[]{:S(2)}) collective-permute-start(bf16[256,1152]{1,0:T(8,128)(2,1)} %collective-permute-done.9.refs_1_), channel_id=1, source_target_pairs={{0,128},{1,129},{2,130},{3,131},{4,132},{5,133},{6,134},{7,135},{8... | collective-permute-start | bytes 1769480 | tf_op jit(solution)/shard_map/ppermute | solution.py:92
  113.6 3.7 %collective-permute-start.11 = (bf16[256,1152]{1,0:T(8,128)(2,1)S(1)}, bf16[256,1152]{1,0:T(8,128)(2,1)}, u32[]{:S(2)}, u32[]{:S(2)}) collective-permute-start(bf16[256,1152]{1,0:T(8,128)(2,1)S(1)} %collective-permute-done.10.refs_3_), channel_id=1, source_target_pairs={{0,384},{1,385},{2,386},{3,387},{4,388},{5,389},{6,390},{7,391},{8... | collective-permute-start | bytes 1769480 | tf_op jit(solution)/shard_map/ppermute | solution.py:92
  118.0 2.8 %all-to-all-done.3.terms_ref = bf16[4,136,384]{2,1,0:T(8,128)(2,1)S(1)} async-done(((bf16[4,136,384]{2,1,0:T(8,128)(2,1)}), bf16[4,136,384]{2,1,0:T(8,128)(2,1)S(1)}, u32[]{:S(2)}, u32[]{:S(2)}) %all-to-all-start.3) | async-done | bytes 417824 | tf_op jit(solution)/shard_map/all_to_all | solution.py:96
  121.6 20.3 %all-gather.1 = bf16[1536,128]{1,0:T(8,128)(2,1)S(1)} all-gather(bf16[192,128]{1,0:T(8,128)(2,1)S(1)} %shard_map.128), channel_id=3, replica_groups=mesh['engine'=4,'fsdp'=16,'tensor'=8] {'tensor'}, dimensions={0}, use_global_device_ids=true | all-gather | bytes 442368 | tf_op jit(solution)/shard_map/all_gather | solution.py:252
  141.9 4.1 %shard_map.129 = bf16[128,2048]{1,0:T(8,128)(2,1)} custom-call(s32[3]{0:T(128)S(1)} %pad_add_fusion.place_ref, bf16[8,192,128]{2,1,0:T(8,128)(2,1)S(1)} %bitcast.72, bf16[256,1152]{1,0:T(8,128)(2,1)S(1)} %bitcast.71, bf16[256,1152]{1,0:T(8,128)(2,1)} %collective-permute-done.9.refs_1_, bf16[256,1152]{1,0:T(8,128)(2,1)} %collective-permute-done.4.refs_2_, ...), custom_call_target="tpu_custom_call" | custom-call | tf_op jit(solution)/shard_map/pallas_call | solution.py:155
  (69 shorter events, 8.3 us)
Async XLA Ops:
  0.0 0.8 copy-start
  0.0 14.5 %copy-start.8 = (bf16[2048]{0:T(1024)(128)(2,1)S(1)}, bf16[2048]{0:T(1024)(128)(2,1)}, u32[]{:S(2)}) copy-start(bf16[2048]{0:T(1024)(128)(2,1)} %param.14) | copy-start | bytes 12292
  0.0 14.5 %copy-start.6 = (bf16[128,2048]{1,0:T(8,128)(2,1)S(1)}, bf16[128,2048]{1,0:T(8,128)(2,1)}, u32[]{:S(2)}) copy-start(bf16[128,2048]{1,0:T(8,128)(2,1)} %param.13) | copy-start | bytes 1572868
  2.8 24.6 %copy-start.7 = (bf16[1,32,256]{2,1,0:T(8,128)(2,1)S(1)}, bf16[1,32,256]{2,1,0:T(8,128)(2,1)}, u32[]{:S(2)}) copy-start(bf16[1,32,256]{2,1,0:T(8,128)(2,1)} %param.18) | copy-start | bytes 49156
  3.6 31.1 %all-to-all-start = ((bf16[8,32,1152]{2,1,0:T(8,128)(2,1)}), bf16[8,32,1152]{2,1,0:T(8,128)(2,1)S(1)}, u32[]{:S(2)}, u32[]{:S(2)}) async-start(bf16[8,32,1152]{2,1,0:T(8,128)(2,1)} %broadcast_in_dim.18), calls=%async_computation | async-start | bytes 1179648 | tf_op jit(solution)/shard_map/all_to_all | solution.py:96
  14.6 16.5 %collective-permute-start.1 = (bf16[128,2048]{1,0:T(8,128)(2,1)S(1)}, bf16[128,2048]{1,0:T(8,128)(2,1)S(1)}, u32[]{:S(2)}, u32[]{:S(2)}) collective-permute-start(bf16[128,2048]{1,0:T(8,128)(2,1)S(1)} %multiply_convert_fusion.refs_0_), channel_id=1, source_target_pairs={{0,128},{1,129},{2,130},{3,131},{4,132},{5,133},{6,134},{7,135},{8... | collective-permute-start | bytes 1572872 | tf_op jit(solution)/shard_map/ppermute | solution.py:92
  17.8 14.1 %collective-permute-start.2 = (bf16[128,2048]{1,0:T(8,128)(2,1)S(1)}, bf16[128,2048]{1,0:T(8,128)(2,1)S(1)}, u32[]{:S(2)}, u32[]{:S(2)}) collective-permute-start(bf16[128,2048]{1,0:T(8,128)(2,1)S(1)} %multiply_convert_fusion.refs_0_), channel_id=1, source_target_pairs={{0,384},{1,385},{2,386},{3,387},{4,388},{5,389},{6,390},{7,391},{8... | collective-permute-start | bytes 1572872 | tf_op jit(solution)/shard_map/ppermute | solution.py:92
  21.1 10.0 %collective-permute-start = (bf16[256,128]{1,0:T(8,128)(2,1)S(1)}, bf16[256,128]{1,0:T(8,128)(2,1)S(1)}, u32[]{:S(2)}, u32[]{:S(2)}) collective-permute-start(bf16[256,128]{1,0:T(8,128)(2,1)S(1)} %fusion.1), channel_id=1, source_target_pairs={{0,0},{1,112},{2,128},{3,240},{4,256},{5,368},{6,384},{7,496},{8,8... | collective-permute-start | bytes 196616 | tf_op jit(solution)/shard_map/ppermute | solution.py:92
  36.0 18.7 %copy-start.9 = (s32[1,128]{1,0:T(1,128)S(1)}, s32[1,128]{1,0:T(1,128)}, u32[]{:S(2)}) copy-start(s32[1,128]{1,0:T(1,128)} %param.24) | copy-start | bytes 1540
  36.1 38.2 %all-to-all-start.1 = ((bf16[16,320,128]{2,1,0:T(8,128)(2,1)}), bf16[16,320,128]{2,1,0:T(8,128)(2,1)S(1)}, u32[]{:S(2)}, u32[]{:S(2)}) async-start(bf16[16,320,128]{2,1,0:T(8,128)(2,1)} %broadcast_in_dim.17), calls=%async_computation.1 | async-start | bytes 2621440 | tf_op jit(solution)/shard_map/all_to_all | solution.py:96
  46.9 22.2 %collective-permute-start.3 = (bf16[256,1152]{1,0:T(8,128)(2,1)S(1)}, bf16[256,1152]{1,0:T(8,128)(2,1)}, u32[]{:S(2)}, u32[]{:S(2)}) collective-permute-start(bf16[256,1152]{1,0:T(8,128)(2,1)S(1)} %bitcast.68), channel_id=1, source_target_pairs={{0,128},{1,129},{2,130},{3,131},{4,132},{5,133},{6,134},{7,135},{8... | collective-permute-start | bytes 1769480 | tf_op jit(solution)/shard_map/ppermute | solution.py:92
  49.3 19.7 %collective-permute-start.4 = (bf16[256,1152]{1,0:T(8,128)(2,1)S(1)}, bf16[256,1152]{1,0:T(8,128)(2,1)}, u32[]{:S(2)}, u32[]{:S(2)}) collective-permute-start(bf16[256,1152]{1,0:T(8,128)(2,1)S(1)} %bitcast.69), channel_id=1, source_target_pairs={{0,384},{1,385},{2,386},{3,387},{4,388},{5,389},{6,390},{7,391},{8... | collective-permute-start | bytes 1769480 | tf_op jit(solution)/shard_map/ppermute | solution.py:92
  55.5 18.7 %collective-permute-start.5 = (bf16[64,2048]{1,0:T(8,128)(2,1)}, bf16[64,2048]{1,0:T(8,128)(2,1)}, u32[]{:S(2)}, u32[]{:S(2)}) collective-permute-start(bf16[64,2048]{1,0:T(8,128)(2,1)} %slice.65), channel_id=1, source_target_pairs={{0,128},{1,129},{2,130},{3,131},{4,132},{5,133},{6,134},{7,135},{8... | collective-permute-start | bytes 786440 | tf_op jit(solution)/shard_map/ppermute | solution.py:92
  58.9 15.5 %collective-permute-start.6 = (bf16[64,2048]{1,0:T(8,128)(2,1)}, bf16[64,2048]{1,0:T(8,128)(2,1)}, u32[]{:S(2)}, u32[]{:S(2)}) collective-permute-start(bf16[64,2048]{1,0:T(8,128)(2,1)} %slice.66), channel_id=1, source_target_pairs={{0,384},{1,385},{2,386},{3,387},{4,388},{5,389},{6,390},{7,391},{8... | collective-permute-start | bytes 786440 | tf_op jit(solution)/shard_map/ppermute | solution.py:92
  65.4 16.1 %collective-permute-start.9 = (bf16[256,1152]{1,0:T(8,128)(2,1)S(1)}, bf16[256,1152]{1,0:T(8,128)(2,1)}, u32[]{:S(2)}, u32[]{:S(2)}) collective-permute-start(bf16[256,1152]{1,0:T(8,128)(2,1)S(1)} %bitcast.70), channel_id=1, source_target_pairs={{0,8},{1,9},{2,10},{3,11},{4,12},{5,13},{6,14},{7,15},{8,0},{9,1},... | collective-permute-start | bytes 1769480 | tf_op jit(solution)/shard_map/ppermute | solution.py:92
  77.4 10.4 %all-to-all-start.2 = ((bf16[4,128,512]{2,1,0:T(8,128)(2,1)}), bf16[4,128,512]{2,1,0:T(8,128)(2,1)S(1)}, u32[]{:S(2)}, u32[]{:S(2)}) async-start(bf16[4,128,512]{2,1,0:T(8,128)(2,1)} %shard_map.127), calls=%async_computation.2 | async-start | bytes 1048576 | tf_op jit(solution)/shard_map/all_to_all | solution.py:96
  81.5 16.6 %collective-permute-start.10 = (bf16[256,1152]{1,0:T(8,128)(2,1)}, bf16[256,1152]{1,0:T(8,128)(2,1)S(1)}, u32[]{:S(2)}, u32[]{:S(2)}) collective-permute-start(bf16[256,1152]{1,0:T(8,128)(2,1)} %collective-permute-done.9.refs_1_), channel_id=1, source_target_pairs={{0,384},{1,385},{2,386},{3,387},{4,388},{5,389},{6,390},{7,391},{8... | collective-permute-start | bytes 1769480 | tf_op jit(solution)/shard_map/ppermute | solution.py:92
  85.5 15.8 %collective-permute-start.8 = (bf16[256,1152]{1,0:T(8,128)(2,1)}, bf16[256,1152]{1,0:T(8,128)(2,1)S(1)}, u32[]{:S(2)}, u32[]{:S(2)}) collective-permute-start(bf16[256,1152]{1,0:T(8,128)(2,1)} %collective-permute-done.3.refs_6_), channel_id=1, source_target_pairs={{0,128},{1,129},{2,130},{3,131},{4,132},{5,133},{6,134},{7,135},{8... | collective-permute-start | bytes 1769480 | tf_op jit(solution)/shard_map/ppermute | solution.py:92
  88.1 8.7 %collective-permute-start.7 = (bf16[128,768]{1,0:T(8,128)(2,1)S(1)}, bf16[128,768]{1,0:T(8,128)(2,1)S(1)}, u32[]{:S(2)}, u32[]{:S(2)}) collective-permute-start(bf16[128,768]{1,0:T(8,128)(2,1)S(1)} %convert_dynamic-update-slice_fusion), channel_id=1, source_target_pairs={{0,1},{1,0},{2,3},{3,2},{4,5},{5,4},{6,7},{7,6},{8,9},{9,8},{10,11... | collective-permute-start | bytes 589832 | tf_op jit(solution)/shard_map/ppermute | solution.py:92
  96.8 24.0 %copy-start.1 = (f32[128,128]{1,0:T(8,128)S(1)}, f32[128,128]{1,0:T(8,128)}, u32[]{:S(2)}) copy-start(f32[128,128]{1,0:T(8,128)} %get-tuple-element.38.cosine_ref) | copy-start | bytes 196612
  96.8 24.0 %copy-start.2 = (f32[128,128]{1,0:T(8,128)S(1)}, f32[128,128]{1,0:T(8,128)}, u32[]{:S(2)}) copy-start(f32[128,128]{1,0:T(8,128)} %get-tuple-element.39.sine_ref) | copy-start | bytes 196612
  96.9 24.0 %copy-start.3 = (bf16[1,512,128]{2,1,0:T(8,128)(2,1)S(1)}, bf16[1,512,128]{2,1,0:T(8,128)(2,1)}, u32[]{:S(2)}) copy-start(bf16[1,512,128]{2,1,0:T(8,128)(2,1)} %param.22) | copy-start | bytes 393220
  96.9 24.0 %copy-start.4 = (bf16[1,512,128]{2,1,0:T(8,128)(2,1)S(1)}, bf16[1,512,128]{2,1,0:T(8,128)(2,1)}, u32[]{:S(2)}) copy-start(bf16[1,512,128]{2,1,0:T(8,128)(2,1)} %param.23) | copy-start | bytes 393220
  96.9 24.0 %copy-start.5 = (bf16[128,64]{0,1:T(8,128)(2,1)S(1)}, bf16[128,64]{0,1:T(8,128)(2,1)}, u32[]{:S(2)}) copy-start(bf16[128,64]{0,1:T(8,128)(2,1)} %param.20) | copy-start | bytes 49156
  101.3 19.6 %all-to-all-start.3 = ((bf16[4,136,384]{2,1,0:T(8,128)(2,1)}), bf16[4,136,384]{2,1,0:T(8,128)(2,1)S(1)}, u32[]{:S(2)}, u32[]{:S(2)}) async-start(bf16[4,136,384]{2,1,0:T(8,128)(2,1)} %pad_maximum_fusion), calls=%async_computation.3 | async-start | bytes 835584 | tf_op jit(solution)/shard_map/all_to_all | solution.py:96
  110.8 31.0 %collective-permute-start.12 = (bf16[256,1152]{1,0:T(8,128)(2,1)}, bf16[256,1152]{1,0:T(8,128)(2,1)S(1)}, u32[]{:S(2)}, u32[]{:S(2)}) collective-permute-start(bf16[256,1152]{1,0:T(8,128)(2,1)} %collective-permute-done.9.refs_1_), channel_id=1, source_target_pairs={{0,128},{1,129},{2,130},{3,131},{4,132},{5,133},{6,134},{7,135},{8... | collective-permute-start | bytes 1769480 | tf_op jit(solution)/shard_map/ppermute | solution.py:92
  113.6 28.2 %collective-permute-start.11 = (bf16[256,1152]{1,0:T(8,128)(2,1)S(1)}, bf16[256,1152]{1,0:T(8,128)(2,1)}, u32[]{:S(2)}, u32[]{:S(2)}) collective-permute-start(bf16[256,1152]{1,0:T(8,128)(2,1)S(1)} %collective-permute-done.10.refs_3_), channel_id=1, source_target_pairs={{0,384},{1,385},{2,386},{3,387},{4,388},{5,389},{6,390},{7,391},{8... | collective-permute-start | bytes 1769480 | tf_op jit(solution)/shard_map/ppermute | solution.py:92

commit v6 on v5

--- a/solution.py
+++ b/solution.py
@@ -214,8 +214,6 @@
     tokens = (scaled, after, across_low, across_high, before)
     theirs = move(mine, other_y)
     mine_before, mine_after = move(mine, next_engine), move(mine, last_engine)
-    gathered, mine_before, mine_after = lax.optimization_barrier((gathered, mine_before, mine_after))
-    mine_across = move(mine_before, next_engine)
 
     terms = compute(terms_kernel, (4, 128, 512), place, (gathered, *tokens))
     theirs_before, theirs_after = move(theirs, next_engine), move(theirs, last_engine)
@@ -238,10 +236,11 @@
             for i in range(4)
         ]
     )
-    terms, mine_across, theirs_after, cosine, sine = lax.optimization_barrier(
-        (terms, mine_across, theirs_after, cosine, sine)
+    terms, mine_before, mine_after, theirs_after, cosine, sine = lax.optimization_barrier(
+        (terms, mine_before, mine_after, theirs_after, cosine, sine)
     )
     theirs_across = move(theirs_after, last_engine)
+    mine_across = move(mine_before, next_engine)
     terms = exchange(terms, "tensor", ACROSS)
     heads = compute(
         attend_kernel,

time: 147 us -> 142 us (0.966)
  starting transfers between devices: 82 us -> 78.8 us
  waiting for transfers between devices: 20.8 us -> 17.6 us
  blocking collectives: 22.5 us -> 24.8 us
    all_to_all x4, waiting for transfers between devices: 11.3 us -> 7.91 us  [exchange(): lax.all_to_all(array, axis, split_axis=0, concat_axis=0, tiled=True, axis...]
    all_to_all x4, starting transfers between devices: 31.3 us -> 28.5 us  [exchange(): lax.all_to_all(array, axis, split_axis=0, concat_axis=0, tiled=True, axis...]
    all_gather x1, blocking collectives: 2.16 us -> 3.97 us  [per_device(): lax.all_gather(squares, 'tensor', axis=0, tiled=True, axis_index_groups=C...]
  transfers between devices with their start and end apart: 17 -> 17, of which waited for: 11 -> 6; matrix products, arithmetic and copies ran while one was open for 5% -> 5% of each run, Pallas kernels for 3% -> 3%
where the time goes in v6:
time: 142 us; the launch traced here: 141 us
  starting transfers between devices  78.8 us (55%)
  blocking collectives  24.8 us (17%)
  waiting for transfers between devices  17.6 us (12%)
  Pallas kernels  7.77 us (5%)
  other arithmetic  5.24 us (4%)
  local copies, waits for them, and re-layouts  4.87 us (3%)
    ppermute x13, starting transfers between devices, move(): return lax.ppermute(array, AXES, pairs)  50.2 us
    all_to_all x4, starting transfers between devices, exchange(): lax.all_to_all(array, axis, split_axis=0, concat_axis=0, tiled=True, axis...  28.5 us
    all_gather x1, blocking collectives, per_device(): heads = lax.all_gather(heads[None], 'tensor', axis=0, tiled=True)  20.8 us
    ppermute x13, waiting for transfers between devices, move(): return lax.ppermute(array, AXES, pairs)  9.72 us
    all_to_all x4, waiting for transfers between devices, exchange(): lax.all_to_all(array, axis, split_axis=0, concat_axis=0, tiled=True, axis...  7.91 us
    pallas_call x3, Pallas kernels, compute(): pl.pallas_call(kernel, out_shape=jax.ShapeDtypeStruct(shape, jnp.bfloat16...  7.77 us
    all_gather x1, blocking collectives, per_device(): lax.all_gather(squares, 'tensor', axis=0, tiled=True, axis_index_groups=C...  3.97 us
  transfers between devices with their start and end apart: 17, of which 6 were waited for; matrix products, arithmetic and copies ran while one was open for 5% of the time, Pallas kernels for 3%

profile of v6, /device:TPU:1, one launch (start us, length us, event | category | flops | bytes accessed | tf_op | source)
XLA Modules:
  0.0 141.3 jit_solution(2557530340879291076)
XLA Ops:
  0.0 1.0 concatenate.46
  1.0 1.1 fusion.1
  2.9 10.9 %all-to-all-start = ((bf16[8,32,1152]{2,1,0:T(8,128)(2,1)}), bf16[8,32,1152]{2,1,0:T(8,128)(2,1)S(1)}, u32[]{:S(2)}, u32[]{:S(2)}) async-start(bf16[8,32,1152]{2,1,0:T(8,128)(2,1)} %broadcast_in_dim.18), calls=%async_computation | async-start | bytes 1179648 | tf_op jit(solution)/shard_map/all_to_all | solution.py:96
  13.9 4.4 %collective-permute-start.2 = (bf16[128,2048]{1,0:T(8,128)(2,1)S(1)}, bf16[128,2048]{1,0:T(8,128)(2,1)S(1)}, u32[]{:S(2)}, u32[]{:S(2)}) collective-permute-start(bf16[128,2048]{1,0:T(8,128)(2,1)S(1)} %multiply_convert_fusion.refs_0_), channel_id=1, source_target_pairs={{0,384},{1,385},{2,386},{3,387},{4,388},{5,389},{6,390},{7,391},{8... | collective-permute-start | bytes 1572872 | tf_op jit(solution)/shard_map/ppermute | solution.py:92
  18.3 1.9 %collective-permute-start.1 = (bf16[128,2048]{1,0:T(8,128)(2,1)S(1)}, bf16[128,2048]{1,0:T(8,128)(2,1)S(1)}, u32[]{:S(2)}, u32[]{:S(2)}) collective-permute-start(bf16[128,2048]{1,0:T(8,128)(2,1)S(1)} %multiply_convert_fusion.refs_0_), channel_id=1, source_target_pairs={{0,128},{1,129},{2,130},{3,131},{4,132},{5,133},{6,134},{7,135},{8... | collective-permute-start | bytes 1572872 | tf_op jit(solution)/shard_map/ppermute | solution.py:92
  20.3 6.0 %collective-permute-start = (bf16[256,128]{1,0:T(8,128)(2,1)S(1)}, bf16[256,128]{1,0:T(8,128)(2,1)S(1)}, u32[]{:S(2)}, u32[]{:S(2)}) collective-permute-start(bf16[256,128]{1,0:T(8,128)(2,1)S(1)} %fusion.1), channel_id=1, source_target_pairs={{0,0},{1,112},{2,128},{3,240},{4,256},{5,368},{6,384},{7,496},{8,8... | collective-permute-start | bytes 196616 | tf_op jit(solution)/shard_map/ppermute | solution.py:92
  26.3 4.2 %collective-permute-done = bf16[256,128]{1,0:T(8,128)(2,1)S(1)} collective-permute-done((bf16[256,128]{1,0:T(8,128)(2,1)S(1)}, bf16[256,128]{1,0:T(8,128)(2,1)S(1)}, u32[]{:S(2)}, u32[]{:S(2)}) %collective-permute-start) | collective-permute-done | bytes 65568 | tf_op jit(solution)/shard_map/ppermute | solution.py:92
  30.5 3.2 %collective-permute-done.1.refs_4_ = bf16[128,2048]{1,0:T(8,128)(2,1)S(1)} collective-permute-done((bf16[128,2048]{1,0:T(8,128)(2,1)S(1)}, bf16[128,2048]{1,0:T(8,128)(2,1)S(1)}, u32[]{:S(2)}, u32[]{:S(2)}) %collective-permute-start.1) | collective-permute-done | bytes 524320 | tf_op jit(solution)/shard_map/ppermute | solution.py:92
  33.6 1.3 broadcast_in_dim.17
  35.0 7.8 %all-to-all-start.1 = ((bf16[16,320,128]{2,1,0:T(8,128)(2,1)}), bf16[16,320,128]{2,1,0:T(8,128)(2,1)S(1)}, u32[]{:S(2)}, u32[]{:S(2)}) async-start(bf16[16,320,128]{2,1,0:T(8,128)(2,1)} %broadcast_in_dim.17), calls=%async_computation.1 | async-start | bytes 2621440 | tf_op jit(solution)/shard_map/all_to_all | solution.py:96
  42.8 1.2 multiply_reduce_fusion
  44.0 4.0 %all-gather.2 = f32[2,1,128]{2,1,0:T(1,128)S(1)} all-gather(f32[1,1,128]{2,1,0:T(1,128)S(1)} %bitcast.79), channel_id=2, replica_groups={{0,1},{2,3},{4,5},{6,7},{8,9},{10,11},{12,13},{14,15},{16,17},{18,19},{..., dimensions={0}, use_global_device_ids=true | all-gather | bytes 1536 | tf_op jit(solution)/shard_map/all_gather | solution.py:209
  49.5 3.5 %collective-permute-start.3 = (bf16[64,2048]{1,0:T(8,128)(2,1)}, bf16[64,2048]{1,0:T(8,128)(2,1)}, u32[]{:S(2)}, u32[]{:S(2)}) collective-permute-start(bf16[64,2048]{1,0:T(8,128)(2,1)} %slice.65), channel_id=1, source_target_pairs={{0,128},{1,129},{2,130},{3,131},{4,132},{5,133},{6,134},{7,135},{8... | collective-permute-start | bytes 786440 | tf_op jit(solution)/shard_map/ppermute | solution.py:92
  53.0 4.1 %collective-permute-start.4 = (bf16[64,2048]{1,0:T(8,128)(2,1)}, bf16[64,2048]{1,0:T(8,128)(2,1)}, u32[]{:S(2)}, u32[]{:S(2)}) collective-permute-start(bf16[64,2048]{1,0:T(8,128)(2,1)} %slice.66), channel_id=1, source_target_pairs={{0,384},{1,385},{2,386},{3,387},{4,388},{5,389},{6,390},{7,391},{8... | collective-permute-start | bytes 786440 | tf_op jit(solution)/shard_map/ppermute | solution.py:92
  57.1 1.0 fusion.14
  58.1 1.7 %pad_maximum_fusion.9 = (f32[128,128]{1,0:T(8,128)}, f32[128,128]{1,0:T(8,128)}) fusion(f32[128,64]{1,0:T(8,128)} %get-tuple-element.50, f32[128,64]{1,0:T(8,128)} %get-tuple-element.49, f32[128,64]{1,0:T(8,128)} %get-tuple-element.48), kind=kLoop, calls=%fused_computation.30 | loop fusion | flops 32768 | bytes 229376 | tf_op jit(solution)/shard_map/concatenate | solution.py:16
  59.8 3.5 %collective-permute-start.8 = (bf16[256,1152]{1,0:T(8,128)(2,1)S(1)}, bf16[256,1152]{1,0:T(8,128)(2,1)}, u32[]{:S(2)}, u32[]{:S(2)}) collective-permute-start(bf16[256,1152]{1,0:T(8,128)(2,1)S(1)} %bitcast.68), channel_id=1, source_target_pairs={{0,8},{1,9},{2,10},{3,11},{4,12},{5,13},{6,14},{7,15},{8,0},{9,1},... | collective-permute-start | bytes 1769480 | tf_op jit(solution)/shard_map/ppermute | solution.py:92
  63.4 3.4 %collective-permute-start.7 = (bf16[256,1152]{1,0:T(8,128)(2,1)S(1)}, bf16[256,1152]{1,0:T(8,128)(2,1)}, u32[]{:S(2)}, u32[]{:S(2)}) collective-permute-start(bf16[256,1152]{1,0:T(8,128)(2,1)S(1)} %bitcast.69), channel_id=1, source_target_pairs={{0,384},{1,385},{2,386},{3,387},{4,388},{5,389},{6,390},{7,391},{8... | collective-permute-start | bytes 1769480 | tf_op jit(solution)/shard_map/ppermute | solution.py:92
  66.8 1.9 %collective-permute-start.6 = (bf16[256,1152]{1,0:T(8,128)(2,1)S(1)}, bf16[256,1152]{1,0:T(8,128)(2,1)}, u32[]{:S(2)}, u32[]{:S(2)}) collective-permute-start(bf16[256,1152]{1,0:T(8,128)(2,1)S(1)} %bitcast.70), channel_id=1, source_target_pairs={{0,128},{1,129},{2,130},{3,131},{4,132},{5,133},{6,134},{7,135},{8... | collective-permute-start | bytes 1769480 | tf_op jit(solution)/shard_map/ppermute | solution.py:92
  68.7 5.2 %all-to-all-done.1.weight_ref = bf16[16,320,128]{2,1,0:T(8,128)(2,1)S(1)} async-done(((bf16[16,320,128]{2,1,0:T(8,128)(2,1)}), bf16[16,320,128]{2,1,0:T(8,128)(2,1)S(1)}, u32[]{:S(2)}, u32[]{:S(2)}) %all-to-all-start.1) | async-done | bytes 1310752 | tf_op jit(solution)/shard_map/all_to_all | solution.py:96
  73.9 3.0 %shard_map.127 = bf16[4,128,512]{2,1,0:T(8,128)(2,1)} custom-call(s32[3]{0:T(128)S(1)} %pad_add_fusion.place_ref, bf16[16,320,128]{2,1,0:T(8,128)(2,1)S(1)} %all-to-all-done.1.weight_ref, bf16[128,2048]{1,0:T(8,128)(2,1)S(1)} %multiply_convert_fusion.refs_0_, bf16[128,2048]{1,0:T(8,128)(2,1)S(1)} %collective-permute-done.2.refs_1_, ...), custom_call_target="tpu_custom_call" | custom-call | tf_op jit(solution)/shard_map/pallas_call | solution.py:155
  76.9 3.5 %all-to-all-start.2 = ((bf16[4,128,512]{2,1,0:T(8,128)(2,1)}), bf16[4,128,512]{2,1,0:T(8,128)(2,1)S(1)}, u32[]{:S(2)}, u32[]{:S(2)}) async-start(bf16[4,128,512]{2,1,0:T(8,128)(2,1)} %shard_map.127), calls=%async_computation.2 | async-start | bytes 1048576 | tf_op jit(solution)/shard_map/all_to_all | solution.py:96
  80.4 4.5 %collective-permute-start.9 = (bf16[256,1152]{1,0:T(8,128)(2,1)}, bf16[256,1152]{1,0:T(8,128)(2,1)S(1)}, u32[]{:S(2)}, u32[]{:S(2)}) collective-permute-start(bf16[256,1152]{1,0:T(8,128)(2,1)} %collective-permute-done.8.refs_1_), channel_id=1, source_target_pairs={{0,384},{1,385},{2,386},{3,387},{4,388},{5,389},{6,390},{7,391},{8... | collective-permute-start | bytes 1769480 | tf_op jit(solution)/shard_map/ppermute | solution.py:92
  85.0 2.7 %all-to-all-done.2 = bf16[4,128,512]{2,1,0:T(8,128)(2,1)S(1)} async-done(((bf16[4,128,512]{2,1,0:T(8,128)(2,1)}), bf16[4,128,512]{2,1,0:T(8,128)(2,1)S(1)}, u32[]{:S(2)}, u32[]{:S(2)}) %all-to-all-start.2) | async-done | bytes 524320 | tf_op jit(solution)/shard_map/all_to_all | solution.py:96
  88.0 6.0 %collective-permute-start.5 = (bf16[128,768]{1,0:T(8,128)(2,1)S(1)}, bf16[128,768]{1,0:T(8,128)(2,1)S(1)}, u32[]{:S(2)}, u32[]{:S(2)}) collective-permute-start(bf16[128,768]{1,0:T(8,128)(2,1)S(1)} %convert_dynamic-update-slice_fusion), channel_id=1, source_target_pairs={{0,1},{1,0},{2,3},{3,2},{4,5},{5,4},{6,7},{7,6},{8,9},{9,8},{10,11... | collective-permute-start | bytes 589832 | tf_op jit(solution)/shard_map/ppermute | solution.py:92
  96.2 1.4 collective-permute-done.9.refs_3_
  97.5 6.4 %all-to-all-start.3 = ((bf16[4,136,384]{2,1,0:T(8,128)(2,1)}), bf16[4,136,384]{2,1,0:T(8,128)(2,1)S(1)}, u32[]{:S(2)}, u32[]{:S(2)}) async-start(bf16[4,136,384]{2,1,0:T(8,128)(2,1)} %pad_maximum_fusion), calls=%async_computation.3 | async-start | bytes 835584 | tf_op jit(solution)/shard_map/all_to_all | solution.py:96
  103.9 5.7 %collective-permute-start.12 = (bf16[256,1152]{1,0:T(8,128)(2,1)}, bf16[256,1152]{1,0:T(8,128)(2,1)S(1)}, u32[]{:S(2)}, u32[]{:S(2)}) collective-permute-start(bf16[256,1152]{1,0:T(8,128)(2,1)} %collective-permute-done.8.refs_1_), channel_id=1, source_target_pairs={{0,128},{1,129},{2,130},{3,131},{4,132},{5,133},{6,134},{7,135},{8... | collective-permute-start | bytes 1769480 | tf_op jit(solution)/shard_map/ppermute | solution.py:92
  109.6 1.9 %collective-permute-start.11 = (bf16[256,1152]{1,0:T(8,128)(2,1)S(1)}, bf16[256,1152]{1,0:T(8,128)(2,1)S(1)}, u32[]{:S(2)}, u32[]{:S(2)}) collective-permute-start(bf16[256,1152]{1,0:T(8,128)(2,1)S(1)} %collective-permute-done.9.refs_3_), channel_id=1, source_target_pairs={{0,384},{1,385},{2,386},{3,387},{4,388},{5,389},{6,390},{7,391},{8... | collective-permute-start | bytes 1769480 | tf_op jit(solution)/shard_map/ppermute | solution.py:92
  111.6 3.4 %collective-permute-start.10 = (bf16[256,1152]{1,0:T(8,128)(2,1)}, bf16[256,1152]{1,0:T(8,128)(2,1)}, u32[]{:S(2)}, u32[]{:S(2)}) collective-permute-start(bf16[256,1152]{1,0:T(8,128)(2,1)} %collective-permute-done.6.refs_6_), channel_id=1, source_target_pairs={{0,128},{1,129},{2,130},{3,131},{4,132},{5,133},{6,134},{7,135},{8... | collective-permute-start | bytes 1769480 | tf_op jit(solution)/shard_map/ppermute | solution.py:92
  116.4 20.8 %all-gather.1 = bf16[1536,128]{1,0:T(8,128)(2,1)S(1)} all-gather(bf16[192,128]{1,0:T(8,128)(2,1)S(1)} %shard_map.128), channel_id=3, replica_groups=mesh['engine'=4,'fsdp'=16,'tensor'=8] {'tensor'}, dimensions={0}, use_global_device_ids=true | all-gather | bytes 442368 | tf_op jit(solution)/shard_map/all_gather | solution.py:251
  137.2 4.1 %shard_map.129 = bf16[128,2048]{1,0:T(8,128)(2,1)} custom-call(s32[3]{0:T(128)S(1)} %pad_add_fusion.place_ref, bf16[8,192,128]{2,1,0:T(8,128)(2,1)S(1)} %bitcast.72, bf16[256,1152]{1,0:T(8,128)(2,1)S(1)} %bitcast.71, bf16[256,1152]{1,0:T(8,128)(2,1)} %collective-permute-done.8.refs_1_, bf16[256,1152]{1,0:T(8,128)(2,1)} %collective-permute-done.7.refs_2_, ...), custom_call_target="tpu_custom_call" | custom-call | tf_op jit(solution)/shard_map/pallas_call | solution.py:155
  (69 shorter events, 5.6 us)
Async XLA Ops:
  0.0 1.0 copy-start
  0.0 13.8 %copy-start.8 = (bf16[2048]{0:T(1024)(128)(2,1)S(1)}, bf16[2048]{0:T(1024)(128)(2,1)}, u32[]{:S(2)}) copy-start(bf16[2048]{0:T(1024)(128)(2,1)} %param.14) | copy-start | bytes 12292
  0.0 13.8 %copy-start.6 = (bf16[128,2048]{1,0:T(8,128)(2,1)S(1)}, bf16[128,2048]{1,0:T(8,128)(2,1)}, u32[]{:S(2)}) copy-start(bf16[128,2048]{1,0:T(8,128)(2,1)} %param.13) | copy-start | bytes 1572868
  2.1 24.2 %copy-start.7 = (bf16[1,32,256]{2,1,0:T(8,128)(2,1)S(1)}, bf16[1,32,256]{2,1,0:T(8,128)(2,1)}, u32[]{:S(2)}) copy-start(bf16[1,32,256]{2,1,0:T(8,128)(2,1)} %param.18) | copy-start | bytes 49156
  2.9 30.7 %all-to-all-start = ((bf16[8,32,1152]{2,1,0:T(8,128)(2,1)}), bf16[8,32,1152]{2,1,0:T(8,128)(2,1)S(1)}, u32[]{:S(2)}, u32[]{:S(2)}) async-start(bf16[8,32,1152]{2,1,0:T(8,128)(2,1)} %broadcast_in_dim.18), calls=%async_computation | async-start | bytes 1179648 | tf_op jit(solution)/shard_map/all_to_all | solution.py:96
  13.9 16.5 %collective-permute-start.2 = (bf16[128,2048]{1,0:T(8,128)(2,1)S(1)}, bf16[128,2048]{1,0:T(8,128)(2,1)S(1)}, u32[]{:S(2)}, u32[]{:S(2)}) collective-permute-start(bf16[128,2048]{1,0:T(8,128)(2,1)S(1)} %multiply_convert_fusion.refs_0_), channel_id=1, source_target_pairs={{0,384},{1,385},{2,386},{3,387},{4,388},{5,389},{6,390},{7,391},{8... | collective-permute-start | bytes 1572872 | tf_op jit(solution)/shard_map/ppermute | solution.py:92
  18.3 15.3 %collective-permute-start.1 = (bf16[128,2048]{1,0:T(8,128)(2,1)S(1)}, bf16[128,2048]{1,0:T(8,128)(2,1)S(1)}, u32[]{:S(2)}, u32[]{:S(2)}) collective-permute-start(bf16[128,2048]{1,0:T(8,128)(2,1)S(1)} %multiply_convert_fusion.refs_0_), channel_id=1, source_target_pairs={{0,128},{1,129},{2,130},{3,131},{4,132},{5,133},{6,134},{7,135},{8... | collective-permute-start | bytes 1572872 | tf_op jit(solution)/shard_map/ppermute | solution.py:92
  20.3 10.2 %collective-permute-start = (bf16[256,128]{1,0:T(8,128)(2,1)S(1)}, bf16[256,128]{1,0:T(8,128)(2,1)S(1)}, u32[]{:S(2)}, u32[]{:S(2)}) collective-permute-start(bf16[256,128]{1,0:T(8,128)(2,1)S(1)} %fusion.1), channel_id=1, source_target_pairs={{0,0},{1,112},{2,128},{3,240},{4,256},{5,368},{6,384},{7,496},{8,8... | collective-permute-start | bytes 196616 | tf_op jit(solution)/shard_map/ppermute | solution.py:92
  35.0 7.8 %copy-start.9 = (s32[1,128]{1,0:T(1,128)S(1)}, s32[1,128]{1,0:T(1,128)}, u32[]{:S(2)}) copy-start(s32[1,128]{1,0:T(1,128)} %param.24) | copy-start | bytes 1540
  35.0 38.9 %all-to-all-start.1 = ((bf16[16,320,128]{2,1,0:T(8,128)(2,1)}), bf16[16,320,128]{2,1,0:T(8,128)(2,1)S(1)}, u32[]{:S(2)}, u32[]{:S(2)}) async-start(bf16[16,320,128]{2,1,0:T(8,128)(2,1)} %broadcast_in_dim.17), calls=%async_computation.1 | async-start | bytes 2621440 | tf_op jit(solution)/shard_map/all_to_all | solution.py:96
  49.5 19.2 %collective-permute-start.3 = (bf16[64,2048]{1,0:T(8,128)(2,1)}, bf16[64,2048]{1,0:T(8,128)(2,1)}, u32[]{:S(2)}, u32[]{:S(2)}) collective-permute-start(bf16[64,2048]{1,0:T(8,128)(2,1)} %slice.65), channel_id=1, source_target_pairs={{0,128},{1,129},{2,130},{3,131},{4,132},{5,133},{6,134},{7,135},{8... | collective-permute-start | bytes 786440 | tf_op jit(solution)/shard_map/ppermute | solution.py:92
  53.0 15.7 %collective-permute-start.4 = (bf16[64,2048]{1,0:T(8,128)(2,1)}, bf16[64,2048]{1,0:T(8,128)(2,1)}, u32[]{:S(2)}, u32[]{:S(2)}) collective-permute-start(bf16[64,2048]{1,0:T(8,128)(2,1)} %slice.66), channel_id=1, source_target_pairs={{0,384},{1,385},{2,386},{3,387},{4,388},{5,389},{6,390},{7,391},{8... | collective-permute-start | bytes 786440 | tf_op jit(solution)/shard_map/ppermute | solution.py:92
  59.8 20.7 %collective-permute-start.8 = (bf16[256,1152]{1,0:T(8,128)(2,1)S(1)}, bf16[256,1152]{1,0:T(8,128)(2,1)}, u32[]{:S(2)}, u32[]{:S(2)}) collective-permute-start(bf16[256,1152]{1,0:T(8,128)(2,1)S(1)} %bitcast.68), channel_id=1, source_target_pairs={{0,8},{1,9},{2,10},{3,11},{4,12},{5,13},{6,14},{7,15},{8,0},{9,1},... | collective-permute-start | bytes 1769480 | tf_op jit(solution)/shard_map/ppermute | solution.py:92
  63.4 32.7 %collective-permute-start.7 = (bf16[256,1152]{1,0:T(8,128)(2,1)S(1)}, bf16[256,1152]{1,0:T(8,128)(2,1)}, u32[]{:S(2)}, u32[]{:S(2)}) collective-permute-start(bf16[256,1152]{1,0:T(8,128)(2,1)S(1)} %bitcast.69), channel_id=1, source_target_pairs={{0,384},{1,385},{2,386},{3,387},{4,388},{5,389},{6,390},{7,391},{8... | collective-permute-start | bytes 1769480 | tf_op jit(solution)/shard_map/ppermute | solution.py:92
  66.8 29.4 %collective-permute-start.6 = (bf16[256,1152]{1,0:T(8,128)(2,1)S(1)}, bf16[256,1152]{1,0:T(8,128)(2,1)}, u32[]{:S(2)}, u32[]{:S(2)}) collective-permute-start(bf16[256,1152]{1,0:T(8,128)(2,1)S(1)} %bitcast.70), channel_id=1, source_target_pairs={{0,128},{1,129},{2,130},{3,131},{4,132},{5,133},{6,134},{7,135},{8... | collective-permute-start | bytes 1769480 | tf_op jit(solution)/shard_map/ppermute | solution.py:92
  76.9 10.9 %all-to-all-start.2 = ((bf16[4,128,512]{2,1,0:T(8,128)(2,1)}), bf16[4,128,512]{2,1,0:T(8,128)(2,1)S(1)}, u32[]{:S(2)}, u32[]{:S(2)}) async-start(bf16[4,128,512]{2,1,0:T(8,128)(2,1)} %shard_map.127), calls=%async_computation.2 | async-start | bytes 1048576 | tf_op jit(solution)/shard_map/all_to_all | solution.py:96
  80.4 17.1 %collective-permute-start.9 = (bf16[256,1152]{1,0:T(8,128)(2,1)}, bf16[256,1152]{1,0:T(8,128)(2,1)S(1)}, u32[]{:S(2)}, u32[]{:S(2)}) collective-permute-start(bf16[256,1152]{1,0:T(8,128)(2,1)} %collective-permute-done.8.refs_1_), channel_id=1, source_target_pairs={{0,384},{1,385},{2,386},{3,387},{4,388},{5,389},{6,390},{7,391},{8... | collective-permute-start | bytes 1769480 | tf_op jit(solution)/shard_map/ppermute | solution.py:92
  88.0 7.1 %collective-permute-start.5 = (bf16[128,768]{1,0:T(8,128)(2,1)S(1)}, bf16[128,768]{1,0:T(8,128)(2,1)S(1)}, u32[]{:S(2)}, u32[]{:S(2)}) collective-permute-start(bf16[128,768]{1,0:T(8,128)(2,1)S(1)} %convert_dynamic-update-slice_fusion), channel_id=1, source_target_pairs={{0,1},{1,0},{2,3},{3,2},{4,5},{5,4},{6,7},{7,6},{8,9},{9,8},{10,11... | collective-permute-start | bytes 589832 | tf_op jit(solution)/shard_map/ppermute | solution.py:92
  95.2 20.4 %copy-start.1 = (f32[128,128]{1,0:T(8,128)S(1)}, f32[128,128]{1,0:T(8,128)}, u32[]{:S(2)}) copy-start(f32[128,128]{1,0:T(8,128)} %get-tuple-element.34.cosine_ref) | copy-start | bytes 196612
  95.2 20.4 %copy-start.2 = (f32[128,128]{1,0:T(8,128)S(1)}, f32[128,128]{1,0:T(8,128)}, u32[]{:S(2)}) copy-start(f32[128,128]{1,0:T(8,128)} %get-tuple-element.35.sine_ref) | copy-start | bytes 196612
  95.2 20.4 %copy-start.3 = (bf16[1,512,128]{2,1,0:T(8,128)(2,1)S(1)}, bf16[1,512,128]{2,1,0:T(8,128)(2,1)}, u32[]{:S(2)}) copy-start(bf16[1,512,128]{2,1,0:T(8,128)(2,1)} %param.22) | copy-start | bytes 393220
  95.2 20.4 %copy-start.4 = (bf16[1,512,128]{2,1,0:T(8,128)(2,1)S(1)}, bf16[1,512,128]{2,1,0:T(8,128)(2,1)}, u32[]{:S(2)}) copy-start(bf16[1,512,128]{2,1,0:T(8,128)(2,1)} %param.23) | copy-start | bytes 393220
  95.2 20.4 %copy-start.5 = (bf16[128,64]{0,1:T(8,128)(2,1)S(1)}, bf16[128,64]{0,1:T(8,128)(2,1)}, u32[]{:S(2)}) copy-start(bf16[128,64]{0,1:T(8,128)(2,1)} %param.20) | copy-start | bytes 49156
  97.5 18.0 %all-to-all-start.3 = ((bf16[4,136,384]{2,1,0:T(8,128)(2,1)}), bf16[4,136,384]{2,1,0:T(8,128)(2,1)S(1)}, u32[]{:S(2)}, u32[]{:S(2)}) async-start(bf16[4,136,384]{2,1,0:T(8,128)(2,1)} %pad_maximum_fusion), calls=%async_computation.3 | async-start | bytes 835584 | tf_op jit(solution)/shard_map/all_to_all | solution.py:96
  103.9 33.3 %collective-permute-start.12 = (bf16[256,1152]{1,0:T(8,128)(2,1)}, bf16[256,1152]{1,0:T(8,128)(2,1)S(1)}, u32[]{:S(2)}, u32[]{:S(2)}) collective-permute-start(bf16[256,1152]{1,0:T(8,128)(2,1)} %collective-permute-done.8.refs_1_), channel_id=1, source_target_pairs={{0,128},{1,129},{2,130},{3,131},{4,132},{5,133},{6,134},{7,135},{8... | collective-permute-start | bytes 1769480 | tf_op jit(solution)/shard_map/ppermute | solution.py:92
  109.6 27.6 %collective-permute-start.11 = (bf16[256,1152]{1,0:T(8,128)(2,1)S(1)}, bf16[256,1152]{1,0:T(8,128)(2,1)S(1)}, u32[]{:S(2)}, u32[]{:S(2)}) collective-permute-start(bf16[256,1152]{1,0:T(8,128)(2,1)S(1)} %collective-permute-done.9.refs_3_), channel_id=1, source_target_pairs={{0,384},{1,385},{2,386},{3,387},{4,388},{5,389},{6,390},{7,391},{8... | collective-permute-start | bytes 1769480 | tf_op jit(solution)/shard_map/ppermute | solution.py:92
  111.6 25.6 %collective-permute-start.10 = (bf16[256,1152]{1,0:T(8,128)(2,1)}, bf16[256,1152]{1,0:T(8,128)(2,1)}, u32[]{:S(2)}, u32[]{:S(2)}) collective-permute-start(bf16[256,1152]{1,0:T(8,128)(2,1)} %collective-permute-done.6.refs_6_), channel_id=1, source_target_pairs={{0,128},{1,129},{2,130},{3,131},{4,132},{5,133},{6,134},{7,135},{8... | collective-permute-start | bytes 1769480 | tf_op jit(solution)/shard_map/ppermute | solution.py:92

commit v7 on v6

--- a/solution.py
+++ b/solution.py
@@ -118,16 +118,17 @@
         [weight_ref[:, i : i + 32].reshape(512, 128) for i in (256, 288)], axis=1
     )
     some = pl.ds(pl.multiple_of(engine * 512, 512), 512)
-    for ref, step, start in zip(token_refs, (0, 1, 2, 2, 3), (0, 0, 0, 64, 0), strict=True):
-        rows = ref.shape[0]
-        terms = jnp.concatenate(
-            [
-                jnp.dot(ref[...], query_weight, preferred_element_type=jnp.float32),
-                jnp.dot(ref[:, some], kv_weight, preferred_element_type=jnp.float32),
-            ],
-            axis=1,
-        )
-        out_ref[lax.rem(engine + step, 4), start : start + rows] = terms.astype(jnp.bfloat16)
+    tokens = jnp.concatenate([ref[...] for ref in token_refs], axis=0)
+    some_tokens = jnp.concatenate([ref[:, some] for ref in token_refs], axis=0)
+    terms = jnp.concatenate(
+        [
+            jnp.dot(tokens, query_weight, preferred_element_type=jnp.float32),
+            jnp.dot(some_tokens, kv_weight, preferred_element_type=jnp.float32),
+        ],
+        axis=1,
+    ).astype(jnp.bfloat16)
+    for step in range(4):
+        out_ref[lax.rem(engine + step, 4)] = terms[step * 128 : step * 128 + 128]
 
 
 def project_kernel(place_ref, heads_ref, *refs):

time: 142 us -> 142 us (level)
  transfers between devices with their start and end apart: 17 -> 17, of which waited for: 6 -> 6; matrix products, arithmetic and copies ran while one was open for 5% -> 5% of each run, Pallas kernels for 3% -> 2%
where the time goes in v7:
time: 142 us; the launch traced here: 141 us
  starting transfers between devices  78.5 us (55%)
  blocking collectives  24.8 us (17%)
  waiting for transfers between devices  17.9 us (13%)
  Pallas kernels  7.46 us (5%)
  other arithmetic  5.24 us (4%)
  local copies, waits for them, and re-layouts  4.87 us (3%)
    ppermute x13, starting transfers between devices, move(): return lax.ppermute(array, AXES, pairs)  49.9 us
    all_to_all x4, starting transfers between devices, exchange(): lax.all_to_all(array, axis, split_axis=0, concat_axis=0, tiled=True, axis...  28.5 us
    all_gather x1, blocking collectives, per_device(): heads = lax.all_gather(heads[None], 'tensor', axis=0, tiled=True)  20.8 us
    ppermute x13, waiting for transfers between devices, move(): return lax.ppermute(array, AXES, pairs)  9.72 us
    all_to_all x4, waiting for transfers between devices, exchange(): lax.all_to_all(array, axis, split_axis=0, concat_axis=0, tiled=True, axis...  8.23 us
    pallas_call x3, Pallas kernels, compute(): pl.pallas_call(kernel, out_shape=jax.ShapeDtypeStruct(shape, jnp.bfloat16...  7.46 us
    all_gather x1, blocking collectives, per_device(): lax.all_gather(squares, 'tensor', axis=0, tiled=True, axis_index_groups=C...  3.97 us
  transfers between devices with their start and end apart: 17, of which 6 were waited for; matrix products, arithmetic and copies ran while one was open for 5% of the time, Pallas kernels for 2%

profile of v7, /device:TPU:1, one launch (start us, length us, event | category | flops | bytes accessed | tf_op | source)
XLA Modules:
  0.0 141.0 jit_solution(7367141166696603382)
XLA Ops:
  0.0 1.0 concatenate.46
  1.0 1.1 fusion.1
  2.9 10.9 %all-to-all-start = ((bf16[8,32,1152]{2,1,0:T(8,128)(2,1)}), bf16[8,32,1152]{2,1,0:T(8,128)(2,1)S(1)}, u32[]{:S(2)}, u32[]{:S(2)}) async-start(bf16[8,32,1152]{2,1,0:T(8,128)(2,1)} %broadcast_in_dim.18), calls=%async_computation | async-start | bytes 1179648 | tf_op jit(solution)/shard_map/all_to_all | solution.py:96
  13.9 4.4 %collective-permute-start.2 = (bf16[128,2048]{1,0:T(8,128)(2,1)S(1)}, bf16[128,2048]{1,0:T(8,128)(2,1)S(1)}, u32[]{:S(2)}, u32[]{:S(2)}) collective-permute-start(bf16[128,2048]{1,0:T(8,128)(2,1)S(1)} %multiply_convert_fusion.refs_0_), channel_id=1, source_target_pairs={{0,384},{1,385},{2,386},{3,387},{4,388},{5,389},{6,390},{7,391},{8... | collective-permute-start | bytes 1572872 | tf_op jit(solution)/shard_map/ppermute | solution.py:92
  18.3 1.9 %collective-permute-start.1 = (bf16[128,2048]{1,0:T(8,128)(2,1)S(1)}, bf16[128,2048]{1,0:T(8,128)(2,1)S(1)}, u32[]{:S(2)}, u32[]{:S(2)}) collective-permute-start(bf16[128,2048]{1,0:T(8,128)(2,1)S(1)} %multiply_convert_fusion.refs_0_), channel_id=1, source_target_pairs={{0,128},{1,129},{2,130},{3,131},{4,132},{5,133},{6,134},{7,135},{8... | collective-permute-start | bytes 1572872 | tf_op jit(solution)/shard_map/ppermute | solution.py:92
  20.3 6.0 %collective-permute-start = (bf16[256,128]{1,0:T(8,128)(2,1)S(1)}, bf16[256,128]{1,0:T(8,128)(2,1)S(1)}, u32[]{:S(2)}, u32[]{:S(2)}) collective-permute-start(bf16[256,128]{1,0:T(8,128)(2,1)S(1)} %fusion.1), channel_id=1, source_target_pairs={{0,0},{1,112},{2,128},{3,240},{4,256},{5,368},{6,384},{7,496},{8,8... | collective-permute-start | bytes 196616 | tf_op jit(solution)/shard_map/ppermute | solution.py:92
  26.3 4.2 %collective-permute-done = bf16[256,128]{1,0:T(8,128)(2,1)S(1)} collective-permute-done((bf16[256,128]{1,0:T(8,128)(2,1)S(1)}, bf16[256,128]{1,0:T(8,128)(2,1)S(1)}, u32[]{:S(2)}, u32[]{:S(2)}) %collective-permute-start) | collective-permute-done | bytes 65568 | tf_op jit(solution)/shard_map/ppermute | solution.py:92
  30.5 3.2 %collective-permute-done.1.refs_4_ = bf16[128,2048]{1,0:T(8,128)(2,1)S(1)} collective-permute-done((bf16[128,2048]{1,0:T(8,128)(2,1)S(1)}, bf16[128,2048]{1,0:T(8,128)(2,1)S(1)}, u32[]{:S(2)}, u32[]{:S(2)}) %collective-permute-start.1) | collective-permute-done | bytes 524320 | tf_op jit(solution)/shard_map/ppermute | solution.py:92
  33.6 1.3 broadcast_in_dim.17
  35.0 7.8 %all-to-all-start.1 = ((bf16[16,320,128]{2,1,0:T(8,128)(2,1)}), bf16[16,320,128]{2,1,0:T(8,128)(2,1)S(1)}, u32[]{:S(2)}, u32[]{:S(2)}) async-start(bf16[16,320,128]{2,1,0:T(8,128)(2,1)} %broadcast_in_dim.17), calls=%async_computation.1 | async-start | bytes 2621440 | tf_op jit(solution)/shard_map/all_to_all | solution.py:96
  42.8 1.2 multiply_reduce_fusion
  44.0 4.0 %all-gather.2 = f32[2,1,128]{2,1,0:T(1,128)S(1)} all-gather(f32[1,1,128]{2,1,0:T(1,128)S(1)} %bitcast.79), channel_id=2, replica_groups={{0,1},{2,3},{4,5},{6,7},{8,9},{10,11},{12,13},{14,15},{16,17},{18,19},{..., dimensions={0}, use_global_device_ids=true | all-gather | bytes 1536 | tf_op jit(solution)/shard_map/all_gather | solution.py:210
  49.5 3.5 %collective-permute-start.3 = (bf16[64,2048]{1,0:T(8,128)(2,1)}, bf16[64,2048]{1,0:T(8,128)(2,1)}, u32[]{:S(2)}, u32[]{:S(2)}) collective-permute-start(bf16[64,2048]{1,0:T(8,128)(2,1)} %slice.65), channel_id=1, source_target_pairs={{0,128},{1,129},{2,130},{3,131},{4,132},{5,133},{6,134},{7,135},{8... | collective-permute-start | bytes 786440 | tf_op jit(solution)/shard_map/ppermute | solution.py:92
  53.0 4.1 %collective-permute-start.4 = (bf16[64,2048]{1,0:T(8,128)(2,1)}, bf16[64,2048]{1,0:T(8,128)(2,1)}, u32[]{:S(2)}, u32[]{:S(2)}) collective-permute-start(bf16[64,2048]{1,0:T(8,128)(2,1)} %slice.66), channel_id=1, source_target_pairs={{0,384},{1,385},{2,386},{3,387},{4,388},{5,389},{6,390},{7,391},{8... | collective-permute-start | bytes 786440 | tf_op jit(solution)/shard_map/ppermute | solution.py:92
  57.1 1.0 fusion.14
  58.1 1.7 %pad_maximum_fusion.9 = (f32[128,128]{1,0:T(8,128)}, f32[128,128]{1,0:T(8,128)}) fusion(f32[128,64]{1,0:T(8,128)} %get-tuple-element.50, f32[128,64]{1,0:T(8,128)} %get-tuple-element.49, f32[128,64]{1,0:T(8,128)} %get-tuple-element.48), kind=kLoop, calls=%fused_computation.30 | loop fusion | flops 32768 | bytes 229376 | tf_op jit(solution)/shard_map/concatenate | solution.py:16
  59.8 3.5 %collective-permute-start.8 = (bf16[256,1152]{1,0:T(8,128)(2,1)S(1)}, bf16[256,1152]{1,0:T(8,128)(2,1)}, u32[]{:S(2)}, u32[]{:S(2)}) collective-permute-start(bf16[256,1152]{1,0:T(8,128)(2,1)S(1)} %bitcast.68), channel_id=1, source_target_pairs={{0,8},{1,9},{2,10},{3,11},{4,12},{5,13},{6,14},{7,15},{8,0},{9,1},... | collective-permute-start | bytes 1769480 | tf_op jit(solution)/shard_map/ppermute | solution.py:92
  63.4 3.4 %collective-permute-start.7 = (bf16[256,1152]{1,0:T(8,128)(2,1)S(1)}, bf16[256,1152]{1,0:T(8,128)(2,1)}, u32[]{:S(2)}, u32[]{:S(2)}) collective-permute-start(bf16[256,1152]{1,0:T(8,128)(2,1)S(1)} %bitcast.69), channel_id=1, source_target_pairs={{0,384},{1,385},{2,386},{3,387},{4,388},{5,389},{6,390},{7,391},{8... | collective-permute-start | bytes 1769480 | tf_op jit(solution)/shard_map/ppermute | solution.py:92
  66.8 1.9 %collective-permute-start.6 = (bf16[256,1152]{1,0:T(8,128)(2,1)S(1)}, bf16[256,1152]{1,0:T(8,128)(2,1)}, u32[]{:S(2)}, u32[]{:S(2)}) collective-permute-start(bf16[256,1152]{1,0:T(8,128)(2,1)S(1)} %bitcast.70), channel_id=1, source_target_pairs={{0,128},{1,129},{2,130},{3,131},{4,132},{5,133},{6,134},{7,135},{8... | collective-permute-start | bytes 1769480 | tf_op jit(solution)/shard_map/ppermute | solution.py:92
  68.7 5.2 %all-to-all-done.1.weight_ref = bf16[16,320,128]{2,1,0:T(8,128)(2,1)S(1)} async-done(((bf16[16,320,128]{2,1,0:T(8,128)(2,1)}), bf16[16,320,128]{2,1,0:T(8,128)(2,1)S(1)}, u32[]{:S(2)}, u32[]{:S(2)}) %all-to-all-start.1) | async-done | bytes 1310752 | tf_op jit(solution)/shard_map/all_to_all | solution.py:96
  73.9 2.7 %shard_map.127 = bf16[4,128,512]{2,1,0:T(8,128)(2,1)} custom-call(s32[3]{0:T(128)S(1)} %pad_add_fusion.place_ref, bf16[16,320,128]{2,1,0:T(8,128)(2,1)S(1)} %all-to-all-done.1.weight_ref, bf16[128,2048]{1,0:T(8,128)(2,1)S(1)} %multiply_convert_fusion.refs_0_, bf16[128,2048]{1,0:T(8,128)(2,1)S(1)} %collective-permute-done.2.refs_1_, ...), custom_call_target="tpu_custom_call" | custom-call | tf_op jit(solution)/shard_map/pallas_call | solution.py:156
  76.6 3.5 %all-to-all-start.2 = ((bf16[4,128,512]{2,1,0:T(8,128)(2,1)}), bf16[4,128,512]{2,1,0:T(8,128)(2,1)S(1)}, u32[]{:S(2)}, u32[]{:S(2)}) async-start(bf16[4,128,512]{2,1,0:T(8,128)(2,1)} %shard_map.127), calls=%async_computation.2 | async-start | bytes 1048576 | tf_op jit(solution)/shard_map/all_to_all | solution.py:96
  80.1 4.5 %collective-permute-start.9 = (bf16[256,1152]{1,0:T(8,128)(2,1)}, bf16[256,1152]{1,0:T(8,128)(2,1)S(1)}, u32[]{:S(2)}, u32[]{:S(2)}) collective-permute-start(bf16[256,1152]{1,0:T(8,128)(2,1)} %collective-permute-done.8.refs_1_), channel_id=1, source_target_pairs={{0,384},{1,385},{2,386},{3,387},{4,388},{5,389},{6,390},{7,391},{8... | collective-permute-start | bytes 1769480 | tf_op jit(solution)/shard_map/ppermute | solution.py:92
  84.7 3.1 %all-to-all-done.2 = bf16[4,128,512]{2,1,0:T(8,128)(2,1)S(1)} async-done(((bf16[4,128,512]{2,1,0:T(8,128)(2,1)}), bf16[4,128,512]{2,1,0:T(8,128)(2,1)S(1)}, u32[]{:S(2)}, u32[]{:S(2)}) %all-to-all-start.2) | async-done | bytes 524320 | tf_op jit(solution)/shard_map/all_to_all | solution.py:96
  88.0 5.7 %collective-permute-start.5 = (bf16[128,768]{1,0:T(8,128)(2,1)S(1)}, bf16[128,768]{1,0:T(8,128)(2,1)S(1)}, u32[]{:S(2)}, u32[]{:S(2)}) collective-permute-start(bf16[128,768]{1,0:T(8,128)(2,1)S(1)} %convert_dynamic-update-slice_fusion), channel_id=1, source_target_pairs={{0,1},{1,0},{2,3},{3,2},{4,5},{5,4},{6,7},{7,6},{8,9},{9,8},{10,11... | collective-permute-start | bytes 589832 | tf_op jit(solution)/shard_map/ppermute | solution.py:92
  95.8 1.4 collective-permute-done.9.refs_3_
  97.2 6.4 %all-to-all-start.3 = ((bf16[4,136,384]{2,1,0:T(8,128)(2,1)}), bf16[4,136,384]{2,1,0:T(8,128)(2,1)S(1)}, u32[]{:S(2)}, u32[]{:S(2)}) async-start(bf16[4,136,384]{2,1,0:T(8,128)(2,1)} %pad_maximum_fusion), calls=%async_computation.3 | async-start | bytes 835584 | tf_op jit(solution)/shard_map/all_to_all | solution.py:96
  103.6 5.7 %collective-permute-start.12 = (bf16[256,1152]{1,0:T(8,128)(2,1)}, bf16[256,1152]{1,0:T(8,128)(2,1)S(1)}, u32[]{:S(2)}, u32[]{:S(2)}) collective-permute-start(bf16[256,1152]{1,0:T(8,128)(2,1)} %collective-permute-done.8.refs_1_), channel_id=1, source_target_pairs={{0,128},{1,129},{2,130},{3,131},{4,132},{5,133},{6,134},{7,135},{8... | collective-permute-start | bytes 1769480 | tf_op jit(solution)/shard_map/ppermute | solution.py:92
  109.3 1.9 %collective-permute-start.11 = (bf16[256,1152]{1,0:T(8,128)(2,1)S(1)}, bf16[256,1152]{1,0:T(8,128)(2,1)S(1)}, u32[]{:S(2)}, u32[]{:S(2)}) collective-permute-start(bf16[256,1152]{1,0:T(8,128)(2,1)S(1)} %collective-permute-done.9.refs_3_), channel_id=1, source_target_pairs={{0,384},{1,385},{2,386},{3,387},{4,388},{5,389},{6,390},{7,391},{8... | collective-permute-start | bytes 1769480 | tf_op jit(solution)/shard_map/ppermute | solution.py:92
  111.3 3.4 %collective-permute-start.10 = (bf16[256,1152]{1,0:T(8,128)(2,1)}, bf16[256,1152]{1,0:T(8,128)(2,1)}, u32[]{:S(2)}, u32[]{:S(2)}) collective-permute-start(bf16[256,1152]{1,0:T(8,128)(2,1)} %collective-permute-done.6.refs_6_), channel_id=1, source_target_pairs={{0,128},{1,129},{2,130},{3,131},{4,132},{5,133},{6,134},{7,135},{8... | collective-permute-start | bytes 1769480 | tf_op jit(solution)/shard_map/ppermute | solution.py:92
  116.1 20.8 %all-gather.1 = bf16[1536,128]{1,0:T(8,128)(2,1)S(1)} all-gather(bf16[192,128]{1,0:T(8,128)(2,1)S(1)} %shard_map.128), channel_id=3, replica_groups=mesh['engine'=4,'fsdp'=16,'tensor'=8] {'tensor'}, dimensions={0}, use_global_device_ids=true | all-gather | bytes 442368 | tf_op jit(solution)/shard_map/all_gather | solution.py:252
  136.9 4.1 %shard_map.129 = bf16[128,2048]{1,0:T(8,128)(2,1)} custom-call(s32[3]{0:T(128)S(1)} %pad_add_fusion.place_ref, bf16[8,192,128]{2,1,0:T(8,128)(2,1)S(1)} %bitcast.72, bf16[256,1152]{1,0:T(8,128)(2,1)S(1)} %bitcast.71, bf16[256,1152]{1,0:T(8,128)(2,1)} %collective-permute-done.8.refs_1_, bf16[256,1152]{1,0:T(8,128)(2,1)} %collective-permute-done.7.refs_2_, ...), custom_call_target="tpu_custom_call" | custom-call | tf_op jit(solution)/shard_map/pallas_call | solution.py:156
  (69 shorter events, 5.6 us)
Async XLA Ops:
  0.0 1.0 copy-start
  0.0 13.8 %copy-start.8 = (bf16[2048]{0:T(1024)(128)(2,1)S(1)}, bf16[2048]{0:T(1024)(128)(2,1)}, u32[]{:S(2)}) copy-start(bf16[2048]{0:T(1024)(128)(2,1)} %param.14) | copy-start | bytes 12292
  0.0 13.8 %copy-start.6 = (bf16[128,2048]{1,0:T(8,128)(2,1)S(1)}, bf16[128,2048]{1,0:T(8,128)(2,1)}, u32[]{:S(2)}) copy-start(bf16[128,2048]{1,0:T(8,128)(2,1)} %param.13) | copy-start | bytes 1572868
  2.1 24.2 %copy-start.7 = (bf16[1,32,256]{2,1,0:T(8,128)(2,1)S(1)}, bf16[1,32,256]{2,1,0:T(8,128)(2,1)}, u32[]{:S(2)}) copy-start(bf16[1,32,256]{2,1,0:T(8,128)(2,1)} %param.18) | copy-start | bytes 49156
  2.9 30.7 %all-to-all-start = ((bf16[8,32,1152]{2,1,0:T(8,128)(2,1)}), bf16[8,32,1152]{2,1,0:T(8,128)(2,1)S(1)}, u32[]{:S(2)}, u32[]{:S(2)}) async-start(bf16[8,32,1152]{2,1,0:T(8,128)(2,1)} %broadcast_in_dim.18), calls=%async_computation | async-start | bytes 1179648 | tf_op jit(solution)/shard_map/all_to_all | solution.py:96
  13.9 16.5 %collective-permute-start.2 = (bf16[128,2048]{1,0:T(8,128)(2,1)S(1)}, bf16[128,2048]{1,0:T(8,128)(2,1)S(1)}, u32[]{:S(2)}, u32[]{:S(2)}) collective-permute-start(bf16[128,2048]{1,0:T(8,128)(2,1)S(1)} %multiply_convert_fusion.refs_0_), channel_id=1, source_target_pairs={{0,384},{1,385},{2,386},{3,387},{4,388},{5,389},{6,390},{7,391},{8... | collective-permute-start | bytes 1572872 | tf_op jit(solution)/shard_map/ppermute | solution.py:92
  18.3 15.3 %collective-permute-start.1 = (bf16[128,2048]{1,0:T(8,128)(2,1)S(1)}, bf16[128,2048]{1,0:T(8,128)(2,1)S(1)}, u32[]{:S(2)}, u32[]{:S(2)}) collective-permute-start(bf16[128,2048]{1,0:T(8,128)(2,1)S(1)} %multiply_convert_fusion.refs_0_), channel_id=1, source_target_pairs={{0,128},{1,129},{2,130},{3,131},{4,132},{5,133},{6,134},{7,135},{8... | collective-permute-start | bytes 1572872 | tf_op jit(solution)/shard_map/ppermute | solution.py:92
  20.3 10.2 %collective-permute-start = (bf16[256,128]{1,0:T(8,128)(2,1)S(1)}, bf16[256,128]{1,0:T(8,128)(2,1)S(1)}, u32[]{:S(2)}, u32[]{:S(2)}) collective-permute-start(bf16[256,128]{1,0:T(8,128)(2,1)S(1)} %fusion.1), channel_id=1, source_target_pairs={{0,0},{1,112},{2,128},{3,240},{4,256},{5,368},{6,384},{7,496},{8,8... | collective-permute-start | bytes 196616 | tf_op jit(solution)/shard_map/ppermute | solution.py:92
  35.0 7.8 %copy-start.9 = (s32[1,128]{1,0:T(1,128)S(1)}, s32[1,128]{1,0:T(1,128)}, u32[]{:S(2)}) copy-start(s32[1,128]{1,0:T(1,128)} %param.24) | copy-start | bytes 1540
  35.0 38.9 %all-to-all-start.1 = ((bf16[16,320,128]{2,1,0:T(8,128)(2,1)}), bf16[16,320,128]{2,1,0:T(8,128)(2,1)S(1)}, u32[]{:S(2)}, u32[]{:S(2)}) async-start(bf16[16,320,128]{2,1,0:T(8,128)(2,1)} %broadcast_in_dim.17), calls=%async_computation.1 | async-start | bytes 2621440 | tf_op jit(solution)/shard_map/all_to_all | solution.py:96
  49.5 19.2 %collective-permute-start.3 = (bf16[64,2048]{1,0:T(8,128)(2,1)}, bf16[64,2048]{1,0:T(8,128)(2,1)}, u32[]{:S(2)}, u32[]{:S(2)}) collective-permute-start(bf16[64,2048]{1,0:T(8,128)(2,1)} %slice.65), channel_id=1, source_target_pairs={{0,128},{1,129},{2,130},{3,131},{4,132},{5,133},{6,134},{7,135},{8... | collective-permute-start | bytes 786440 | tf_op jit(solution)/shard_map/ppermute | solution.py:92
  53.0 15.7 %collective-permute-start.4 = (bf16[64,2048]{1,0:T(8,128)(2,1)}, bf16[64,2048]{1,0:T(8,128)(2,1)}, u32[]{:S(2)}, u32[]{:S(2)}) collective-permute-start(bf16[64,2048]{1,0:T(8,128)(2,1)} %slice.66), channel_id=1, source_target_pairs={{0,384},{1,385},{2,386},{3,387},{4,388},{5,389},{6,390},{7,391},{8... | collective-permute-start | bytes 786440 | tf_op jit(solution)/shard_map/ppermute | solution.py:92
  59.8 20.4 %collective-permute-start.8 = (bf16[256,1152]{1,0:T(8,128)(2,1)S(1)}, bf16[256,1152]{1,0:T(8,128)(2,1)}, u32[]{:S(2)}, u32[]{:S(2)}) collective-permute-start(bf16[256,1152]{1,0:T(8,128)(2,1)S(1)} %bitcast.68), channel_id=1, source_target_pairs={{0,8},{1,9},{2,10},{3,11},{4,12},{5,13},{6,14},{7,15},{8,0},{9,1},... | collective-permute-start | bytes 1769480 | tf_op jit(solution)/shard_map/ppermute | solution.py:92
  63.4 32.4 %collective-permute-start.7 = (bf16[256,1152]{1,0:T(8,128)(2,1)S(1)}, bf16[256,1152]{1,0:T(8,128)(2,1)}, u32[]{:S(2)}, u32[]{:S(2)}) collective-permute-start(bf16[256,1152]{1,0:T(8,128)(2,1)S(1)} %bitcast.69), channel_id=1, source_target_pairs={{0,384},{1,385},{2,386},{3,387},{4,388},{5,389},{6,390},{7,391},{8... | collective-permute-start | bytes 1769480 | tf_op jit(solution)/shard_map/ppermute | solution.py:92
  66.8 29.1 %collective-permute-start.6 = (bf16[256,1152]{1,0:T(8,128)(2,1)S(1)}, bf16[256,1152]{1,0:T(8,128)(2,1)}, u32[]{:S(2)}, u32[]{:S(2)}) collective-permute-start(bf16[256,1152]{1,0:T(8,128)(2,1)S(1)} %bitcast.70), channel_id=1, source_target_pairs={{0,128},{1,129},{2,130},{3,131},{4,132},{5,133},{6,134},{7,135},{8... | collective-permute-start | bytes 1769480 | tf_op jit(solution)/shard_map/ppermute | solution.py:92
  76.6 11.2 %all-to-all-start.2 = ((bf16[4,128,512]{2,1,0:T(8,128)(2,1)}), bf16[4,128,512]{2,1,0:T(8,128)(2,1)S(1)}, u32[]{:S(2)}, u32[]{:S(2)}) async-start(bf16[4,128,512]{2,1,0:T(8,128)(2,1)} %shard_map.127), calls=%async_computation.2 | async-start | bytes 1048576 | tf_op jit(solution)/shard_map/all_to_all | solution.py:96
  80.1 17.1 %collective-permute-start.9 = (bf16[256,1152]{1,0:T(8,128)(2,1)}, bf16[256,1152]{1,0:T(8,128)(2,1)S(1)}, u32[]{:S(2)}, u32[]{:S(2)}) collective-permute-start(bf16[256,1152]{1,0:T(8,128)(2,1)} %collective-permute-done.8.refs_1_), channel_id=1, source_target_pairs={{0,384},{1,385},{2,386},{3,387},{4,388},{5,389},{6,390},{7,391},{8... | collective-permute-start | bytes 1769480 | tf_op jit(solution)/shard_map/ppermute | solution.py:92
  88.0 6.8 %collective-permute-start.5 = (bf16[128,768]{1,0:T(8,128)(2,1)S(1)}, bf16[128,768]{1,0:T(8,128)(2,1)S(1)}, u32[]{:S(2)}, u32[]{:S(2)}) collective-permute-start(bf16[128,768]{1,0:T(8,128)(2,1)S(1)} %convert_dynamic-update-slice_fusion), channel_id=1, source_target_pairs={{0,1},{1,0},{2,3},{3,2},{4,5},{5,4},{6,7},{7,6},{8,9},{9,8},{10,11... | collective-permute-start | bytes 589832 | tf_op jit(solution)/shard_map/ppermute | solution.py:92
  94.9 20.4 %copy-start.1 = (f32[128,128]{1,0:T(8,128)S(1)}, f32[128,128]{1,0:T(8,128)}, u32[]{:S(2)}) copy-start(f32[128,128]{1,0:T(8,128)} %get-tuple-element.34.cosine_ref) | copy-start | bytes 196612
  94.9 20.4 %copy-start.2 = (f32[128,128]{1,0:T(8,128)S(1)}, f32[128,128]{1,0:T(8,128)}, u32[]{:S(2)}) copy-start(f32[128,128]{1,0:T(8,128)} %get-tuple-element.35.sine_ref) | copy-start | bytes 196612
  94.9 20.4 %copy-start.3 = (bf16[1,512,128]{2,1,0:T(8,128)(2,1)S(1)}, bf16[1,512,128]{2,1,0:T(8,128)(2,1)}, u32[]{:S(2)}) copy-start(bf16[1,512,128]{2,1,0:T(8,128)(2,1)} %param.22) | copy-start | bytes 393220
  94.9 20.4 %copy-start.4 = (bf16[1,512,128]{2,1,0:T(8,128)(2,1)S(1)}, bf16[1,512,128]{2,1,0:T(8,128)(2,1)}, u32[]{:S(2)}) copy-start(bf16[1,512,128]{2,1,0:T(8,128)(2,1)} %param.23) | copy-start | bytes 393220
  94.9 20.4 %copy-start.5 = (bf16[128,64]{0,1:T(8,128)(2,1)S(1)}, bf16[128,64]{0,1:T(8,128)(2,1)}, u32[]{:S(2)}) copy-start(bf16[128,64]{0,1:T(8,128)(2,1)} %param.20) | copy-start | bytes 49156
  97.2 18.1 %all-to-all-start.3 = ((bf16[4,136,384]{2,1,0:T(8,128)(2,1)}), bf16[4,136,384]{2,1,0:T(8,128)(2,1)S(1)}, u32[]{:S(2)}, u32[]{:S(2)}) async-start(bf16[4,136,384]{2,1,0:T(8,128)(2,1)} %pad_maximum_fusion), calls=%async_computation.3 | async-start | bytes 835584 | tf_op jit(solution)/shard_map/all_to_all | solution.py:96
  103.6 33.3 %collective-permute-start.12 = (bf16[256,1152]{1,0:T(8,128)(2,1)}, bf16[256,1152]{1,0:T(8,128)(2,1)S(1)}, u32[]{:S(2)}, u32[]{:S(2)}) collective-permute-start(bf16[256,1152]{1,0:T(8,128)(2,1)} %collective-permute-done.8.refs_1_), channel_id=1, source_target_pairs={{0,128},{1,129},{2,130},{3,131},{4,132},{5,133},{6,134},{7,135},{8... | collective-permute-start | bytes 1769480 | tf_op jit(solution)/shard_map/ppermute | solution.py:92
  109.3 27.6 %collective-permute-start.11 = (bf16[256,1152]{1,0:T(8,128)(2,1)S(1)}, bf16[256,1152]{1,0:T(8,128)(2,1)S(1)}, u32[]{:S(2)}, u32[]{:S(2)}) collective-permute-start(bf16[256,1152]{1,0:T(8,128)(2,1)S(1)} %collective-permute-done.9.refs_3_), channel_id=1, source_target_pairs={{0,384},{1,385},{2,386},{3,387},{4,388},{5,389},{6,390},{7,391},{8... | collective-permute-start | bytes 1769480 | tf_op jit(solution)/shard_map/ppermute | solution.py:92
  111.3 25.6 %collective-permute-start.10 = (bf16[256,1152]{1,0:T(8,128)(2,1)}, bf16[256,1152]{1,0:T(8,128)(2,1)}, u32[]{:S(2)}, u32[]{:S(2)}) collective-permute-start(bf16[256,1152]{1,0:T(8,128)(2,1)} %collective-permute-done.6.refs_6_), channel_id=1, source_target_pairs={{0,128},{1,129},{2,130},{3,131},{4,132},{5,133},{6,134},{7,135},{8... | collective-permute-start | bytes 1769480 | tf_op jit(solution)/shard_map/ppermute | solution.py:92

commit v8 on v7

--- a/solution.py
+++ b/solution.py
@@ -145,11 +145,12 @@
             for z in range(8):
                 at = pl.multiple_of(z * 64 + half * 32, 32)
                 weight_ref[step, pl.ds(at, 32)] = ref[z * 32 : z * 32 + 32]
-        out = lax.dot_general(
-            heads, weight_ref[step], inner, preferred_element_type=jnp.float32
-        )
+    out = lax.dot_general(
+        heads, weight_ref[...].reshape(2048, 1152), inner, preferred_element_type=jnp.float32
+    ).astype(jnp.bfloat16)
+    for step in range(4):
         place = pl.multiple_of(lax.rem(engine + step, 4) * 512, 512)
-        out_ref[:, pl.ds(place, 512)] = out.astype(jnp.bfloat16)
+        out_ref[:, pl.ds(place, 512)] = out[:, step * 512 : step * 512 + 512]
 
 
 def compute(kernel, shape, place, arrays, scratch=()):

time: 142 us -> 142 us (level)
  no operation moved by 1% of the time
where the time goes in v8:
time: 142 us; the launch traced here: 141 us
  starting transfers between devices  78.5 us (55%)
  blocking collectives  24.8 us (17%)
  waiting for transfers between devices  17.9 us (13%)
  Pallas kernels  7.8 us (5%)
  other arithmetic  5.24 us (4%)
  local copies, waits for them, and re-layouts  4.87 us (3%)
    ppermute x13, starting transfers between devices, move(): return lax.ppermute(array, AXES, pairs)  49.9 us
    all_to_all x4, starting transfers between devices, exchange(): lax.all_to_all(array, axis, split_axis=0, concat_axis=0, tiled=True, axis...  28.5 us
    all_gather x1, blocking collectives, per_device(): heads = lax.all_gather(heads[None], 'tensor', axis=0, tiled=True)  20.8 us
    ppermute x13, waiting for transfers between devices, move(): return lax.ppermute(array, AXES, pairs)  9.72 us
    all_to_all x4, waiting for transfers between devices, exchange(): lax.all_to_all(array, axis, split_axis=0, concat_axis=0, tiled=True, axis...  8.23 us
    pallas_call x3, Pallas kernels, compute(): pl.pallas_call(kernel, out_shape=jax.ShapeDtypeStruct(shape, jnp.bfloat16...  7.8 us
    all_gather x1, blocking collectives, per_device(): lax.all_gather(squares, 'tensor', axis=0, tiled=True, axis_index_groups=C...  3.97 us
  transfers between devices with their start and end apart: 17, of which 6 were waited for; matrix products, arithmetic and copies ran while one was open for 5% of the time, Pallas kernels for 2%

profile of v8, /device:TPU:1, one launch (start us, length us, event | category | flops | bytes accessed | tf_op | source)
XLA Modules:
  0.0 141.3 jit_solution(11975269146814777394)
XLA Ops:
  0.0 1.0 concatenate.46
  1.0 1.1 fusion.1
  2.9 10.9 %all-to-all-start = ((bf16[8,32,1152]{2,1,0:T(8,128)(2,1)}), bf16[8,32,1152]{2,1,0:T(8,128)(2,1)S(1)}, u32[]{:S(2)}, u32[]{:S(2)}) async-start(bf16[8,32,1152]{2,1,0:T(8,128)(2,1)} %broadcast_in_dim.18), calls=%async_computation | async-start | bytes 1179648 | tf_op jit(solution)/shard_map/all_to_all | solution.py:96
  13.9 4.4 %collective-permute-start.2 = (bf16[128,2048]{1,0:T(8,128)(2,1)S(1)}, bf16[128,2048]{1,0:T(8,128)(2,1)S(1)}, u32[]{:S(2)}, u32[]{:S(2)}) collective-permute-start(bf16[128,2048]{1,0:T(8,128)(2,1)S(1)} %multiply_convert_fusion.refs_0_), channel_id=1, source_target_pairs={{0,384},{1,385},{2,386},{3,387},{4,388},{5,389},{6,390},{7,391},{8... | collective-permute-start | bytes 1572872 | tf_op jit(solution)/shard_map/ppermute | solution.py:92
  18.3 1.9 %collective-permute-start.1 = (bf16[128,2048]{1,0:T(8,128)(2,1)S(1)}, bf16[128,2048]{1,0:T(8,128)(2,1)S(1)}, u32[]{:S(2)}, u32[]{:S(2)}) collective-permute-start(bf16[128,2048]{1,0:T(8,128)(2,1)S(1)} %multiply_convert_fusion.refs_0_), channel_id=1, source_target_pairs={{0,128},{1,129},{2,130},{3,131},{4,132},{5,133},{6,134},{7,135},{8... | collective-permute-start | bytes 1572872 | tf_op jit(solution)/shard_map/ppermute | solution.py:92
  20.3 6.0 %collective-permute-start = (bf16[256,128]{1,0:T(8,128)(2,1)S(1)}, bf16[256,128]{1,0:T(8,128)(2,1)S(1)}, u32[]{:S(2)}, u32[]{:S(2)}) collective-permute-start(bf16[256,128]{1,0:T(8,128)(2,1)S(1)} %fusion.1), channel_id=1, source_target_pairs={{0,0},{1,112},{2,128},{3,240},{4,256},{5,368},{6,384},{7,496},{8,8... | collective-permute-start | bytes 196616 | tf_op jit(solution)/shard_map/ppermute | solution.py:92
  26.3 4.2 %collective-permute-done = bf16[256,128]{1,0:T(8,128)(2,1)S(1)} collective-permute-done((bf16[256,128]{1,0:T(8,128)(2,1)S(1)}, bf16[256,128]{1,0:T(8,128)(2,1)S(1)}, u32[]{:S(2)}, u32[]{:S(2)}) %collective-permute-start) | collective-permute-done | bytes 65568 | tf_op jit(solution)/shard_map/ppermute | solution.py:92
  30.5 3.2 %collective-permute-done.1.refs_4_ = bf16[128,2048]{1,0:T(8,128)(2,1)S(1)} collective-permute-done((bf16[128,2048]{1,0:T(8,128)(2,1)S(1)}, bf16[128,2048]{1,0:T(8,128)(2,1)S(1)}, u32[]{:S(2)}, u32[]{:S(2)}) %collective-permute-start.1) | collective-permute-done | bytes 524320 | tf_op jit(solution)/shard_map/ppermute | solution.py:92
  33.6 1.3 broadcast_in_dim.17
  35.0 7.8 %all-to-all-start.1 = ((bf16[16,320,128]{2,1,0:T(8,128)(2,1)}), bf16[16,320,128]{2,1,0:T(8,128)(2,1)S(1)}, u32[]{:S(2)}, u32[]{:S(2)}) async-start(bf16[16,320,128]{2,1,0:T(8,128)(2,1)} %broadcast_in_dim.17), calls=%async_computation.1 | async-start | bytes 2621440 | tf_op jit(solution)/shard_map/all_to_all | solution.py:96
  42.8 1.2 multiply_reduce_fusion
  44.0 4.0 %all-gather.2 = f32[2,1,128]{2,1,0:T(1,128)S(1)} all-gather(f32[1,1,128]{2,1,0:T(1,128)S(1)} %bitcast.79), channel_id=2, replica_groups={{0,1},{2,3},{4,5},{6,7},{8,9},{10,11},{12,13},{14,15},{16,17},{18,19},{..., dimensions={0}, use_global_device_ids=true | all-gather | bytes 1536 | tf_op jit(solution)/shard_map/all_gather | solution.py:211
  49.5 3.5 %collective-permute-start.3 = (bf16[64,2048]{1,0:T(8,128)(2,1)}, bf16[64,2048]{1,0:T(8,128)(2,1)}, u32[]{:S(2)}, u32[]{:S(2)}) collective-permute-start(bf16[64,2048]{1,0:T(8,128)(2,1)} %slice.65), channel_id=1, source_target_pairs={{0,128},{1,129},{2,130},{3,131},{4,132},{5,133},{6,134},{7,135},{8... | collective-permute-start | bytes 786440 | tf_op jit(solution)/shard_map/ppermute | solution.py:92
  53.0 4.1 %collective-permute-start.4 = (bf16[64,2048]{1,0:T(8,128)(2,1)}, bf16[64,2048]{1,0:T(8,128)(2,1)}, u32[]{:S(2)}, u32[]{:S(2)}) collective-permute-start(bf16[64,2048]{1,0:T(8,128)(2,1)} %slice.66), channel_id=1, source_target_pairs={{0,384},{1,385},{2,386},{3,387},{4,388},{5,389},{6,390},{7,391},{8... | collective-permute-start | bytes 786440 | tf_op jit(solution)/shard_map/ppermute | solution.py:92
  57.1 1.0 fusion.14
  58.1 1.7 %pad_maximum_fusion.9 = (f32[128,128]{1,0:T(8,128)}, f32[128,128]{1,0:T(8,128)}) fusion(f32[128,64]{1,0:T(8,128)} %get-tuple-element.50, f32[128,64]{1,0:T(8,128)} %get-tuple-element.49, f32[128,64]{1,0:T(8,128)} %get-tuple-element.48), kind=kLoop, calls=%fused_computation.30 | loop fusion | flops 32768 | bytes 229376 | tf_op jit(solution)/shard_map/concatenate | solution.py:16
  59.8 3.5 %collective-permute-start.8 = (bf16[256,1152]{1,0:T(8,128)(2,1)S(1)}, bf16[256,1152]{1,0:T(8,128)(2,1)}, u32[]{:S(2)}, u32[]{:S(2)}) collective-permute-start(bf16[256,1152]{1,0:T(8,128)(2,1)S(1)} %bitcast.68), channel_id=1, source_target_pairs={{0,8},{1,9},{2,10},{3,11},{4,12},{5,13},{6,14},{7,15},{8,0},{9,1},... | collective-permute-start | bytes 1769480 | tf_op jit(solution)/shard_map/ppermute | solution.py:92
  63.4 3.4 %collective-permute-start.7 = (bf16[256,1152]{1,0:T(8,128)(2,1)S(1)}, bf16[256,1152]{1,0:T(8,128)(2,1)}, u32[]{:S(2)}, u32[]{:S(2)}) collective-permute-start(bf16[256,1152]{1,0:T(8,128)(2,1)S(1)} %bitcast.69), channel_id=1, source_target_pairs={{0,384},{1,385},{2,386},{3,387},{4,388},{5,389},{6,390},{7,391},{8... | collective-permute-start | bytes 1769480 | tf_op jit(solution)/shard_map/ppermute | solution.py:92
  66.8 1.9 %collective-permute-start.6 = (bf16[256,1152]{1,0:T(8,128)(2,1)S(1)}, bf16[256,1152]{1,0:T(8,128)(2,1)}, u32[]{:S(2)}, u32[]{:S(2)}) collective-permute-start(bf16[256,1152]{1,0:T(8,128)(2,1)S(1)} %bitcast.70), channel_id=1, source_target_pairs={{0,128},{1,129},{2,130},{3,131},{4,132},{5,133},{6,134},{7,135},{8... | collective-permute-start | bytes 1769480 | tf_op jit(solution)/shard_map/ppermute | solution.py:92
  68.7 5.2 %all-to-all-done.1.weight_ref = bf16[16,320,128]{2,1,0:T(8,128)(2,1)S(1)} async-done(((bf16[16,320,128]{2,1,0:T(8,128)(2,1)}), bf16[16,320,128]{2,1,0:T(8,128)(2,1)S(1)}, u32[]{:S(2)}, u32[]{:S(2)}) %all-to-all-start.1) | async-done | bytes 1310752 | tf_op jit(solution)/shard_map/all_to_all | solution.py:96
  73.9 2.7 %shard_map.127 = bf16[4,128,512]{2,1,0:T(8,128)(2,1)} custom-call(s32[3]{0:T(128)S(1)} %pad_add_fusion.place_ref, bf16[16,320,128]{2,1,0:T(8,128)(2,1)S(1)} %all-to-all-done.1.weight_ref, bf16[128,2048]{1,0:T(8,128)(2,1)S(1)} %multiply_convert_fusion.refs_0_, bf16[128,2048]{1,0:T(8,128)(2,1)S(1)} %collective-permute-done.2.refs_1_, ...), custom_call_target="tpu_custom_call" | custom-call | tf_op jit(solution)/shard_map/pallas_call | solution.py:157
  76.6 3.5 %all-to-all-start.2 = ((bf16[4,128,512]{2,1,0:T(8,128)(2,1)}), bf16[4,128,512]{2,1,0:T(8,128)(2,1)S(1)}, u32[]{:S(2)}, u32[]{:S(2)}) async-start(bf16[4,128,512]{2,1,0:T(8,128)(2,1)} %shard_map.127), calls=%async_computation.2 | async-start | bytes 1048576 | tf_op jit(solution)/shard_map/all_to_all | solution.py:96
  80.1 4.5 %collective-permute-start.9 = (bf16[256,1152]{1,0:T(8,128)(2,1)}, bf16[256,1152]{1,0:T(8,128)(2,1)S(1)}, u32[]{:S(2)}, u32[]{:S(2)}) collective-permute-start(bf16[256,1152]{1,0:T(8,128)(2,1)} %collective-permute-done.8.refs_1_), channel_id=1, source_target_pairs={{0,384},{1,385},{2,386},{3,387},{4,388},{5,389},{6,390},{7,391},{8... | collective-permute-start | bytes 1769480 | tf_op jit(solution)/shard_map/ppermute | solution.py:92
  84.7 3.1 %all-to-all-done.2 = bf16[4,128,512]{2,1,0:T(8,128)(2,1)S(1)} async-done(((bf16[4,128,512]{2,1,0:T(8,128)(2,1)}), bf16[4,128,512]{2,1,0:T(8,128)(2,1)S(1)}, u32[]{:S(2)}, u32[]{:S(2)}) %all-to-all-start.2) | async-done | bytes 524320 | tf_op jit(solution)/shard_map/all_to_all | solution.py:96
  88.0 5.7 %collective-permute-start.5 = (bf16[128,768]{1,0:T(8,128)(2,1)S(1)}, bf16[128,768]{1,0:T(8,128)(2,1)S(1)}, u32[]{:S(2)}, u32[]{:S(2)}) collective-permute-start(bf16[128,768]{1,0:T(8,128)(2,1)S(1)} %convert_dynamic-update-slice_fusion), channel_id=1, source_target_pairs={{0,1},{1,0},{2,3},{3,2},{4,5},{5,4},{6,7},{7,6},{8,9},{9,8},{10,11... | collective-permute-start | bytes 589832 | tf_op jit(solution)/shard_map/ppermute | solution.py:92
  95.8 1.4 collective-permute-done.9.refs_3_
  97.2 6.4 %all-to-all-start.3 = ((bf16[4,136,384]{2,1,0:T(8,128)(2,1)}), bf16[4,136,384]{2,1,0:T(8,128)(2,1)S(1)}, u32[]{:S(2)}, u32[]{:S(2)}) async-start(bf16[4,136,384]{2,1,0:T(8,128)(2,1)} %pad_maximum_fusion), calls=%async_computation.3 | async-start | bytes 835584 | tf_op jit(solution)/shard_map/all_to_all | solution.py:96
  103.6 5.7 %collective-permute-start.12 = (bf16[256,1152]{1,0:T(8,128)(2,1)}, bf16[256,1152]{1,0:T(8,128)(2,1)S(1)}, u32[]{:S(2)}, u32[]{:S(2)}) collective-permute-start(bf16[256,1152]{1,0:T(8,128)(2,1)} %collective-permute-done.8.refs_1_), channel_id=1, source_target_pairs={{0,128},{1,129},{2,130},{3,131},{4,132},{5,133},{6,134},{7,135},{8... | collective-permute-start | bytes 1769480 | tf_op jit(solution)/shard_map/ppermute | solution.py:92
  109.3 1.9 %collective-permute-start.11 = (bf16[256,1152]{1,0:T(8,128)(2,1)S(1)}, bf16[256,1152]{1,0:T(8,128)(2,1)S(1)}, u32[]{:S(2)}, u32[]{:S(2)}) collective-permute-start(bf16[256,1152]{1,0:T(8,128)(2,1)S(1)} %collective-permute-done.9.refs_3_), channel_id=1, source_target_pairs={{0,384},{1,385},{2,386},{3,387},{4,388},{5,389},{6,390},{7,391},{8... | collective-permute-start | bytes 1769480 | tf_op jit(solution)/shard_map/ppermute | solution.py:92
  111.3 3.4 %collective-permute-start.10 = (bf16[256,1152]{1,0:T(8,128)(2,1)}, bf16[256,1152]{1,0:T(8,128)(2,1)}, u32[]{:S(2)}, u32[]{:S(2)}) collective-permute-start(bf16[256,1152]{1,0:T(8,128)(2,1)} %collective-permute-done.6.refs_6_), channel_id=1, source_target_pairs={{0,128},{1,129},{2,130},{3,131},{4,132},{5,133},{6,134},{7,135},{8... | collective-permute-start | bytes 1769480 | tf_op jit(solution)/shard_map/ppermute | solution.py:92
  116.1 20.8 %all-gather.1 = bf16[1536,128]{1,0:T(8,128)(2,1)S(1)} all-gather(bf16[192,128]{1,0:T(8,128)(2,1)S(1)} %shard_map.128), channel_id=3, replica_groups=mesh['engine'=4,'fsdp'=16,'tensor'=8] {'tensor'}, dimensions={0}, use_global_device_ids=true | all-gather | bytes 442368 | tf_op jit(solution)/shard_map/all_gather | solution.py:253
  136.9 4.4 %shard_map.129 = bf16[128,2048]{1,0:T(8,128)(2,1)} custom-call(s32[3]{0:T(128)S(1)} %pad_add_fusion.place_ref, bf16[8,192,128]{2,1,0:T(8,128)(2,1)S(1)} %bitcast.72, bf16[256,1152]{1,0:T(8,128)(2,1)S(1)} %bitcast.71, bf16[256,1152]{1,0:T(8,128)(2,1)} %collective-permute-done.8.refs_1_, bf16[256,1152]{1,0:T(8,128)(2,1)} %collective-permute-done.7.refs_2_, ...), custom_call_target="tpu_custom_call" | custom-call | tf_op jit(solution)/shard_map/pallas_call | solution.py:157
  (69 shorter events, 5.6 us)
Async XLA Ops:
  0.0 1.0 copy-start
  0.0 13.8 %copy-start.8 = (bf16[2048]{0:T(1024)(128)(2,1)S(1)}, bf16[2048]{0:T(1024)(128)(2,1)}, u32[]{:S(2)}) copy-start(bf16[2048]{0:T(1024)(128)(2,1)} %param.14) | copy-start | bytes 12292
  0.0 13.8 %copy-start.6 = (bf16[128,2048]{1,0:T(8,128)(2,1)S(1)}, bf16[128,2048]{1,0:T(8,128)(2,1)}, u32[]{:S(2)}) copy-start(bf16[128,2048]{1,0:T(8,128)(2,1)} %param.13) | copy-start | bytes 1572868
  2.1 24.2 %copy-start.7 = (bf16[1,32,256]{2,1,0:T(8,128)(2,1)S(1)}, bf16[1,32,256]{2,1,0:T(8,128)(2,1)}, u32[]{:S(2)}) copy-start(bf16[1,32,256]{2,1,0:T(8,128)(2,1)} %param.18) | copy-start | bytes 49156
  2.9 30.7 %all-to-all-start = ((bf16[8,32,1152]{2,1,0:T(8,128)(2,1)}), bf16[8,32,1152]{2,1,0:T(8,128)(2,1)S(1)}, u32[]{:S(2)}, u32[]{:S(2)}) async-start(bf16[8,32,1152]{2,1,0:T(8,128)(2,1)} %broadcast_in_dim.18), calls=%async_computation | async-start | bytes 1179648 | tf_op jit(solution)/shard_map/all_to_all | solution.py:96
  13.9 16.5 %collective-permute-start.2 = (bf16[128,2048]{1,0:T(8,128)(2,1)S(1)}, bf16[128,2048]{1,0:T(8,128)(2,1)S(1)}, u32[]{:S(2)}, u32[]{:S(2)}) collective-permute-start(bf16[128,2048]{1,0:T(8,128)(2,1)S(1)} %multiply_convert_fusion.refs_0_), channel_id=1, source_target_pairs={{0,384},{1,385},{2,386},{3,387},{4,388},{5,389},{6,390},{7,391},{8... | collective-permute-start | bytes 1572872 | tf_op jit(solution)/shard_map/ppermute | solution.py:92
  18.3 15.3 %collective-permute-start.1 = (bf16[128,2048]{1,0:T(8,128)(2,1)S(1)}, bf16[128,2048]{1,0:T(8,128)(2,1)S(1)}, u32[]{:S(2)}, u32[]{:S(2)}) collective-permute-start(bf16[128,2048]{1,0:T(8,128)(2,1)S(1)} %multiply_convert_fusion.refs_0_), channel_id=1, source_target_pairs={{0,128},{1,129},{2,130},{3,131},{4,132},{5,133},{6,134},{7,135},{8... | collective-permute-start | bytes 1572872 | tf_op jit(solution)/shard_map/ppermute | solution.py:92
  20.3 10.2 %collective-permute-start = (bf16[256,128]{1,0:T(8,128)(2,1)S(1)}, bf16[256,128]{1,0:T(8,128)(2,1)S(1)}, u32[]{:S(2)}, u32[]{:S(2)}) collective-permute-start(bf16[256,128]{1,0:T(8,128)(2,1)S(1)} %fusion.1), channel_id=1, source_target_pairs={{0,0},{1,112},{2,128},{3,240},{4,256},{5,368},{6,384},{7,496},{8,8... | collective-permute-start | bytes 196616 | tf_op jit(solution)/shard_map/ppermute | solution.py:92
  35.0 7.8 %copy-start.9 = (s32[1,128]{1,0:T(1,128)S(1)}, s32[1,128]{1,0:T(1,128)}, u32[]{:S(2)}) copy-start(s32[1,128]{1,0:T(1,128)} %param.24) | copy-start | bytes 1540
  35.0 38.9 %all-to-all-start.1 = ((bf16[16,320,128]{2,1,0:T(8,128)(2,1)}), bf16[16,320,128]{2,1,0:T(8,128)(2,1)S(1)}, u32[]{:S(2)}, u32[]{:S(2)}) async-start(bf16[16,320,128]{2,1,0:T(8,128)(2,1)} %broadcast_in_dim.17), calls=%async_computation.1 | async-start | bytes 2621440 | tf_op jit(solution)/shard_map/all_to_all | solution.py:96
  49.5 19.2 %collective-permute-start.3 = (bf16[64,2048]{1,0:T(8,128)(2,1)}, bf16[64,2048]{1,0:T(8,128)(2,1)}, u32[]{:S(2)}, u32[]{:S(2)}) collective-permute-start(bf16[64,2048]{1,0:T(8,128)(2,1)} %slice.65), channel_id=1, source_target_pairs={{0,128},{1,129},{2,130},{3,131},{4,132},{5,133},{6,134},{7,135},{8... | collective-permute-start | bytes 786440 | tf_op jit(solution)/shard_map/ppermute | solution.py:92
  53.0 15.7 %collective-permute-start.4 = (bf16[64,2048]{1,0:T(8,128)(2,1)}, bf16[64,2048]{1,0:T(8,128)(2,1)}, u32[]{:S(2)}, u32[]{:S(2)}) collective-permute-start(bf16[64,2048]{1,0:T(8,128)(2,1)} %slice.66), channel_id=1, source_target_pairs={{0,384},{1,385},{2,386},{3,387},{4,388},{5,389},{6,390},{7,391},{8... | collective-permute-start | bytes 786440 | tf_op jit(solution)/shard_map/ppermute | solution.py:92
  59.8 20.4 %collective-permute-start.8 = (bf16[256,1152]{1,0:T(8,128)(2,1)S(1)}, bf16[256,1152]{1,0:T(8,128)(2,1)}, u32[]{:S(2)}, u32[]{:S(2)}) collective-permute-start(bf16[256,1152]{1,0:T(8,128)(2,1)S(1)} %bitcast.68), channel_id=1, source_target_pairs={{0,8},{1,9},{2,10},{3,11},{4,12},{5,13},{6,14},{7,15},{8,0},{9,1},... | collective-permute-start | bytes 1769480 | tf_op jit(solution)/shard_map/ppermute | solution.py:92
  63.4 32.4 %collective-permute-start.7 = (bf16[256,1152]{1,0:T(8,128)(2,1)S(1)}, bf16[256,1152]{1,0:T(8,128)(2,1)}, u32[]{:S(2)}, u32[]{:S(2)}) collective-permute-start(bf16[256,1152]{1,0:T(8,128)(2,1)S(1)} %bitcast.69), channel_id=1, source_target_pairs={{0,384},{1,385},{2,386},{3,387},{4,388},{5,389},{6,390},{7,391},{8... | collective-permute-start | bytes 1769480 | tf_op jit(solution)/shard_map/ppermute | solution.py:92
  66.8 29.1 %collective-permute-start.6 = (bf16[256,1152]{1,0:T(8,128)(2,1)S(1)}, bf16[256,1152]{1,0:T(8,128)(2,1)}, u32[]{:S(2)}, u32[]{:S(2)}) collective-permute-start(bf16[256,1152]{1,0:T(8,128)(2,1)S(1)} %bitcast.70), channel_id=1, source_target_pairs={{0,128},{1,129},{2,130},{3,131},{4,132},{5,133},{6,134},{7,135},{8... | collective-permute-start | bytes 1769480 | tf_op jit(solution)/shard_map/ppermute | solution.py:92
  76.6 11.2 %all-to-all-start.2 = ((bf16[4,128,512]{2,1,0:T(8,128)(2,1)}), bf16[4,128,512]{2,1,0:T(8,128)(2,1)S(1)}, u32[]{:S(2)}, u32[]{:S(2)}) async-start(bf16[4,128,512]{2,1,0:T(8,128)(2,1)} %shard_map.127), calls=%async_computation.2 | async-start | bytes 1048576 | tf_op jit(solution)/shard_map/all_to_all | solution.py:96
  80.1 17.1 %collective-permute-start.9 = (bf16[256,1152]{1,0:T(8,128)(2,1)}, bf16[256,1152]{1,0:T(8,128)(2,1)S(1)}, u32[]{:S(2)}, u32[]{:S(2)}) collective-permute-start(bf16[256,1152]{1,0:T(8,128)(2,1)} %collective-permute-done.8.refs_1_), channel_id=1, source_target_pairs={{0,384},{1,385},{2,386},{3,387},{4,388},{5,389},{6,390},{7,391},{8... | collective-permute-start | bytes 1769480 | tf_op jit(solution)/shard_map/ppermute | solution.py:92
  88.0 6.8 %collective-permute-start.5 = (bf16[128,768]{1,0:T(8,128)(2,1)S(1)}, bf16[128,768]{1,0:T(8,128)(2,1)S(1)}, u32[]{:S(2)}, u32[]{:S(2)}) collective-permute-start(bf16[128,768]{1,0:T(8,128)(2,1)S(1)} %convert_dynamic-update-slice_fusion), channel_id=1, source_target_pairs={{0,1},{1,0},{2,3},{3,2},{4,5},{5,4},{6,7},{7,6},{8,9},{9,8},{10,11... | collective-permute-start | bytes 589832 | tf_op jit(solution)/shard_map/ppermute | solution.py:92
  94.9 20.4 %copy-start.1 = (f32[128,128]{1,0:T(8,128)S(1)}, f32[128,128]{1,0:T(8,128)}, u32[]{:S(2)}) copy-start(f32[128,128]{1,0:T(8,128)} %get-tuple-element.34.cosine_ref) | copy-start | bytes 196612
  94.9 20.4 %copy-start.2 = (f32[128,128]{1,0:T(8,128)S(1)}, f32[128,128]{1,0:T(8,128)}, u32[]{:S(2)}) copy-start(f32[128,128]{1,0:T(8,128)} %get-tuple-element.35.sine_ref) | copy-start | bytes 196612
  94.9 20.4 %copy-start.3 = (bf16[1,512,128]{2,1,0:T(8,128)(2,1)S(1)}, bf16[1,512,128]{2,1,0:T(8,128)(2,1)}, u32[]{:S(2)}) copy-start(bf16[1,512,128]{2,1,0:T(8,128)(2,1)} %param.22) | copy-start | bytes 393220
  94.9 20.4 %copy-start.4 = (bf16[1,512,128]{2,1,0:T(8,128)(2,1)S(1)}, bf16[1,512,128]{2,1,0:T(8,128)(2,1)}, u32[]{:S(2)}) copy-start(bf16[1,512,128]{2,1,0:T(8,128)(2,1)} %param.23) | copy-start | bytes 393220
  94.9 20.4 %copy-start.5 = (bf16[128,64]{0,1:T(8,128)(2,1)S(1)}, bf16[128,64]{0,1:T(8,128)(2,1)}, u32[]{:S(2)}) copy-start(bf16[128,64]{0,1:T(8,128)(2,1)} %param.20) | copy-start | bytes 49156
  97.2 18.1 %all-to-all-start.3 = ((bf16[4,136,384]{2,1,0:T(8,128)(2,1)}), bf16[4,136,384]{2,1,0:T(8,128)(2,1)S(1)}, u32[]{:S(2)}, u32[]{:S(2)}) async-start(bf16[4,136,384]{2,1,0:T(8,128)(2,1)} %pad_maximum_fusion), calls=%async_computation.3 | async-start | bytes 835584 | tf_op jit(solution)/shard_map/all_to_all | solution.py:96
  103.6 33.3 %collective-permute-start.12 = (bf16[256,1152]{1,0:T(8,128)(2,1)}, bf16[256,1152]{1,0:T(8,128)(2,1)S(1)}, u32[]{:S(2)}, u32[]{:S(2)}) collective-permute-start(bf16[256,1152]{1,0:T(8,128)(2,1)} %collective-permute-done.8.refs_1_), channel_id=1, source_target_pairs={{0,128},{1,129},{2,130},{3,131},{4,132},{5,133},{6,134},{7,135},{8... | collective-permute-start | bytes 1769480 | tf_op jit(solution)/shard_map/ppermute | solution.py:92
  109.3 27.6 %collective-permute-start.11 = (bf16[256,1152]{1,0:T(8,128)(2,1)S(1)}, bf16[256,1152]{1,0:T(8,128)(2,1)S(1)}, u32[]{:S(2)}, u32[]{:S(2)}) collective-permute-start(bf16[256,1152]{1,0:T(8,128)(2,1)S(1)} %collective-permute-done.9.refs_3_), channel_id=1, source_target_pairs={{0,384},{1,385},{2,386},{3,387},{4,388},{5,389},{6,390},{7,391},{8... | collective-permute-start | bytes 1769480 | tf_op jit(solution)/shard_map/ppermute | solution.py:92
  111.3 25.6 %collective-permute-start.10 = (bf16[256,1152]{1,0:T(8,128)(2,1)}, bf16[256,1152]{1,0:T(8,128)(2,1)}, u32[]{:S(2)}, u32[]{:S(2)}) collective-permute-start(bf16[256,1152]{1,0:T(8,128)(2,1)} %collective-permute-done.6.refs_6_), channel_id=1, source_target_pairs={{0,128},{1,129},{2,130},{3,131},{4,132},{5,133},{6,134},{7,135},{8... | collective-permute-start | bytes 1769480 | tf_op jit(solution)/shard_map/ppermute | solution.py:92
